TPU v7x, 128 devices: a whole 4x4x4 slice. The times are simulated.
128 devices in a mesh: dp: 32 (over x, y, z_hi), tensor: 4 (over z_lo, core).
Axes of the slice: x: 4, y: 4, z: 4 (z_hi: 2, z_lo: 2; z = z_hi * 2 + z_lo), core: 2. Of those that a mesh axis runs over, the one named last changes fastest.
Arguments:
- image: bfloat16 [64, 256, 2048], P('dp'), may hold values from -6 to 6
- text: bfloat16 [64, 16, 4096], P('dp'), may hold values from -6 to 6
- masked: int32 [64, 256], P('dp'), may hold values 0 or 1
- text_len: int32 [64], P('dp'), may hold values from 1 to 16, as said below
- cotangent: bfloat16 [64, 256, 2048], P('dp'), may hold values from -6 to 6
- self_query: bfloat16 [2048, 2048], P(None, 'tensor'), may hold values from -0.1875 to 0.1875
- self_key: bfloat16 [2048, 2048], P(None, 'tensor'), may hold values from -0.1875 to 0.1875
- self_value: bfloat16 [2048, 2048], P(None, 'tensor'), may hold values from -0.125 to 0.125
- self_output: bfloat16 [2048, 2048], P('tensor'), may hold values from -0.25 to 0.25
- text_query: bfloat16 [2048, 2048], P(None, 'tensor'), may hold values from -0.1875 to 0.1875
- text_key: bfloat16 [4096, 2048], P(None, 'tensor'), may hold values from -0.125 to 0.125
- text_value: bfloat16 [4096, 2048], P(None, 'tensor'), may hold values from -0.09375 to 0.09375
- text_output: bfloat16 [2048, 2048], P('tensor'), may hold values from -0.25 to 0.25
- expand: bfloat16 [2048, 8192], P(None, 'tensor'), may hold values from -0.125 to 0.125
- contract: bfloat16 [8192, 2048], P('tensor'), may hold values from -0.09375 to 0.09375
- first_gain: float32 [2048], replicated, may hold values from 0.1 to 1.9
- second_gain: float32 [2048], replicated, may hold values from 0.1 to 1.9
- third_gain: float32 [2048], replicated, may hold values from 0.1 to 1.9
- mask_token: float32 [2048], replicated, may hold values from -6 to 6
Outputs:
- layer_out: bfloat16 [64, 256, 2048], P('dp')
- image_grad: bfloat16 [64, 256, 2048], P('dp')
- self_query_grad: float32 [2048, 2048], P('dp', 'tensor')
- self_key_grad: float32 [2048, 2048], P('dp', 'tensor')
- self_value_grad: float32 [2048, 2048], P('dp', 'tensor')
- self_output_grad: float32 [2048, 2048], P('tensor', 'dp')
- text_query_grad: float32 [2048, 2048], P('dp', 'tensor')
- text_key_grad: float32 [4096, 2048], P('dp', 'tensor')
- text_value_grad: float32 [4096, 2048], P('dp', 'tensor')
- text_output_grad: float32 [2048, 2048], P('tensor', 'dp')
- expand_grad: float32 [2048, 8192], P('dp', 'tensor')
- contract_grad: float32 [8192, 2048], P('tensor', 'dp')
- first_gain_grad: float32 [2048], P('dp')
- second_gain_grad: float32 [2048], P('dp')
- third_gain_grad: float32 [2048], P('dp')
- mask_token_grad: float32 [2048], P('dp')
Inputs may be any that keep to these rules, and one draw needn't show every extreme that they name: One item, drawn from the seed, has text_len = 16.
All inputs are finite; a program needn't handle non-finite values. No bound on the sum of `masked` on one device may be relied on, other than what follows from the above.
Results may differ from a plain program's by a relative error of at most 0.025.
The roundings to bfloat16 on the way count: a program that leaves them out, or rounds other values in their place, can miss the bound.
Values sent between devices are 32-bit elements; how exact they have to be, the bound alone decides.
A program may use at most 320 MiB of HBM per device.

v0:
```python
import jax
import jax.numpy as jnp
from jax import lax
from jax.sharding import PartitionSpec as P

HEAD = 128
MICRO = 2


def layer_norm(rows, gain):
    mean = jnp.mean(rows, axis=-1, keepdims=True)
    centred = rows - mean
    spread = jnp.mean(centred * centred, axis=-1, keepdims=True)
    return centred * lax.rsqrt(spread + 1e-05) * gain


def product(left, right):
    return jnp.dot(left, right, preferred_element_type=jnp.float32)


def outer_sum(left, right):
    return lax.dot_general(
        left, right, (((0,), (0,)), ((), ())), preferred_element_type=jnp.float32
    )


def back_product(left, right):
    return lax.dot_general(
        left, right, (((1,), (1,)), ((), ())), preferred_element_type=jnp.float32
    )


def attend_scores(query, keys, valid):
    scale = query.shape[-1] ** (-0.5)
    scores = jnp.einsum("bqhd,bkhd->bhqk", query, keys, preferred_element_type=jnp.float32) * scale
    return jnp.where(valid[:, None, None, :], scores, -1e30)


def attend_forward(query, keys, values, valid):
    scores = attend_scores(query, keys, valid)
    total = jax.nn.logsumexp(scores, axis=-1, keepdims=True)
    weights_low = jnp.exp(scores - total).astype(jnp.bfloat16)
    mixed = jnp.einsum("bhqk,bkhd->bqhd", weights_low, values, preferred_element_type=jnp.float32)
    return (mixed.astype(jnp.bfloat16), total)


def attend_backward(query, keys, values, valid, total, upstream):
    scale = query.shape[-1] ** (-0.5)
    probs = jnp.exp(attend_scores(query, keys, valid) - total)
    probs_low = probs.astype(jnp.bfloat16)
    grad_values = jnp.einsum(
        "bhqk,bqhd->bkhd", probs_low, upstream, preferred_element_type=jnp.float32
    ).astype(jnp.bfloat16)
    grad_probs = jnp.einsum("bqhd,bkhd->bhqk", upstream, values, preferred_element_type=jnp.float32)
    inner = jnp.sum(grad_probs * probs, axis=-1, keepdims=True)
    grad_scores = (probs * (grad_probs - inner)).astype(jnp.bfloat16)
    grad_query = (
        jnp.einsum("bhqk,bkhd->bqhd", grad_scores, keys, preferred_element_type=jnp.float32) * scale
    ).astype(jnp.bfloat16)
    grad_keys = (
        jnp.einsum("bhqk,bqhd->bkhd", grad_scores, query, preferred_element_type=jnp.float32)
        * scale
    ).astype(jnp.bfloat16)
    return (grad_query, grad_keys, grad_values)


def shards(
    image,
    text,
    masked,
    text_len,
    cotangent,
    self_query,
    self_key,
    self_value,
    self_output,
    text_query,
    text_key,
    text_value,
    text_output,
    expand,
    contract,
    first_gain,
    second_gain,
    third_gain,
    mask_token,
):
    width = image.shape[2]
    length = image.shape[1]
    words = text.shape[1]
    group = image.shape[0] // MICRO
    heads = self_query.shape[1] // HEAD
    count = group * length
    order = [
        "self_query",
        "self_key",
        "self_value",
        "self_output",
        "text_query",
        "text_key",
        "text_value",
        "text_output",
        "expand",
        "contract",
        "first_gain",
        "second_gain",
        "third_gain",
        "mask_token",
    ]
    params = [
        self_query,
        self_key,
        self_value,
        self_output,
        text_query,
        text_key,
        text_value,
        text_output,
        expand,
        contract,
        first_gain,
        second_gain,
        third_gain,
        mask_token,
    ]
    totals = {}
    for label, weight in zip(order, params):
        totals[label] = jnp.zeros(weight.shape, jnp.float32)
    reduced = {}
    outputs = []
    input_grads = []
    for micro in range(MICRO):
        first_item = micro * group
        picked = slice(first_item, first_item + group)
        hidden_mask = masked[picked].reshape(count, 1) == 1
        start = jnp.where(
            hidden_mask,
            mask_token[None, :],
            image[picked].reshape(count, width).astype(jnp.float32),
        )
        normed_one = layer_norm(start, first_gain).astype(jnp.bfloat16)
        query = (
            product(normed_one, self_query).astype(jnp.bfloat16).reshape(group, length, heads, HEAD)
        )
        keys = (
            product(normed_one, self_key).astype(jnp.bfloat16).reshape(group, length, heads, HEAD)
        )
        values = (
            product(normed_one, self_value).astype(jnp.bfloat16).reshape(group, length, heads, HEAD)
        )
        every = jnp.ones((group, length), jnp.bool_)
        self_mixed, self_total = attend_forward(query, keys, values, every)
        self_rows = self_mixed.reshape(count, heads * HEAD)
        first = start + lax.psum(product(self_rows, self_output), "tensor")
        normed_two = layer_norm(first, second_gain).astype(jnp.bfloat16)
        cross_query = (
            product(normed_two, text_query).astype(jnp.bfloat16).reshape(group, length, heads, HEAD)
        )
        text_rows = text[picked].reshape(group * words, text.shape[2])
        cross_keys = (
            product(text_rows, text_key).astype(jnp.bfloat16).reshape(group, words, heads, HEAD)
        )
        cross_values = (
            product(text_rows, text_value).astype(jnp.bfloat16).reshape(group, words, heads, HEAD)
        )
        present = jnp.arange(words)[None, :] < text_len[picked][:, None]
        cross_mixed, cross_total = attend_forward(cross_query, cross_keys, cross_values, present)
        cross_rows = cross_mixed.reshape(count, heads * HEAD)
        second = first + lax.psum(product(cross_rows, text_output), "tensor")
        normed_three = layer_norm(second, third_gain).astype(jnp.bfloat16)
        raised = product(normed_three, expand)
        active = jax.nn.gelu(raised).astype(jnp.bfloat16)
        result = second + lax.psum(product(active, contract), "tensor")
        outputs.append(result.astype(jnp.bfloat16).reshape(group, length, width))
        upstream = cotangent[picked].reshape(count, width)
        totals["contract"] = totals["contract"] + outer_sum(active, upstream)
        grad_active = back_product(upstream, contract)
        gelu_pull = jax.vjp(jax.nn.gelu, raised)[1]
        grad_raised = gelu_pull(grad_active)[0].astype(jnp.bfloat16)
        totals["expand"] = totals["expand"] + outer_sum(normed_three, grad_raised)
        grad_three = lax.psum(back_product(grad_raised, expand), "tensor")
        norm_pull = jax.vjp(layer_norm, second, third_gain)[1]
        grad_rows, grad_gain = norm_pull(grad_three)
        totals["third_gain"] = totals["third_gain"] + grad_gain
        grad_second = upstream.astype(jnp.float32) + grad_rows
        cross_out_grad = grad_second.astype(jnp.bfloat16)
        totals["text_output"] = totals["text_output"] + outer_sum(cross_rows, cross_out_grad)
        grad_cross_mixed = (
            back_product(cross_out_grad, text_output)
            .astype(jnp.bfloat16)
            .reshape(group, length, heads, HEAD)
        )
        grad_cq, grad_ck, grad_cv = attend_backward(
            cross_query, cross_keys, cross_values, present, cross_total, grad_cross_mixed
        )
        grad_cq_rows = grad_cq.reshape(count, heads * HEAD)
        totals["text_query"] = totals["text_query"] + outer_sum(normed_two, grad_cq_rows)
        totals["text_key"] = totals["text_key"] + outer_sum(
            text_rows, grad_ck.reshape(group * words, heads * HEAD)
        )
        totals["text_value"] = totals["text_value"] + outer_sum(
            text_rows, grad_cv.reshape(group * words, heads * HEAD)
        )
        grad_two = lax.psum(back_product(grad_cq_rows, text_query), "tensor")
        norm_pull = jax.vjp(layer_norm, first, second_gain)[1]
        grad_rows, grad_gain = norm_pull(grad_two)
        totals["second_gain"] = totals["second_gain"] + grad_gain
        grad_first = grad_second + grad_rows
        self_out_grad = grad_first.astype(jnp.bfloat16)
        totals["self_output"] = totals["self_output"] + outer_sum(self_rows, self_out_grad)
        grad_self_mixed = (
            back_product(self_out_grad, self_output)
            .astype(jnp.bfloat16)
            .reshape(group, length, heads, HEAD)
        )
        grad_q, grad_k, grad_v = attend_backward(
            query, keys, values, every, self_total, grad_self_mixed
        )
        grad_q_rows = grad_q.reshape(count, heads * HEAD)
        grad_k_rows = grad_k.reshape(count, heads * HEAD)
        grad_v_rows = grad_v.reshape(count, heads * HEAD)
        totals["self_query"] = totals["self_query"] + outer_sum(normed_one, grad_q_rows)
        totals["self_key"] = totals["self_key"] + outer_sum(normed_one, grad_k_rows)
        totals["self_value"] = totals["self_value"] + outer_sum(normed_one, grad_v_rows)
        shares = (
            back_product(grad_q_rows, self_query)
            + back_product(grad_k_rows, self_key)
            + back_product(grad_v_rows, self_value)
        )
        grad_one = lax.psum(shares, "tensor")
        norm_pull = jax.vjp(layer_norm, start, first_gain)[1]
        grad_rows, grad_gain = norm_pull(grad_one)
        totals["first_gain"] = totals["first_gain"] + grad_gain
        grad_start = grad_first + grad_rows
        totals["mask_token"] = totals["mask_token"] + jnp.sum(
            jnp.where(hidden_mask, grad_start, 0.0), axis=0
        )
        input_grads.append(
            jnp.where(hidden_mask, 0.0, grad_start)
            .astype(jnp.bfloat16)
            .reshape(group, length, width)
        )
    summed = (
        lax.psum_scatter(totals["self_query"], "dp", scatter_dimension=0, tiled=True),
        lax.psum_scatter(totals["self_key"], "dp", scatter_dimension=0, tiled=True),
        lax.psum_scatter(totals["self_value"], "dp", scatter_dimension=0, tiled=True),
        lax.psum_scatter(totals["self_output"], "dp", scatter_dimension=1, tiled=True),
        lax.psum_scatter(totals["text_query"], "dp", scatter_dimension=0, tiled=True),
        lax.psum_scatter(totals["text_key"], "dp", scatter_dimension=0, tiled=True),
        lax.psum_scatter(totals["text_value"], "dp", scatter_dimension=0, tiled=True),
        lax.psum_scatter(totals["text_output"], "dp", scatter_dimension=1, tiled=True),
        lax.psum_scatter(totals["expand"], "dp", scatter_dimension=0, tiled=True),
        lax.psum_scatter(totals["contract"], "dp", scatter_dimension=1, tiled=True),
        lax.psum_scatter(totals["first_gain"], "dp", scatter_dimension=0, tiled=True),
        lax.psum_scatter(totals["second_gain"], "dp", scatter_dimension=0, tiled=True),
        lax.psum_scatter(totals["third_gain"], "dp", scatter_dimension=0, tiled=True),
        lax.psum_scatter(totals["mask_token"], "dp", scatter_dimension=0, tiled=True),
    )
    for label, value in zip(order, summed):
        reduced[label] = value
    layer_out = jnp.concatenate(outputs, axis=0)
    image_grad = jnp.concatenate(input_grads, axis=0)
    return (
        layer_out,
        image_grad,
        reduced["self_query"],
        reduced["self_key"],
        reduced["self_value"],
        reduced["self_output"],
        reduced["text_query"],
        reduced["text_key"],
        reduced["text_value"],
        reduced["text_output"],
        reduced["expand"],
        reduced["contract"],
        reduced["first_gain"],
        reduced["second_gain"],
        reduced["third_gain"],
        reduced["mask_token"],
    )


def solution(mesh):
    return jax.shard_map(
        shards,
        mesh=mesh,
        in_specs=(
            P("dp", None, None),
            P("dp", None, None),
            P("dp", None),
            P("dp"),
            P("dp", None, None),
            P(None, "tensor"),
            P(None, "tensor"),
            P(None, "tensor"),
            P("tensor", None),
            P(None, "tensor"),
            P(None, "tensor"),
            P(None, "tensor"),
            P("tensor", None),
            P(None, "tensor"),
            P("tensor", None),
            P(),
            P(),
            P(),
            P(),
        ),
        out_specs=(
            P("dp", None, None),
            P("dp", None, None),
            P("dp", "tensor"),
            P("dp", "tensor"),
            P("dp", "tensor"),
            P("tensor", "dp"),
            P("dp", "tensor"),
            P("dp", "tensor"),
            P("dp", "tensor"),
            P("tensor", "dp"),
            P("dp", "tensor"),
            P("tensor", "dp"),
            P("dp"),
            P("dp"),
            P("dp"),
            P("dp"),
        ),
        check_vma=False,
    )
```

profile of v0, /device:TPU:0, one launch (start us, length us, event | category | flops | bytes accessed | tf_op | source)
XLA Modules:
  0.0 2967.3 jit_solution(10701594580890499248)
XLA Ops:
  8.2 1.7 fusion.3
  10.0 2.3 fusion.12
  27.5 2.0 fusion.230
  29.6 2.0 fusion.228
  34.7 3.6 fusion.75
  43.0 83.0 %all-reduce.24.cloned.1.call-done = (f32[256,2048]{1,0:T(8,128)}, f32[256,2048]{1,0:T(8,128)}) async-done(((f32[256,2048]{1,0:T(8,128)}, f32[256,2048]{1,0:T(8,128)}), (f32[256,2048]{1,0:T(8,128)}, f32[256,2048]{1,0:T(8,128)})) %all-reduce.24.cloned.1.call-update) | async-done | bytes 4194320 | tf_op jit(solution)/shard_map/psum | solution.py:154
  126.0 3.6 fusion.219
  131.1 1.7 copy-done.39
  135.7 2.1 fusion.229
  137.8 2.0 fusion.231
  140.1 92.7 %all-reduce.22.cloned.1.call-done = (f32[256,2048]{1,0:T(8,128)}, f32[256,2048]{1,0:T(8,128)}) async-done(((f32[256,2048]{1,0:T(8,128)}, f32[256,2048]{1,0:T(8,128)}), (f32[256,2048]{1,0:T(8,128)}, f32[256,2048]{1,0:T(8,128)})) %all-reduce.22.cloned.1.call-update) | async-done | bytes 4194320 | tf_op jit(solution)/shard_map/psum | solution.py:169
  232.8 4.0 fusion.217
  238.7 6.6 fusion.194
  245.4 2.5 fusion.195
  248.0 7.6 fusion.42
  255.6 7.2 fusion.49
  262.8 4.0 fusion.235
  266.8 3.7 fusion.232
  270.6 92.9 %all-reduce.20.cloned.1.call-done = (f32[256,2048]{1,0:T(8,128)}, f32[256,2048]{1,0:T(8,128)}) async-done(((f32[256,2048]{1,0:T(8,128)}, f32[256,2048]{1,0:T(8,128)}), (f32[256,2048]{1,0:T(8,128)}, f32[256,2048]{1,0:T(8,128)})) %all-reduce.20.cloned.1.call-update) | async-done | bytes 4194320 | tf_op jit(solution)/shard_map/psum | solution.py:181
  363.5 5.4 multiply_reduce_fusion.1
  375.8 2.2 fusion.236
  378.1 2.1 fusion.233
  381.7 7.4 fusion.191
  389.1 8.1 fusion.190
  397.2 75.8 %all-reduce.18.cloned.1.call-done = (f32[256,2048]{1,0:T(8,128)}, f32[256,2048]{1,0:T(8,128)}) async-done(((f32[256,2048]{1,0:T(8,128)}, f32[256,2048]{1,0:T(8,128)}), (f32[256,2048]{1,0:T(8,128)}, f32[256,2048]{1,0:T(8,128)})) %all-reduce.18.cloned.1.call-update) | async-done | bytes 4194320 | tf_op jit(solution)/shard_map/psum | solution.py:204
  473.1 4.8 multiply_reduce_fusion.3
  480.9 2.1 add_add_fusion.10
  485.8 1.8 copy.182
  487.6 2.4 convolution_convert_fusion.2
  495.2 1.8 copy.181
  505.6 2.1 convolution_add_fusion.10
  508.6 2.1 convolution_add_fusion.8
  514.6 4.6 add_bitcast_fusion
  521.8 4.6 add_bitcast_fusion.1
  527.3 2.5 fusion.192
  529.8 3.0 convolution_add_fusion.3
  534.9 2.8 convolution_add_fusion.2
  538.6 2.3 fusion.101
  541.0 2.9 convolution_add_fusion.4
  546.4 3.1 convolution_add_fusion.5
  551.4 3.1 convolution_add_fusion.6
  556.4 3.1 convolution_add_fusion.7
  560.1 10.4 fusion.193
  570.5 14.5 convolution_add_fusion.1
  585.4 10.3 fusion.87
  595.6 11.2 convolution_add_fusion
  608.8 63.2 %all-reduce.16.cloned.1.call-done = (f32[256,2048]{1,0:T(8,128)}, f32[256,2048]{1,0:T(8,128)}, f32[256,2048]{1,0:T(8,128)}, f32[256,2048]{1,0:T(8,128)}) async-done(((f32[256,2048]{1,0:T(8,128)}, f32[256,2048]{1,0:T(8,128)}, f32[256,2048]{1,0:T(8,128)}, f32[256,2048]{1,0:T(8,128)}), (f32[256,2048]{1,0:T(8,128)}, f32[256,2048]{1,0:T(8,128)}, f32[256,2048]{1,0:T(8,128)}, ...) | async-done | bytes 8388624 | tf_op jit(solution)/shard_map/psum | solution.py:173
  671.9 3.8 fusion.11
  675.8 1.8 fusion.211
  679.3 1.6 select_reduce_fusion
  680.9 184.3 %all-reduce.4 = (f32[2048]{0:T(1024)S(1)}, f32[2048]{0:T(1024)S(1)}, f32[2048]{0:T(1024)S(1)}, f32[2048]{0:T(1024)S(1)}) all-reduce(f32[2048]{0:T(1024)S(1)} %add.306, f32[2048]{0:T(1024)S(1)} %add.307, f32[2048]{0:T(1024)S(1)} %add.308, f32[2048]{0:T(1024)S(1)} %add.309), channel_id=12, replica_groups=mesh['dp'=32,'tensor'=4] {'dp'}, use_global_device_ids=true, to_apply=%region_60.61.clone | all-reduce | flops 8192 | bytes 65536
  867.5 2.9 pad_maximum_fusion.1
  874.5 6.4 reduce-scatter.23.cloned.1.call-done
  880.9 1.8 copy.168
  882.7 204.6 %reduce-scatter.21.cloned.1.call-done = f32[128,512]{0,1:T(8,128)} async-done(((f32[4096,512]{0,1:T(8,128)}), f32[128,512]{0,1:T(8,128)}) %reduce-scatter.21.cloned.1.call-update) | async-done | bytes 262160 | tf_op jit(solution)/shard_map/reduce_scatter | solution.py:249
  1087.3 1.8 copy.167
  1089.1 191.1 %reduce-scatter.19.cloned.1.call-done = f32[64,512]{1,0:T(8,128)} async-done(((f32[2048,512]{1,0:T(8,128)}), f32[64,512]{1,0:T(8,128)}) %reduce-scatter.19.cloned.1.call-update) | async-done | bytes 131088 | tf_op jit(solution)/shard_map/reduce_scatter | solution.py:248
  1280.2 190.8 %reduce-scatter.25.cloned.1.call-done = f32[512,64]{0,1:T(8,128)} async-done(((f32[512,2048]{0,1:T(8,128)}), f32[512,64]{0,1:T(8,128)}) %reduce-scatter.25.cloned.1.call-update) | async-done | bytes 131088 | tf_op jit(solution)/shard_map/reduce_scatter | solution.py:251
  1471.0 190.3 %reduce-scatter.17.cloned.1.call-done = f32[512,64]{0,1:T(8,128)} async-done(((f32[512,2048]{0,1:T(8,128)}), f32[512,64]{0,1:T(8,128)}) %reduce-scatter.17.cloned.1.call-update) | async-done | bytes 131088 | tf_op jit(solution)/shard_map/reduce_scatter | solution.py:247
  1661.3 190.8 %reduce-scatter.15.cloned.1.call-done = f32[64,512]{1,0:T(8,128)} async-done(((f32[2048,512]{1,0:T(8,128)}), f32[64,512]{1,0:T(8,128)}) %reduce-scatter.15.cloned.1.call-update) | async-done | bytes 131088 | tf_op jit(solution)/shard_map/reduce_scatter | solution.py:246
  1852.2 190.8 %reduce-scatter.13.cloned.1.call-done = f32[64,512]{1,0:T(8,128)} async-done(((f32[2048,512]{1,0:T(8,128)}), f32[64,512]{1,0:T(8,128)}) %reduce-scatter.13.cloned.1.call-update) | async-done | bytes 131088 | tf_op jit(solution)/shard_map/reduce_scatter | solution.py:245
  2043.0 191.4 %reduce-scatter.11.cloned.1.call-done = f32[64,512]{1,0:T(8,128)} async-done(((f32[2048,512]{1,0:T(8,128)}), f32[64,512]{1,0:T(8,128)}) %reduce-scatter.11.cloned.1.call-update) | async-done | bytes 131088 | tf_op jit(solution)/shard_map/reduce_scatter | solution.py:244
  2234.4 360.1 %reduce-scatter.27.cloned.1.call-done = f32[64,2048]{1,0:T(8,128)} async-done(((f32[2048,2048]{1,0:T(8,128)}), f32[64,2048]{1,0:T(8,128)}) %reduce-scatter.27.cloned.1.call-update) | async-done | bytes 524304 | tf_op jit(solution)/shard_map/reduce_scatter | solution.py:252
  2594.5 365.8 %reduce-scatter.29.cloned.1.call-done = f32[2048,64]{0,1:T(8,128)} async-done(((f32[2048,2048]{0,1:T(8,128)}), f32[2048,64]{0,1:T(8,128)}) %reduce-scatter.29.cloned.1.call-update) | async-done | bytes 524304 | tf_op jit(solution)/shard_map/reduce_scatter | solution.py:253
  (531 shorter events, 84.9 us)
Async XLA Ops:
  7.2 128.5 %copy-start = (bf16[512,2048]{1,0:T(8,128)(2,1)S(1)}, bf16[512,2048]{1,0:T(8,128)(2,1)}, u32[]{:S(2)}) copy-start(bf16[512,2048]{1,0:T(8,128)(2,1)} %param.31) | copy-start | bytes 6291460
  7.2 5.6 copy-start.65
  7.2 118.8 %all-reduce.24.cloned.1.call-start = ((), (), s32[]{:S(2)}) async-start(), calls=%async_computation.24 | async-start | bytes 8388608 | tf_op jit(solution)/shard_map/psum | solution.py:154
  7.3 5.5 copy-start.2
  8.1 117.9 %copy-start.119 = (pred[256]{0:T(512)(128)(4,1)}, pred[256]{0:T(512)(128)(4,1)S(1)}, u32[]{:S(2)}) copy-start(pred[256]{0:T(512)(128)(4,1)S(1)} %get-tuple-element.80) | copy-start | bytes 772
  8.1 117.9 %copy-start.135 = (pred[256]{0:T(512)(128)(4,1)}, pred[256]{0:T(512)(128)(4,1)S(1)}, u32[]{:S(2)}) copy-start(pred[256]{0:T(512)(128)(4,1)S(1)} %get-tuple-element.81) | copy-start | bytes 772
  8.2 5.2 copy-start.37
  8.2 5.2 copy-start.92
  9.9 9.8 copy-start.117
  12.2 6.0 copy-start.137
  12.8 7.0 copy-start.121
  13.3 4.9 copy-start.145
  31.7 201.1 %all-reduce.22.cloned.1.call-start = ((), (), s32[]{:S(2)}) async-start(), calls=%async_computation.23 | async-start | bytes 8388608 | tf_op jit(solution)/shard_map/psum | solution.py:169
  40.5 93.1 %copy-start.127 = (bf16[2,4,8,128]{3,2,1,0:T(8,128)(2,1)}, bf16[2,4,8,128]{3,2,1,0:T(8,128)(2,1)S(1)}, u32[]{:S(2)}) copy-start(bf16[2,4,8,128]{3,2,1,0:T(8,128)(2,1)S(1)} %fusion.73) | copy-start | bytes 49156
  139.9 223.6 %all-reduce.20.cloned.1.call-start = ((), (), s32[]{:S(2)}) async-start(), calls=%async_computation.22 | async-start | bytes 8388608 | tf_op jit(solution)/shard_map/psum | solution.py:181
  236.8 8.6 copy-start.4
  236.8 8.5 copy-start.139
  237.2 8.1 copy-start.151
  237.2 8.2 slice-start
  238.7 6.7 copy-start.160
  238.7 6.7 slice-start.1
  247.9 7.6 copy-start.49
  255.6 11.3 copy-start.96
  270.5 202.5 %all-reduce.18.cloned.1.call-start = ((), (), s32[]{:S(2)}) async-start(), calls=%async_computation.21 | async-start | bytes 8388608 | tf_op jit(solution)/shard_map/psum | solution.py:204
  363.4 5.5 copy-start.174
  363.4 5.5 copy-start.176
  363.4 5.5 copy-start.5
  363.4 5.5 copy-start.9
  363.4 5.5 copy-start.45
  363.5 5.9 copy-start.46
  363.5 5.9 copy-start.140
  363.5 5.9 copy-start.143
  363.5 5.9 copy-start.152
  363.5 5.9 copy-start.161
  380.2 291.8 %all-reduce.16.cloned.1.call-start = ((), (), s32[]{:S(2)}) async-start(), calls=%async_computation.20 | async-start | bytes 16777216 | tf_op jit(solution)/shard_map/psum | solution.py:173
  381.7 7.4 copy-start.58
  389.1 83.9 %copy-start.12 = (f32[256,2048]{1,0:T(8,128)S(1)}, f32[256,2048]{1,0:T(8,128)}, u32[]{:S(2)}) copy-start(f32[256,2048]{1,0:T(8,128)} %copy-done.11) | copy-start | bytes 6291460
  473.1 4.9 copy-start.170
  473.1 4.9 copy-start.172
  473.1 4.9 copy-start.14
  473.1 4.9 copy-start.43
  473.1 4.9 copy-start.44
  473.1 4.9 copy-start.155
  473.1 4.9 copy-start.158
  473.1 4.9 copy-start.164
  473.1 4.9 copy-start.167
  498.3 6.5 copy-start.79
  510.7 370.2 %reduce-scatter.23.cloned.1.call-start = ((), (), s32[]{:S(2)}) async-start(), calls=%async_computation.16 | async-start | bytes 8650752 | tf_op jit(solution)/shard_map/reduce_scatter | solution.py:250
  519.2 568.1 %reduce-scatter.21.cloned.1.call-start = ((), (), s32[]{:S(2)}) async-start(), calls=%async_computation.15 | async-start | bytes 8650752 | tf_op jit(solution)/shard_map/reduce_scatter | solution.py:249
  526.4 753.8 %reduce-scatter.19.cloned.1.call-start = ((), (), s32[]{:S(2)}) async-start(), calls=%async_computation.14 | async-start | bytes 4325376 | tf_op jit(solution)/shard_map/reduce_scatter | solution.py:248
  532.9 938.1 %reduce-scatter.25.cloned.1.call-start = ((), (), s32[]{:S(2)}) async-start(), calls=%async_computation.17 | async-start | bytes 4325376 | tf_op jit(solution)/shard_map/reduce_scatter | solution.py:251
  537.7 1123.6 %reduce-scatter.17.cloned.1.call-start = ((), (), s32[]{:S(2)}) async-start(), calls=%async_computation.13 | async-start | bytes 4325376 | tf_op jit(solution)/shard_map/reduce_scatter | solution.py:247
  544.0 1308.2 %reduce-scatter.15.cloned.1.call-start = ((), (), s32[]{:S(2)}) async-start(), calls=%async_computation.12 | async-start | bytes 4325376 | tf_op jit(solution)/shard_map/reduce_scatter | solution.py:246
  549.6 1493.4 %reduce-scatter.13.cloned.1.call-start = ((), (), s32[]{:S(2)}) async-start(), calls=%async_computation.11 | async-start | bytes 4325376 | tf_op jit(solution)/shard_map/reduce_scatter | solution.py:245
  554.5 1679.8 %reduce-scatter.11.cloned.1.call-start = ((), (), s32[]{:S(2)}) async-start(), calls=%async_computation.10 | async-start | bytes 4325376 | tf_op jit(solution)/shard_map/reduce_scatter | solution.py:244
  559.5 11.0 copy-start.95
  559.5 11.0 copy-start.141
  559.5 11.0 copy-start.153
  559.5 2035.0 %reduce-scatter.27.cloned.1.call-start = ((), (), s32[]{:S(2)}) async-start(), calls=%async_computation.18 | async-start | bytes 17301504 | tf_op jit(solution)/shard_map/reduce_scatter | solution.py:252
  560.1 10.4 copy-start.6
  585.0 2375.3 %reduce-scatter.29.cloned.1.call-start = ((), (), s32[]{:S(2)}) async-start(), calls=%async_computation.19 | async-start | bytes 17301504 | tf_op jit(solution)/shard_map/reduce_scatter | solution.py:253
  585.3 10.3 copy-start.32
  585.3 10.3 copy-start.51
  872.7 2087.6 %copy-start.1 = (bf16[512,2048]{1,0:T(8,128)(2,1)S(1)}, bf16[512,2048]{1,0:T(8,128)(2,1)}, u32[]{:S(2)}) copy-start(bf16[512,2048]{1,0:T(8,128)(2,1)} %param.31) | copy-start | bytes 6291460
  (141 other events, 272.7 us)
Sparse Core Ops, SparseCore 0:
  31.8 94.2 all-reduce.23
  140.0 92.7 all-reduce.21
  270.6 92.7 all-reduce.19
  380.3 92.7 all-reduce.17
  510.8 161.0 all-reduce.15
  674.2 206.6 reduce-scatter.22
  883.3 203.9 reduce-scatter.20
  1090.2 189.9 reduce-scatter.18
  1283.2 187.8 reduce-scatter.24
  1473.8 187.4 reduce-scatter.16
  1664.3 187.8 reduce-scatter.14
  1855.0 187.9 reduce-scatter.12
  2046.0 188.3 reduce-scatter.10
  2237.2 357.2 reduce-scatter.26
  2597.3 362.9 reduce-scatter.28
where the time goes:
time: 2980 us; the launch traced here: 2970 us
  waiting for transfers between devices  2490 us (84%)
  matrix products  186 us (6%)
  blocking collectives  184 us (6%)
  other arithmetic  45.3 us (2%)
  local copies, waits for them, and re-layouts  42.4 us (1%)
    reduce_scatter x1, waiting for transfers between devices, shards(): lax.psum_scatter(totals['contract'], 'dp', scatter_dimension=1, tiled=True)  366 us
    reduce_scatter x1, waiting for transfers between devices, shards(): lax.psum_scatter(totals['expand'], 'dp', scatter_dimension=0, tiled=True)  360 us
    reduce_scatter x1, waiting for transfers between devices, shards(): lax.psum_scatter(totals['text_key'], 'dp', scatter_dimension=0, tiled=True)  205 us
    reduce_scatter x1, waiting for transfers between devices, shards(): lax.psum_scatter(totals['self_query'], 'dp', scatter_dimension=0, tiled=T...  191 us
    reduce_scatter x1, waiting for transfers between devices, shards(): lax.psum_scatter(totals['text_query'], 'dp', scatter_dimension=0, tiled=T...  191 us
    reduce_scatter x1, waiting for transfers between devices, shards(): lax.psum_scatter(totals['self_value'], 'dp', scatter_dimension=0, tiled=T...  191 us
    reduce_scatter x1, waiting for transfers between devices, shards(): lax.psum_scatter(totals['self_key'], 'dp', scatter_dimension=0, tiled=True)  191 us
    reduce_scatter x1, waiting for transfers between devices, shards(): lax.psum_scatter(totals['text_output'], 'dp', scatter_dimension=1, tiled=...  191 us
  transfers between devices with their start and end apart: 15, of which 15 were waited for; matrix products, arithmetic and copies ran while one was open for 4% of the time, Pallas kernels for 0%

commit v1 on v0

v1 whole, which is shorter than its diff:
```python
import jax
import jax.numpy as jnp
from jax import lax
from jax.sharding import PartitionSpec as P

HEAD = 128
EPS = 1e-05

CORE = [(t, t ^ 1) for t in range(4)]
ZLO = [(t, t ^ 2) for t in range(4)]
ZHI = [(d, d ^ 1) for d in range(32)]


def along_x(step):
    return [(d, ((d // 8 + step) % 4) * 8 + d % 8) for d in range(32)]


def along_y(step):
    return [(d, (d // 8) * 8 + ((d // 2 + step) % 4) * 2 + d % 2) for d in range(32)]


def product(left, right):
    return jnp.dot(left, right, preferred_element_type=jnp.float32)


def outer_sum(left, right):
    return lax.dot_general(
        left, right, (((0,), (0,)), ((), ())), preferred_element_type=jnp.float32
    )


def back_product(left, right):
    return lax.dot_general(
        left, right, (((1,), (1,)), ((), ())), preferred_element_type=jnp.float32
    )


def low(value):
    return value.astype(jnp.bfloat16)


def layer_norm(rows, gain):
    mean = jnp.mean(rows, axis=-1, keepdims=True)
    centred = rows - mean
    spread = jnp.mean(centred * centred, axis=-1, keepdims=True)
    return centred * lax.rsqrt(spread + EPS) * gain


def norm_back(rows, gain, grad):
    mean = jnp.mean(rows, axis=-1, keepdims=True)
    centred = rows - mean
    spread = jnp.mean(centred * centred, axis=-1, keepdims=True)
    root = lax.rsqrt(spread + EPS)
    xhat = centred * root
    scaled = grad * gain
    row_grad = root * (
        scaled
        - jnp.mean(scaled, axis=-1, keepdims=True)
        - xhat * jnp.mean(scaled * xhat, axis=-1, keepdims=True)
    )
    return row_grad, jnp.sum(grad * xhat, axis=0)


def heads_of(rows):
    return rows.reshape(rows.shape[0], rows.shape[1] // HEAD, HEAD)


def attend_scores(query, keys, valid):
    scores = jnp.einsum("qhd,khd->hqk", query, keys, preferred_element_type=jnp.float32)
    scores = scores * HEAD ** (-0.5)
    if valid is None:
        return scores
    return jnp.where(valid[None, None, :], scores, -1e30)


def attend_forward(query, keys, values, valid):
    query, keys, values = heads_of(query), heads_of(keys), heads_of(values)
    scores = attend_scores(query, keys, valid)
    total = jax.nn.logsumexp(scores, axis=-1, keepdims=True)
    weights_low = low(jnp.exp(scores - total))
    mixed = jnp.einsum("hqk,khd->qhd", weights_low, values, preferred_element_type=jnp.float32)
    return low(mixed).reshape(mixed.shape[0], -1), total


def attend_backward(query, keys, values, valid, total, upstream):
    query, keys, values = heads_of(query), heads_of(keys), heads_of(values)
    upstream = heads_of(upstream)
    scale = HEAD ** (-0.5)
    probs = jnp.exp(attend_scores(query, keys, valid) - total)
    grad_values = jnp.einsum(
        "hqk,qhd->khd", low(probs), upstream, preferred_element_type=jnp.float32
    )
    grad_probs = jnp.einsum("qhd,khd->hqk", upstream, values, preferred_element_type=jnp.float32)
    inner = jnp.sum(grad_probs * probs, axis=-1, keepdims=True)
    grad_scores = low(probs * (grad_probs - inner))
    grad_query = (
        jnp.einsum("hqk,khd->qhd", grad_scores, keys, preferred_element_type=jnp.float32) * scale
    )
    grad_keys = (
        jnp.einsum("hqk,qhd->khd", grad_scores, query, preferred_element_type=jnp.float32) * scale
    )
    flat = lambda v: low(v).reshape(v.shape[0], -1)
    return flat(grad_query), flat(grad_keys), flat(grad_values)


def core_swap(value):
    return lax.ppermute(value, "tensor", CORE)


def half_sum(part):
    half = part.shape[0] // 2
    mine = part[:half] + core_swap(part[half:])
    return mine + lax.ppermute(mine, "tensor", ZLO)


def whole(mine):
    other = core_swap(mine * 0.5) * 2.0
    return jnp.concatenate([mine, other], axis=0)


def ring_sum(piece, along):
    right = lambda v: lax.ppermute(v, "dp", along(1))
    left = lambda v: lax.ppermute(v, "dp", along(-1))
    far_right = right(piece(2, 0))
    far_left = left(piece(2, 1))
    near_right = right(piece(1, 1))
    near_left = left(piece(3, 0))
    last_right = right(piece(1, 0) + far_right)
    last_left = left(piece(3, 1) + far_left)
    return (
        piece(0, 0) + near_left + last_right,
        piece(0, 1) + near_right + last_left,
    )


class Place:
    def __init__(self):
        dp = lax.axis_index("dp")
        self.x, self.y, self.z = dp // 8, (dp // 2) % 4, dp % 2
        self.core = lax.axis_index("tensor") % 2

    def fold(self, left, right, x_first):
        rows, width = left.shape[0], right.shape[1]
        if x_first:
            blocks = left.reshape(rows, 8, 256).transpose(1, 0, 2)
            one, two, first, second = self.x, self.y, along_x, along_y
        else:
            blocks = (
                left.reshape(rows, 2, 2, 4, 128).transpose(3, 1, 0, 2, 4).reshape(8, rows, 256)
            )
            one, two, first, second = self.y, self.x, along_y, along_x

        def piece(k, h):
            index = ((one + k) % 4) * 2 + h
            block = lax.dynamic_index_in_dim(blocks, index, 0, keepdims=False)
            return outer_sum(block, right)

        halves = ring_sum(piece, first)
        return self.fold_second(jnp.concatenate(halves, axis=0), two, second)

    def fold_second(self, summed, two, second):
        unit = summed.shape[0] // 8

        def piece(k, h):
            return lax.dynamic_slice_in_dim(
                summed, ((two + k) % 4) * 2 * unit + h * unit, unit, axis=0
            )

        return self.fold_third(*ring_sum(piece, second))

    def fold_third(self, low_half, high_half):
        upper = self.z == 1
        keep = jnp.where(upper, high_half, low_half)
        send = jnp.where(upper, low_half, high_half)
        return keep + lax.ppermute(send, "dp", ZHI)

    def mine_first(self, rows):
        half = rows.shape[0] // 2
        first, second = rows[:half], rows[half:]
        odd = self.core == 1
        return jnp.concatenate(
            [jnp.where(odd, second, first), jnp.where(odd, first, second)], axis=0
        )


def everyone(value, along):
    return [value] + [lax.ppermute(value, "dp", along(k)) for k in (1, 2, 3)]


def exchange(blocks, place, along):
    pick = lambda k: lax.dynamic_index_in_dim(blocks, (place + k) % 4, 0, keepdims=False)
    return [pick(0)] + [lax.ppermute(pick(k), "dp", along(k)) for k in (1, 2, 3)]


def shards(
    image,
    text,
    masked,
    text_len,
    cotangent,
    self_query,
    self_key,
    self_value,
    self_output,
    text_query,
    text_key,
    text_value,
    text_output,
    expand,
    contract,
    first_gain,
    second_gain,
    third_gain,
    mask_token,
):
    items, length, width = image.shape
    words = text.shape[1]
    half = length // 2
    place = Place()
    every = range(items)
    wide = jnp.float32

    text_rows = text.reshape(items * words, text.shape[2])
    cross_keys = low(product(text_rows, text_key))
    cross_values = low(product(text_rows, text_value))

    blocks = (text_rows.astype(wide) * 0.5).reshape(items * words, 4, -1).transpose(1, 0, 2)
    mine = jnp.concatenate(exchange(blocks, place.x, along_x), axis=0)
    blocks = mine.reshape(mine.shape[0], 4, -1).transpose(1, 0, 2)
    mine = jnp.concatenate(exchange(blocks, place.y, along_y), axis=0)
    text_columns = low(mine * 2.0)

    hidden, start, normed_one = [], [], []
    query, keys, values, self_rows, self_total = [], [], [], [], []
    first, normed_two = [], []
    for i in every:
        hidden.append(place.mine_first(masked[i].reshape(length, 1)) == 1)
        rows = place.mine_first(image[i]).astype(wide)
        start.append(jnp.where(hidden[i], mask_token[None, :], rows))
        normed_one.append(low(layer_norm(start[i], first_gain)))
        query.append(low(product(normed_one[i], self_query)))
        keys.append(low(product(normed_one[i], self_key)))
        values.append(low(product(normed_one[i], self_value)))
        mixed, total = attend_forward(query[i], keys[i], values[i], None)
        self_rows.append(mixed)
        self_total.append(total)
        first.append(start[i][:half] + half_sum(product(mixed, self_output)))
        normed_two.append(low(whole(layer_norm(first[i], second_gain))))

    cross_query, cross_rows, cross_total, present = [], [], [], []
    second, normed_three = [], []
    picked = lambda v, i: v[i * words : (i + 1) * words]
    for i in every:
        cross_query.append(low(product(normed_two[i], text_query)))
        present.append(jnp.arange(words) < text_len[i])
        mixed, total = attend_forward(
            cross_query[i], picked(cross_keys, i), picked(cross_values, i), present[i]
        )
        cross_rows.append(mixed)
        cross_total.append(total)
        second.append(first[i] + half_sum(product(mixed, text_output)))
        normed_three.append(low(whole(layer_norm(second[i], third_gain))))

    upstream, active, grad_raised = [], [], []
    grad_second, cross_out_grad = [], []
    third = 0.0
    for i in every:
        upstream.append(place.mine_first(cotangent[i]))
        raised = product(normed_three[i], expand)
        gelu, pull = jax.vjp(jax.nn.gelu, raised)
        active.append(low(gelu))
        grad_raised.append(low(pull(back_product(upstream[i], contract))[0]))
        grad = half_sum(back_product(grad_raised[i], expand))
        row_grad, gain_grad = norm_back(second[i], third_gain, grad)
        third = third + gain_grad
        grad_second.append(upstream[i][:half].astype(wide) + row_grad)
        cross_out_grad.append(low(whole(grad_second[i])))

    both = lambda parts: jnp.concatenate(parts, axis=0)
    contract_t = place.fold(both(upstream), both(active), False)
    expand_grad = place.fold(both(normed_three), both(grad_raised), True)
    text_output_t = place.fold(both(cross_out_grad), both(cross_rows), True)

    grad_cq, text_kv, grad_first, self_out_grad = [], [], [], []
    second_sum = 0.0
    for i in every:
        grad_mixed = low(back_product(cross_out_grad[i], text_output))
        grad_q, grad_k, grad_v = attend_backward(
            cross_query[i],
            picked(cross_keys, i),
            picked(cross_values, i),
            present[i],
            cross_total[i],
            grad_mixed,
        )
        grad_cq.append(grad_q)
        text_kv.append(jnp.concatenate([grad_k, grad_v], axis=1))
        grad = half_sum(back_product(grad_q, text_query))
        row_grad, gain_grad = norm_back(first[i], second_gain, grad)
        second_sum = second_sum + gain_grad
        grad_first.append(grad_second[i] + row_grad)
        self_out_grad.append(low(whole(grad_first[i])))

    text_query_grad = place.fold(both(normed_two), both(grad_cq), False)
    self_output_t = place.fold(both(self_out_grad), both(self_rows), True)

    gathered = jnp.concatenate(everyone(both(text_kv).astype(wide) * 0.5, along_x), axis=0)
    gathered = jnp.concatenate(everyone(gathered, along_y), axis=0)
    gathered = low(gathered * 2.0)
    text_grads = outer_sum(text_columns, gathered)
    middle = text_grads.shape[0] // 2
    text_grads = place.fold_third(text_grads[:middle], text_grads[middle:])

    grad_qkv, grad_start = [], []
    first_sum, mask_sum = 0.0, 0.0
    for i in every:
        grad_mixed = low(back_product(self_out_grad[i], self_output))
        grad_q, grad_k, grad_v = attend_backward(
            query[i], keys[i], values[i], None, self_total[i], grad_mixed
        )
        grad_qkv.append((grad_q, grad_k, grad_v))
        shares = (
            back_product(grad_q, self_query)
            + back_product(grad_k, self_key)
            + back_product(grad_v, self_value)
        )
        grad = half_sum(shares)
        row_grad, gain_grad = norm_back(start[i][:half], first_gain, grad)
        first_sum = first_sum + gain_grad
        result = grad_first[i] + row_grad
        mask_sum = mask_sum + jnp.sum(jnp.where(hidden[i][:half], result, 0.0), axis=0)
        grad_start.append(jnp.where(hidden[i][:half], 0.0, result))

    normed = both(normed_one)
    grad_q, grad_k, grad_v = [both(list(parts)) for parts in zip(*grad_qkv)]
    middle = grad_k.shape[1] // 2
    qk = place.fold(normed, jnp.concatenate([grad_q, grad_k[:, :middle]], axis=1), True)
    kv = place.fold(normed, jnp.concatenate([grad_k[:, middle:], grad_v], axis=1), False)
    cut = grad_q.shape[1]
    self_query_grad = qk[:, :cut]
    self_key_grad = jnp.concatenate([qk[:, cut:], kv[:, :middle]], axis=1)
    self_value_grad = kv[:, middle:]

    small = jnp.stack([first_sum, second_sum, third, mask_sum])
    small = small + core_swap(small)
    small = sum(everyone(small, along_x))
    small = sum(everyone(small, along_y))
    small = small + lax.ppermute(small, "dp", ZHI)
    share = width // 32
    small = lax.dynamic_slice_in_dim(small, lax.axis_index("dp") * share, share, axis=1)

    def finished(value):
        both_halves = whole(value)
        return low(place.mine_first(both_halves))

    layer_out = []
    for i in every:
        total = half_sum(product(active[i], contract))
        layer_out.append(finished(second[i] + total))
    image_grad = [finished(g) for g in grad_start]

    cut = text_grads.shape[1] // 2
    return (
        jnp.stack(layer_out),
        jnp.stack(image_grad),
        self_query_grad,
        self_key_grad,
        self_value_grad,
        self_output_t.T,
        text_query_grad,
        text_grads[:, :cut],
        text_grads[:, cut:],
        text_output_t.T,
        expand_grad,
        contract_t.T,
        small[0],
        small[1],
        small[2],
        small[3],
    )


def solution(mesh):
    rows, split = P("dp", None, None), P(None, "tensor")
    turned, grads, grads_t = P("tensor", None), P("dp", "tensor"), P("tensor", "dp")
    return jax.shard_map(
        shards,
        mesh=mesh,
        in_specs=(
            rows,
            rows,
            P("dp", None),
            P("dp"),
            rows,
            split,
            split,
            split,
            turned,
            split,
            split,
            split,
            turned,
            split,
            turned,
            P(),
            P(),
            P(),
            P(),
        ),
        out_specs=(
            rows,
            rows,
            grads,
            grads,
            grads,
            grads_t,
            grads,
            grads,
            grads,
            grads_t,
            grads,
            grads_t,
            P("dp"),
            P("dp"),
            P("dp"),
            P("dp"),
        ),
        check_vma=False,
    )
```

time: 2980 us -> 1030 us (0.35)
  waiting for transfers between devices: 2490 us -> 502 us
  blocking collectives: 184 us -> 0 us
  starting transfers between devices: 2.13 us -> 175 us
  local copies, waits for them, and re-layouts: 42.4 us -> 133 us
  matrix products: 186 us -> 121 us
  other arithmetic: 45.3 us -> 81.1 us
    reduce_scatter x10 -> x0, waiting for transfers between devices: 2080 us -> none  [the longest x1 366 us: shards(): lax.psum_scatter(totals['contract'], 'dp', scatter_dimension=1, tiled=True)]
    ppermute x0 -> x148, waiting for transfers between devices: none -> 502 us  [the longest x42 147 us: ring_sum(): right = lambda v: lax.ppermute(v, 'dp', along(1))]
    psum x5 -> x0, waiting for transfers between devices: 408 us -> none  [the longest x1 92.9 us: shards(): grad_three = lax.psum(back_product(grad_raised, expand), 'tensor')]
    unnamed x1 -> x0, blocking collectives: 184 us -> none
    ppermute x0 -> x148, starting transfers between devices: none -> 175 us  [the longest x42 87.2 us: ring_sum(): left = lambda v: lax.ppermute(v, 'dp', along(-1))]
    dot_general x20 -> x57, matrix products: 84.2 us -> 44.5 us  [outer_sum(): lax.dot_general(left, right, (((0,), (0,)), ((), ())), preferred_element_...]
    select_n x0 -> x20, local copies, waits for them, and re-layouts: none -> 39.3 us  [the longest x10 19.7 us: mine_first(): jnp.where(odd, first, second)]
  transfers between devices with their start and end apart: 15 -> 148, of which waited for: 15 -> 68; matrix products, arithmetic and copies ran while one was open for 4% -> 27% of each run, Pallas kernels for 0% -> 0%
where the time goes in v1:
time: 1030 us; the launch traced here: 1020 us
  waiting for transfers between devices  502 us (49%)
  starting transfers between devices  175 us (17%)
  local copies, waits for them, and re-layouts  133 us (13%)
  matrix products  121 us (12%)
  other arithmetic  81.1 us (8%)
    ppermute x42, waiting for transfers between devices, ring_sum(): right = lambda v: lax.ppermute(v, 'dp', along(1))  147 us
    ppermute x12, waiting for transfers between devices, half_sum(): return mine + lax.ppermute(mine, 'tensor', ZLO)  140 us
    ppermute x42, waiting for transfers between devices, ring_sum(): left = lambda v: lax.ppermute(v, 'dp', along(-1))  115 us
    ppermute x42, starting transfers between devices, ring_sum(): left = lambda v: lax.ppermute(v, 'dp', along(-1))  87.2 us
    ppermute x12, waiting for transfers between devices, everyone(): return [value] + [lax.ppermute(value, 'dp', along(k)) for k in (1, 2, 3)]  74.3 us
    dot_general x57, matrix products, outer_sum(): lax.dot_general(left, right, (((0,), (0,)), ((), ())), preferred_element_...  44.5 us
    unnamed x474, local copies, waits for them, and re-layouts  43.4 us
    dot_general x18, matrix products, product(): return jnp.dot(left, right, preferred_element_type=jnp.float32)  39.5 us
  transfers between devices with their start and end apart: 148, of which 68 were waited for; matrix products, arithmetic and copies ran while one was open for 27% of the time, Pallas kernels for 0%

profile of v1, /device:TPU:0, one launch (start us, length us, event | category | flops | bytes accessed | tf_op | source)
XLA Modules:
  0.0 1017.9 jit_solution(16512844002671207686)
XLA Ops:
  11.2 3.2 convolution_convert_fusion.15
  31.8 16.7 %collective-permute-done.1 = f32[128,2048]{1,0:T(8,128)} collective-permute-done((f32[128,2048]{1,0:T(8,128)S(1)}, f32[128,2048]{1,0:T(8,128)}, u32[]{:S(2)}, u32[]{:S(2)}) %collective-permute-start.1) | collective-permute-done | bytes 1048608 | tf_op jit(solution)/shard_map/ppermute | solution.py:113
  71.9 3.2 constant_dynamic-slice_fusion.6
  83.5 9.3 collective-permute-done.4
  123.7 7.7 multiply_convert_fusion.7
  131.5 5.4 fusion.10
  170.4 3.9 multiply_convert_fusion.3
  182.9 19.0 %collective-permute-done.19 = f32[128,2048]{1,0:T(8,128)S(1)} collective-permute-done((f32[128,2048]{1,0:T(8,128)S(1)}, f32[128,2048]{1,0:T(8,128)S(1)}, u32[]{:S(2)}, u32[]{:S(2)}) %collective-permute-start.19) | collective-permute-done | bytes 1048608 | tf_op jit(solution)/shard_map/ppermute | solution.py:113
  205.6 18.3 %collective-permute-done.7 = f32[128,2048]{1,0:T(8,128)S(1)} collective-permute-done((f32[128,2048]{1,0:T(8,128)S(1)}, f32[128,2048]{1,0:T(8,128)S(1)}, u32[]{:S(2)}, u32[]{:S(2)}) %collective-permute-start.7) | collective-permute-done | bytes 1048608 | tf_op jit(solution)/shard_map/ppermute | solution.py:113
  250.7 19.4 %collective-permute-done.10 = f32[128,2048]{1,0:T(8,128)S(1)} collective-permute-done((f32[128,2048]{1,0:T(8,128)S(1)}, f32[128,2048]{1,0:T(8,128)S(1)}, u32[]{:S(2)}, u32[]{:S(2)}) %collective-permute-start.10) | collective-permute-done | bytes 1048608 | tf_op jit(solution)/shard_map/ppermute | solution.py:113
  288.7 8.5 collective-permute-done.22
  341.1 9.4 collective-permute-done.13
  353.8 18.5 %collective-permute-done.25 = f32[128,2048]{1,0:T(8,128)S(1)} collective-permute-done((f32[128,2048]{1,0:T(8,128)S(1)}, f32[128,2048]{1,0:T(8,128)S(1)}, u32[]{:S(2)}, u32[]{:S(2)}) %collective-permute-start.25) | collective-permute-done | bytes 1048608 | tf_op jit(solution)/shard_map/ppermute | solution.py:113
  374.8 7.6 multiply_convert_fusion.5
  382.4 7.5 fusion.17
  392.5 5.7 fusion.516
  418.3 31.6 %collective-permute-done.115 = f32[256,2048]{1,0:T(8,128)S(1)} collective-permute-done((f32[256,2048]{1,0:T(8,128)S(1)}, f32[256,2048]{1,0:T(8,128)S(1)}, u32[]{:S(2)}, u32[]{:S(2)}) %collective-permute-start.115) | collective-permute-done | bytes 2097184 | tf_op jit(solution)/shard_map/ppermute | solution.py:122
  453.7 20.9 %collective-permute-done.16 = f32[128,2048]{1,0:T(8,128)S(1)} collective-permute-done((f32[128,2048]{1,0:T(8,128)S(1)}, f32[128,2048]{1,0:T(8,128)S(1)}, u32[]{:S(2)}, u32[]{:S(2)}) %collective-permute-start.16) | collective-permute-done | bytes 1048608 | tf_op jit(solution)/shard_map/ppermute | solution.py:113
  482.1 19.0 %collective-permute-done.131 = f32[256,2048]{1,0:T(8,128)S(1)} collective-permute-done((f32[256,2048]{1,0:T(8,128)}, f32[256,2048]{1,0:T(8,128)S(1)}, u32[]{:S(2)}, u32[]{:S(2)}) %collective-permute-start.131) | collective-permute-done | bytes 2097184 | tf_op jit(solution)/shard_map/ppermute | solution.py:123
  512.8 4.8 collective-permute-done.91
  520.5 6.5 collective-permute-done.114
  531.0 19.9 %collective-permute-done.117 = f32[256,2048]{1,0:T(8,128)S(1)} collective-permute-done((f32[256,2048]{1,0:T(8,128)S(1)}, f32[256,2048]{1,0:T(8,128)S(1)}, u32[]{:S(2)}, u32[]{:S(2)}) %collective-permute-start.117) | collective-permute-done | bytes 2097184 | tf_op jit(solution)/shard_map/ppermute | solution.py:122
  550.8 45.6 %collective-permute-done.94 = f32[32,1024]{1,0:T(8,128)S(1)} collective-permute-done((f32[32,1024]{1,0:T(8,128)S(1)}, f32[32,1024]{1,0:T(8,128)S(1)}, u32[]{:S(2)}, u32[]{:S(2)}) %collective-permute-start.94) | collective-permute-done | bytes 131104 | tf_op jit(solution)/shard_map/ppermute | solution.py:187
  598.5 3.2 collective-permute-start.105
  603.5 7.1 collective-permute-done.79
  612.3 3.4 collective-permute-start.99
  619.1 10.1 collective-permute-done.98
  630.4 9.0 collective-permute-done.99
  639.4 3.4 collective-permute-start.132
  648.1 5.4 collective-permute-done.119
  655.3 29.0 %collective-permute-done.127 = f32[256,2048]{1,0:T(8,128)S(1)} collective-permute-done((f32[256,2048]{1,0:T(8,128)}, f32[256,2048]{1,0:T(8,128)S(1)}, u32[]{:S(2)}, u32[]{:S(2)}) %collective-permute-start.127) | collective-permute-done | bytes 2097184 | tf_op jit(solution)/shard_map/ppermute | solution.py:123
  687.2 37.0 %collective-permute-done.130 = f32[256,2048]{1,0:T(8,128)S(1)} collective-permute-done((f32[256,2048]{1,0:T(8,128)}, f32[256,2048]{1,0:T(8,128)S(1)}, u32[]{:S(2)}, u32[]{:S(2)}) %collective-permute-start.130) | collective-permute-done | bytes 2097184 | tf_op jit(solution)/shard_map/ppermute | solution.py:122
  724.1 5.1 collective-permute-done.132
  730.6 4.2 collective-permute-done.75
  741.7 6.6 collective-permute-done.101
  748.3 3.5 collective-permute-start.100
  751.8 4.4 collective-permute-start.121
  769.4 4.1 collective-permute-start.84
  776.2 3.3 collective-permute-start.110
  784.7 6.3 collective-permute-done.87
  793.2 5.4 collective-permute-done.113
  806.0 3.2 collective-permute-done.122
  812.2 5.4 collective-permute-done.125
  817.6 3.2 collective-permute-start.136
  823.3 5.0 collective-permute-done.138
  833.9 5.6 collective-permute-done.139
  861.4 3.2 collective-permute-start.53
  877.4 6.4 collective-permute-done.62
  883.8 6.6 collective-permute-done.64
  891.1 3.3 collective-permute-start.40
  897.3 3.2 collective-permute-done.69
  907.0 5.4 collective-permute-done.40
  912.4 3.2 collective-permute-start.71
  919.0 3.2 collective-permute-start.41
  924.7 4.5 collective-permute-done.36
  931.9 5.4 collective-permute-done.39
  937.3 8.4 collective-permute-done.38
  952.4 8.7 collective-permute-done.52
  961.6 3.4 collective-permute-start.56
  966.5 3.5 collective-permute-start.44
  972.4 4.4 collective-permute-start.45
  991.9 3.3 collective-permute-start.143
  997.0 3.7 collective-permute-done.142
  1009.1 3.6 collective-permute-start.147
  (1057 shorter events, 445.2 us)
Async XLA Ops:
  23.0 25.5 %collective-permute-start.1 = (f32[128,2048]{1,0:T(8,128)S(1)}, f32[128,2048]{1,0:T(8,128)}, u32[]{:S(2)}, u32[]{:S(2)}) collective-permute-start(f32[128,2048]{1,0:T(8,128)S(1)} %slice_add_fusion.11), channel_id=1, source_target_pairs={{0,2},{1,3},{2,0},{3,1},{4,6},{5,7},{6,4},{7,5},{8,10},{9,11},{10,... | collective-permute-start | bytes 3145736 | tf_op jit(solution)/shard_map/ppermute | solution.py:113
  64.2 178.8 %collective-permute-start.9 = (f32[128,2048]{1,0:T(8,128)}, f32[128,2048]{1,0:T(8,128)}, u32[]{:S(2)}, u32[]{:S(2)}) collective-permute-start(f32[128,2048]{1,0:T(8,128)} %slice.289), channel_id=1, source_target_pairs={{0,1},{1,0},{2,3},{3,2},{4,5},{5,4},{6,7},{7,6},{8,9},{9,8},{10,11... | collective-permute-start | bytes 3145736 | tf_op jit(solution)/shard_map/ppermute | solution.py:107
  67.0 25.7 %collective-permute-start.4 = (f32[128,2048]{1,0:T(8,128)}, f32[128,2048]{1,0:T(8,128)}, u32[]{:S(2)}, u32[]{:S(2)}) collective-permute-start(f32[128,2048]{1,0:T(8,128)} %slice_add_fusion.10), channel_id=1, source_target_pairs={{0,2},{1,3},{2,0},{3,1},{4,6},{5,7},{6,4},{7,5},{8,10},{9,11},{10,... | collective-permute-start | bytes 3145736 | tf_op jit(solution)/shard_map/ppermute | solution.py:113
  75.7 152.9 %collective-permute-start.88 = (f32[32,1024]{1,0:T(8,128)}, f32[32,1024]{1,0:T(8,128)}, u32[]{:S(2)}, u32[]{:S(2)}) collective-permute-start(f32[32,1024]{1,0:T(8,128)} %bitcast.540), channel_id=1, source_target_pairs={{0,32},{4,36},{8,40},{12,44},{16,48},{20,52},{24,56},{28,60},{32,6... | collective-permute-start | bytes 393224 | tf_op jit(solution)/shard_map/ppermute | solution.py:192
  77.9 151.7 %collective-permute-start.89 = (f32[32,1024]{1,0:T(8,128)}, f32[32,1024]{1,0:T(8,128)}, u32[]{:S(2)}, u32[]{:S(2)}) collective-permute-start(f32[32,1024]{1,0:T(8,128)} %bitcast.539), channel_id=1, source_target_pairs={{0,64},{4,68},{8,72},{12,76},{16,80},{20,84},{24,88},{28,92},{32,9... | collective-permute-start | bytes 393224 | tf_op jit(solution)/shard_map/ppermute | solution.py:192
  97.0 24.4 %collective-permute-start.5 = (f32[128,2048]{1,0:T(8,128)}, f32[128,2048]{1,0:T(8,128)}, u32[]{:S(2)}, u32[]{:S(2)}) collective-permute-start(f32[128,2048]{1,0:T(8,128)} %get-tuple-element.132), channel_id=1, source_target_pairs={{0,1},{1,0},{2,3},{3,2},{4,5},{5,4},{6,7},{7,6},{8,9},{9,8},{10,11... | collective-permute-start | bytes 3145736 | tf_op jit(solution)/shard_map/ppermute | solution.py:107
  140.5 33.8 %collective-permute-start.18 = (f32[128,2048]{1,0:T(8,128)}, f32[128,2048]{1,0:T(8,128)}, u32[]{:S(2)}, u32[]{:S(2)}) collective-permute-start(f32[128,2048]{1,0:T(8,128)} %slice.297), channel_id=1, source_target_pairs={{0,1},{1,0},{2,3},{3,2},{4,5},{5,4},{6,7},{7,6},{8,9},{9,8},{10,11... | collective-permute-start | bytes 3145736 | tf_op jit(solution)/shard_map/ppermute | solution.py:107
  146.1 33.3 %collective-permute-start.6 = (f32[128,2048]{1,0:T(8,128)}, f32[128,2048]{1,0:T(8,128)}, u32[]{:S(2)}, u32[]{:S(2)}) collective-permute-start(f32[128,2048]{1,0:T(8,128)} %slice.286), channel_id=1, source_target_pairs={{0,1},{1,0},{2,3},{3,2},{4,5},{5,4},{6,7},{7,6},{8,9},{9,8},{10,11... | collective-permute-start | bytes 3145736 | tf_op jit(solution)/shard_map/ppermute | solution.py:107
  175.8 26.0 %collective-permute-start.19 = (f32[128,2048]{1,0:T(8,128)S(1)}, f32[128,2048]{1,0:T(8,128)S(1)}, u32[]{:S(2)}, u32[]{:S(2)}) collective-permute-start(f32[128,2048]{1,0:T(8,128)S(1)} %slice_add_fusion.5), channel_id=1, source_target_pairs={{0,2},{1,3},{2,0},{3,1},{4,6},{5,7},{6,4},{7,5},{8,10},{9,11},{10,... | collective-permute-start | bytes 3145736 | tf_op jit(solution)/shard_map/ppermute | solution.py:113
  180.8 43.1 %collective-permute-start.7 = (f32[128,2048]{1,0:T(8,128)S(1)}, f32[128,2048]{1,0:T(8,128)S(1)}, u32[]{:S(2)}, u32[]{:S(2)}) collective-permute-start(f32[128,2048]{1,0:T(8,128)S(1)} %slice_add_fusion.9), channel_id=1, source_target_pairs={{0,2},{1,3},{2,0},{3,1},{4,6},{5,7},{6,4},{7,5},{8,10},{9,11},{10,... | collective-permute-start | bytes 3145736 | tf_op jit(solution)/shard_map/ppermute | solution.py:113
  201.9 28.7 %collective-permute-start.90 = (f32[32,1024]{1,0:T(8,128)}, f32[32,1024]{1,0:T(8,128)}, u32[]{:S(2)}, u32[]{:S(2)}) collective-permute-start(f32[32,1024]{1,0:T(8,128)} %bitcast.538), channel_id=1, source_target_pairs={{0,96},{4,100},{8,104},{12,108},{16,112},{20,116},{24,120},{28,124... | collective-permute-start | bytes 393224 | tf_op jit(solution)/shard_map/ppermute | solution.py:192
  238.0 273.0 %collective-permute-start.93 = (f32[128,256]{1,0:T(8,128)}, f32[128,256]{1,0:T(8,128)}, u32[]{:S(2)}, u32[]{:S(2)}) collective-permute-start(f32[128,256]{1,0:T(8,128)} %bitcast.534), channel_id=1, source_target_pairs={{0,24},{4,28},{8,0},{12,4},{16,8},{20,12},{24,16},{28,20},{32,56},... | collective-permute-start | bytes 393224 | tf_op jit(solution)/shard_map/ppermute | solution.py:192
  244.4 25.8 %collective-permute-start.10 = (f32[128,2048]{1,0:T(8,128)S(1)}, f32[128,2048]{1,0:T(8,128)S(1)}, u32[]{:S(2)}, u32[]{:S(2)}) collective-permute-start(f32[128,2048]{1,0:T(8,128)S(1)} %slice_add_fusion.8), channel_id=1, source_target_pairs={{0,2},{1,3},{2,0},{3,1},{4,6},{5,7},{6,4},{7,5},{8,10},{9,11},{10,... | collective-permute-start | bytes 3145736 | tf_op jit(solution)/shard_map/ppermute | solution.py:113
  250.7 20.7 %collective-permute-start.21 = (f32[128,2048]{1,0:T(8,128)S(1)}, f32[128,2048]{1,0:T(8,128)S(1)}, u32[]{:S(2)}, u32[]{:S(2)}) collective-permute-start(f32[128,2048]{1,0:T(8,128)S(1)} %slice.299), channel_id=1, source_target_pairs={{0,1},{1,0},{2,3},{3,2},{4,5},{5,4},{6,7},{7,6},{8,9},{9,8},{10,11... | collective-permute-start | bytes 3145736 | tf_op jit(solution)/shard_map/ppermute | solution.py:107
  272.5 24.8 %collective-permute-start.22 = (f32[128,2048]{1,0:T(8,128)}, f32[128,2048]{1,0:T(8,128)}, u32[]{:S(2)}, u32[]{:S(2)}) collective-permute-start(f32[128,2048]{1,0:T(8,128)} %slice_add_fusion.4), channel_id=1, source_target_pairs={{0,2},{1,3},{2,0},{3,1},{4,6},{5,7},{6,4},{7,5},{8,10},{9,11},{10,... | collective-permute-start | bytes 3145736 | tf_op jit(solution)/shard_map/ppermute | solution.py:113
  324.3 26.2 %collective-permute-start.13 = (f32[128,2048]{1,0:T(8,128)S(1)}, f32[128,2048]{1,0:T(8,128)}, u32[]{:S(2)}, u32[]{:S(2)}) collective-permute-start(f32[128,2048]{1,0:T(8,128)S(1)} %slice_add_fusion.7), channel_id=1, source_target_pairs={{0,2},{1,3},{2,0},{3,1},{4,6},{5,7},{6,4},{7,5},{8,10},{9,11},{10,... | collective-permute-start | bytes 3145736 | tf_op jit(solution)/shard_map/ppermute | solution.py:113
  340.8 31.5 %collective-permute-start.25 = (f32[128,2048]{1,0:T(8,128)S(1)}, f32[128,2048]{1,0:T(8,128)S(1)}, u32[]{:S(2)}, u32[]{:S(2)}) collective-permute-start(f32[128,2048]{1,0:T(8,128)S(1)} %slice_add_fusion.3), channel_id=1, source_target_pairs={{0,2},{1,3},{2,0},{3,1},{4,6},{5,7},{6,4},{7,5},{8,10},{9,11},{10,... | collective-permute-start | bytes 3145736 | tf_op jit(solution)/shard_map/ppermute | solution.py:113
  352.6 22.1 %collective-permute-start.14 = (f32[128,2048]{1,0:T(8,128)S(1)}, f32[128,2048]{1,0:T(8,128)S(1)}, u32[]{:S(2)}, u32[]{:S(2)}) collective-permute-start(f32[128,2048]{1,0:T(8,128)S(1)} %get-tuple-element.136), channel_id=1, source_target_pairs={{0,1},{1,0},{2,3},{3,2},{4,5},{5,4},{6,7},{7,6},{8,9},{9,8},{10,11... | collective-permute-start | bytes 3145736 | tf_op jit(solution)/shard_map/ppermute | solution.py:107
  392.4 19.7 %collective-permute-start.27 = (f32[128,2048]{1,0:T(8,128)S(1)}, f32[128,2048]{1,0:T(8,128)S(1)}, u32[]{:S(2)}, u32[]{:S(2)}) collective-permute-start(f32[128,2048]{1,0:T(8,128)S(1)} %slice.303), channel_id=1, source_target_pairs={{0,1},{1,0},{2,3},{3,2},{4,5},{5,4},{6,7},{7,6},{8,9},{9,8},{10,11... | collective-permute-start | bytes 3145736 | tf_op jit(solution)/shard_map/ppermute | solution.py:107
  398.3 19.9 %collective-permute-start.15 = (f32[128,2048]{1,0:T(8,128)S(1)}, f32[128,2048]{1,0:T(8,128)S(1)}, u32[]{:S(2)}, u32[]{:S(2)}) collective-permute-start(f32[128,2048]{1,0:T(8,128)S(1)} %slice.295), channel_id=1, source_target_pairs={{0,1},{1,0},{2,3},{3,2},{4,5},{5,4},{6,7},{7,6},{8,9},{9,8},{10,11... | collective-permute-start | bytes 3145736 | tf_op jit(solution)/shard_map/ppermute | solution.py:107
  400.2 49.7 %collective-permute-start.115 = (f32[256,2048]{1,0:T(8,128)S(1)}, f32[256,2048]{1,0:T(8,128)S(1)}, u32[]{:S(2)}, u32[]{:S(2)}) collective-permute-start(f32[256,2048]{1,0:T(8,128)S(1)} %fusion.174), channel_id=1, source_target_pairs={{0,32},{4,36},{8,40},{12,44},{16,48},{20,52},{24,56},{28,60},{32,6... | collective-permute-start | bytes 6291464 | tf_op jit(solution)/shard_map/ppermute | solution.py:122
  402.9 73.3 %collective-permute-start.118 = (f32[256,2048]{1,0:T(8,128)S(1)}, f32[256,2048]{1,0:T(8,128)S(1)}, u32[]{:S(2)}, u32[]{:S(2)}) collective-permute-start(f32[256,2048]{1,0:T(8,128)S(1)} %fusion.168), channel_id=1, source_target_pairs={{0,96},{4,100},{8,104},{12,108},{16,112},{20,116},{24,120},{28,124... | collective-permute-start | bytes 6291464 | tf_op jit(solution)/shard_map/ppermute | solution.py:123
  412.2 40.2 %collective-permute-start.28 = (f32[128,2048]{1,0:T(8,128)S(1)}, f32[128,2048]{1,0:T(8,128)S(1)}, u32[]{:S(2)}, u32[]{:S(2)}) collective-permute-start(f32[128,2048]{1,0:T(8,128)S(1)} %slice_add_fusion.2), channel_id=1, source_target_pairs={{0,2},{1,3},{2,0},{3,1},{4,6},{5,7},{6,4},{7,5},{8,10},{9,11},{10,... | collective-permute-start | bytes 3145736 | tf_op jit(solution)/shard_map/ppermute | solution.py:113
  418.2 60.3 %collective-permute-start.128 = (f32[256,2048]{1,0:T(8,128)S(1)}, f32[256,2048]{1,0:T(8,128)S(1)}, u32[]{:S(2)}, u32[]{:S(2)}) collective-permute-start(f32[256,2048]{1,0:T(8,128)S(1)} %fusion.162), channel_id=1, source_target_pairs={{0,8},{4,12},{8,16},{12,20},{16,24},{20,28},{24,0},{28,4},{32,40},... | collective-permute-start | bytes 6291464 | tf_op jit(solution)/shard_map/ppermute | solution.py:122
  449.9 24.8 %collective-permute-start.16 = (f32[128,2048]{1,0:T(8,128)S(1)}, f32[128,2048]{1,0:T(8,128)S(1)}, u32[]{:S(2)}, u32[]{:S(2)}) collective-permute-start(f32[128,2048]{1,0:T(8,128)S(1)} %slice_add_fusion.6), channel_id=1, source_target_pairs={{0,2},{1,3},{2,0},{3,1},{4,6},{5,7},{6,4},{7,5},{8,10},{9,11},{10,... | collective-permute-start | bytes 3145736 | tf_op jit(solution)/shard_map/ppermute | solution.py:113
  452.4 48.7 %collective-permute-start.131 = (f32[256,2048]{1,0:T(8,128)}, f32[256,2048]{1,0:T(8,128)S(1)}, u32[]{:S(2)}, u32[]{:S(2)}) collective-permute-start(f32[256,2048]{1,0:T(8,128)} %fusion.156), channel_id=1, source_target_pairs={{0,24},{4,28},{8,0},{12,4},{16,8},{20,12},{24,16},{28,20},{32,56},... | collective-permute-start | bytes 6291464 | tf_op jit(solution)/shard_map/ppermute | solution.py:123
  474.7 36.5 %collective-permute-start.92 = (f32[128,256]{1,0:T(8,128)S(1)}, f32[128,256]{1,0:T(8,128)S(1)}, u32[]{:S(2)}, u32[]{:S(2)}) collective-permute-start(f32[128,256]{1,0:T(8,128)S(1)} %bitcast.713), channel_id=1, source_target_pairs={{0,16},{4,20},{8,24},{12,28},{16,0},{20,4},{24,8},{28,12},{32,48},... | collective-permute-start | bytes 393224 | tf_op jit(solution)/shard_map/ppermute | solution.py:192
  476.2 26.0 %collective-permute-start.29 = (f32[128,2048]{1,0:T(8,128)S(1)}, f32[128,2048]{1,0:T(8,128)S(1)}, u32[]{:S(2)}, u32[]{:S(2)}) collective-permute-start(f32[128,2048]{1,0:T(8,128)S(1)} %broadcast_multiply_fusion.1), channel_id=1, source_target_pairs={{0,1},{1,0},{2,3},{3,2},{4,5},{5,4},{6,7},{7,6},{8,9},{9,8},{10,11... | collective-permute-start | bytes 3145736 | tf_op jit(solution)/shard_map/ppermute | solution.py:107
  478.4 48.6 %collective-permute-start.114 = (f32[256,2048]{1,0:T(8,128)}, f32[256,2048]{1,0:T(8,128)S(1)}, u32[]{:S(2)}, u32[]{:S(2)}) collective-permute-start(f32[256,2048]{1,0:T(8,128)} %fusion.177), channel_id=1, source_target_pairs={{0,96},{4,100},{8,104},{12,108},{16,112},{20,116},{24,120},{28,124... | collective-permute-start | bytes 6291464 | tf_op jit(solution)/shard_map/ppermute | solution.py:123
  501.1 49.8 %collective-permute-start.117 = (f32[256,2048]{1,0:T(8,128)S(1)}, f32[256,2048]{1,0:T(8,128)S(1)}, u32[]{:S(2)}, u32[]{:S(2)}) collective-permute-start(f32[256,2048]{1,0:T(8,128)S(1)} %copy-done.214), channel_id=1, source_target_pairs={{0,32},{4,36},{8,40},{12,44},{16,48},{20,52},{24,56},{28,60},{32,6... | collective-permute-start | bytes 6291464 | tf_op jit(solution)/shard_map/ppermute | solution.py:122
  505.1 134.2 %collective-permute-start.116 = (f32[256,2048]{1,0:T(8,128)S(1)}, f32[256,2048]{1,0:T(8,128)S(1)}, u32[]{:S(2)}, u32[]{:S(2)}) collective-permute-start(f32[256,2048]{1,0:T(8,128)S(1)} %convolution_add_fusion.6), channel_id=1, source_target_pairs={{0,32},{4,36},{8,40},{12,44},{16,48},{20,52},{24,56},{28,60},{32,6... | collective-permute-start | bytes 6291464 | tf_op jit(solution)/shard_map/ppermute | solution.py:122
  511.2 85.2 %collective-permute-start.94 = (f32[32,1024]{1,0:T(8,128)S(1)}, f32[32,1024]{1,0:T(8,128)S(1)}, u32[]{:S(2)}, u32[]{:S(2)}) collective-permute-start(f32[32,1024]{1,0:T(8,128)S(1)} %get-tuple-element.173), channel_id=1, source_target_pairs={{0,32},{4,36},{8,40},{12,44},{16,48},{20,52},{24,56},{28,60},{32,6... | collective-permute-start | bytes 393224 | tf_op jit(solution)/shard_map/ppermute | solution.py:187
  517.6 80.9 %collective-permute-start.95 = (f32[32,1024]{1,0:T(8,128)S(1)}, f32[32,1024]{1,0:T(8,128)S(1)}, u32[]{:S(2)}, u32[]{:S(2)}) collective-permute-start(f32[32,1024]{1,0:T(8,128)S(1)} %get-tuple-element.173), channel_id=1, source_target_pairs={{0,64},{4,68},{8,72},{12,76},{16,80},{20,84},{24,88},{28,92},{32,9... | collective-permute-start | bytes 393224 | tf_op jit(solution)/shard_map/ppermute | solution.py:187
  527.0 71.5 %collective-permute-start.96 = (f32[32,1024]{1,0:T(8,128)S(1)}, f32[32,1024]{1,0:T(8,128)S(1)}, u32[]{:S(2)}, u32[]{:S(2)}) collective-permute-start(f32[32,1024]{1,0:T(8,128)S(1)} %get-tuple-element.173), channel_id=1, source_target_pairs={{0,96},{4,100},{8,104},{12,108},{16,112},{20,116},{24,120},{28,124... | collective-permute-start | bytes 393224 | tf_op jit(solution)/shard_map/ppermute | solution.py:187
  550.8 52.3 %collective-permute-start.76 = (f32[256,512]{1,0:T(8,128)S(1)}, f32[256,512]{1,0:T(8,128)S(1)}, u32[]{:S(2)}, u32[]{:S(2)}) collective-permute-start(f32[256,512]{1,0:T(8,128)S(1)} %fusion.198), channel_id=1, source_target_pairs={{0,8},{4,12},{8,16},{12,20},{16,24},{20,28},{24,0},{28,4},{32,40},... | collective-permute-start | bytes 1572872 | tf_op jit(solution)/shard_map/ppermute | solution.py:122
  610.6 42.9 %collective-permute-start.119 = (f32[256,2048]{1,0:T(8,128)}, f32[256,2048]{1,0:T(8,128)S(1)}, u32[]{:S(2)}, u32[]{:S(2)}) collective-permute-start(f32[256,2048]{1,0:T(8,128)} %convolution_add_fusion.4), channel_id=1, source_target_pairs={{0,96},{4,100},{8,104},{12,108},{16,112},{20,116},{24,120},{28,124... | collective-permute-start | bytes 6291464 | tf_op jit(solution)/shard_map/ppermute | solution.py:123
  612.3 27.1 %collective-permute-start.99 = (f32[128,1024]{1,0:T(8,128)S(1)}, f32[128,1024]{1,0:T(8,128)S(1)}, u32[]{:S(2)}, u32[]{:S(2)}) collective-permute-start(f32[128,1024]{1,0:T(8,128)S(1)} %pad_maximum_fusion.11), channel_id=1, source_target_pairs={{0,24},{4,28},{8,0},{12,4},{16,8},{20,12},{24,16},{28,20},{32,56},... | collective-permute-start | bytes 1572872 | tf_op jit(solution)/shard_map/ppermute | solution.py:187
  618.6 65.7 %collective-permute-start.127 = (f32[256,2048]{1,0:T(8,128)}, f32[256,2048]{1,0:T(8,128)S(1)}, u32[]{:S(2)}, u32[]{:S(2)}) collective-permute-start(f32[256,2048]{1,0:T(8,128)} %fusion.165), channel_id=1, source_target_pairs={{0,24},{4,28},{8,0},{12,4},{16,8},{20,12},{24,16},{28,20},{32,56},... | collective-permute-start | bytes 6291464 | tf_op jit(solution)/shard_map/ppermute | solution.py:123
  629.2 55.1 %collective-permute-start.129 = (f32[256,2048]{1,0:T(8,128)}, f32[256,2048]{1,0:T(8,128)S(1)}, u32[]{:S(2)}, u32[]{:S(2)}) collective-permute-start(f32[256,2048]{1,0:T(8,128)} %convolution_add_fusion.2), channel_id=1, source_target_pairs={{0,8},{4,12},{8,16},{12,20},{16,24},{20,28},{24,0},{28,4},{32,40},... | collective-permute-start | bytes 6291464 | tf_op jit(solution)/shard_map/ppermute | solution.py:122
  639.4 84.8 %collective-permute-start.130 = (f32[256,2048]{1,0:T(8,128)}, f32[256,2048]{1,0:T(8,128)S(1)}, u32[]{:S(2)}, u32[]{:S(2)}) collective-permute-start(f32[256,2048]{1,0:T(8,128)} %fusion.159), channel_id=1, source_target_pairs={{0,8},{4,12},{8,16},{12,20},{16,24},{20,28},{24,0},{28,4},{32,40},... | collective-permute-start | bytes 6291464 | tf_op jit(solution)/shard_map/ppermute | solution.py:122
  639.4 89.8 %collective-permute-start.132 = (f32[256,2048]{1,0:T(8,128)S(1)}, f32[256,2048]{1,0:T(8,128)S(1)}, u32[]{:S(2)}, u32[]{:S(2)}) collective-permute-start(f32[256,2048]{1,0:T(8,128)S(1)} %convolution_add_fusion), channel_id=1, source_target_pairs={{0,24},{4,28},{8,0},{12,4},{16,8},{20,12},{24,16},{28,20},{32,56},... | collective-permute-start | bytes 6291464 | tf_op jit(solution)/shard_map/ppermute | solution.py:123
  653.5 105.6 %collective-permute-start.30 = (f32[128,2048]{1,0:T(8,128)S(1)}, f32[128,2048]{1,0:T(8,128)S(1)}, u32[]{:S(2)}, u32[]{:S(2)}) collective-permute-start(f32[128,2048]{1,0:T(8,128)S(1)} %slice.305), channel_id=1, source_target_pairs={{0,1},{1,0},{2,3},{3,2},{4,5},{5,4},{6,7},{7,6},{8,9},{9,8},{10,11... | collective-permute-start | bytes 3145736 | tf_op jit(solution)/shard_map/ppermute | solution.py:107
  684.3 50.5 %collective-permute-start.75 = (f32[256,512]{1,0:T(8,128)S(1)}, f32[256,512]{1,0:T(8,128)S(1)}, u32[]{:S(2)}, u32[]{:S(2)}) collective-permute-start(f32[256,512]{1,0:T(8,128)S(1)} %fusion.201), channel_id=1, source_target_pairs={{0,24},{4,28},{8,0},{12,4},{16,8},{20,12},{24,16},{28,20},{32,56},... | collective-permute-start | bytes 1572872 | tf_op jit(solution)/shard_map/ppermute | solution.py:123
  684.3 53.5 %collective-permute-start.78 = (f32[256,512]{1,0:T(8,128)S(1)}, f32[256,512]{1,0:T(8,128)S(1)}, u32[]{:S(2)}, u32[]{:S(2)}) collective-permute-start(f32[256,512]{1,0:T(8,128)S(1)} %fusion.195), channel_id=1, source_target_pairs={{0,8},{4,12},{8,16},{12,20},{16,24},{20,28},{24,0},{28,4},{32,40},... | collective-permute-start | bytes 1572872 | tf_op jit(solution)/shard_map/ppermute | solution.py:122
  751.8 47.5 %collective-permute-start.121 = (f32[64,2048]{1,0:T(8,128)S(1)}, f32[64,2048]{1,0:T(8,128)S(1)}, u32[]{:S(2)}, u32[]{:S(2)}) collective-permute-start(f32[64,2048]{1,0:T(8,128)S(1)} %get-tuple-element.100), channel_id=1, source_target_pairs={{0,24},{4,28},{8,0},{12,4},{16,8},{20,12},{24,16},{28,20},{32,56},... | collective-permute-start | bytes 1572872 | tf_op jit(solution)/shard_map/ppermute | solution.py:123
  779.6 19.7 %collective-permute-start.124 = (f32[64,2048]{1,0:T(8,128)S(1)}, f32[64,2048]{1,0:T(8,128)S(1)}, u32[]{:S(2)}, u32[]{:S(2)}) collective-permute-start(f32[64,2048]{1,0:T(8,128)S(1)} %get-tuple-element.99), channel_id=1, source_target_pairs={{0,8},{4,12},{8,16},{12,20},{16,24},{20,28},{24,0},{28,4},{32,40},... | collective-permute-start | bytes 1572872 | tf_op jit(solution)/shard_map/ppermute | solution.py:122
  780.5 21.6 %collective-permute-start.134 = (f32[64,2048]{1,0:T(8,128)S(1)}, f32[64,2048]{1,0:T(8,128)S(1)}, u32[]{:S(2)}, u32[]{:S(2)}) collective-permute-start(f32[64,2048]{1,0:T(8,128)S(1)} %get-tuple-element.94), channel_id=1, source_target_pairs={{0,96},{4,100},{8,104},{12,108},{16,112},{20,116},{24,120},{28,124... | collective-permute-start | bytes 1572872 | tf_op jit(solution)/shard_map/ppermute | solution.py:123
  783.0 19.4 %collective-permute-start.137 = (f32[64,2048]{1,0:T(8,128)S(1)}, f32[64,2048]{1,0:T(8,128)S(1)}, u32[]{:S(2)}, u32[]{:S(2)}) collective-permute-start(f32[64,2048]{1,0:T(8,128)S(1)} %get-tuple-element.93), channel_id=1, source_target_pairs={{0,32},{4,36},{8,40},{12,44},{16,48},{20,52},{24,56},{28,60},{32,6... | collective-permute-start | bytes 1572872 | tf_op jit(solution)/shard_map/ppermute | solution.py:122
  798.6 32.0 %collective-permute-start.31 = (f32[128,2048]{1,0:T(8,128)S(1)}, f32[128,2048]{1,0:T(8,128)S(1)}, u32[]{:S(2)}, u32[]{:S(2)}) collective-permute-start(f32[128,2048]{1,0:T(8,128)S(1)} %slice_add_fusion.1), channel_id=1, source_target_pairs={{0,2},{1,3},{2,0},{3,1},{4,6},{5,7},{6,4},{7,5},{8,10},{9,11},{10,... | collective-permute-start | bytes 3145736 | tf_op jit(solution)/shard_map/ppermute | solution.py:113
  861.4 35.5 %collective-permute-start.53 = (f32[256,768]{1,0:T(8,128)S(1)}, f32[256,768]{1,0:T(8,128)S(1)}, u32[]{:S(2)}, u32[]{:S(2)}) collective-permute-start(f32[256,768]{1,0:T(8,128)S(1)} %fusion.216), channel_id=1, source_target_pairs={{0,24},{4,28},{8,0},{12,4},{16,8},{20,12},{24,16},{28,20},{32,56},... | collective-permute-start | bytes 2359304 | tf_op jit(solution)/shard_map/ppermute | solution.py:123
  864.6 19.3 %collective-permute-start.62 = (f32[256,512]{1,0:T(8,128)S(1)}, f32[256,512]{1,0:T(8,128)S(1)}, u32[]{:S(2)}, u32[]{:S(2)}) collective-permute-start(f32[256,512]{1,0:T(8,128)S(1)} %fusion.213), channel_id=1, source_target_pairs={{0,96},{4,100},{8,104},{12,108},{16,112},{20,116},{24,120},{28,124... | collective-permute-start | bytes 1572872 | tf_op jit(solution)/shard_map/ppermute | solution.py:123
  869.4 21.6 %collective-permute-start.65 = (f32[256,512]{1,0:T(8,128)S(1)}, f32[256,512]{1,0:T(8,128)S(1)}, u32[]{:S(2)}, u32[]{:S(2)}) collective-permute-start(f32[256,512]{1,0:T(8,128)S(1)} %fusion.207), channel_id=1, source_target_pairs={{0,32},{4,36},{8,40},{12,44},{16,48},{20,52},{24,56},{28,60},{32,6... | collective-permute-start | bytes 1572872 | tf_op jit(solution)/shard_map/ppermute | solution.py:122
  875.2 19.2 %collective-permute-start.67 = (f32[256,512]{1,0:T(8,128)S(1)}, f32[256,512]{1,0:T(8,128)S(1)}, u32[]{:S(2)}, u32[]{:S(2)}) collective-permute-start(f32[256,512]{1,0:T(8,128)S(1)} %convolution_add_fusion.28), channel_id=1, source_target_pairs={{0,96},{4,100},{8,104},{12,108},{16,112},{20,116},{24,120},{28,124... | collective-permute-start | bytes 1572872 | tf_op jit(solution)/shard_map/ppermute | solution.py:123
  883.8 38.5 %collective-permute-start.33 = (f32[128,2048]{1,0:T(8,128)S(1)}, f32[128,2048]{1,0:T(8,128)S(1)}, u32[]{:S(2)}, u32[]{:S(2)}) collective-permute-start(f32[128,2048]{1,0:T(8,128)S(1)} %slice.307), channel_id=1, source_target_pairs={{0,1},{1,0},{2,3},{3,2},{4,5},{5,4},{6,7},{7,6},{8,9},{9,8},{10,11... | collective-permute-start | bytes 3145736 | tf_op jit(solution)/shard_map/ppermute | solution.py:107
  891.1 21.3 %collective-permute-start.40 = (f32[256,768]{1,0:T(8,128)S(1)}, f32[256,768]{1,0:T(8,128)S(1)}, u32[]{:S(2)}, u32[]{:S(2)}) collective-permute-start(f32[256,768]{1,0:T(8,128)S(1)} %fusion.228), channel_id=1, source_target_pairs={{0,96},{4,100},{8,104},{12,108},{16,112},{20,116},{24,120},{28,124... | collective-permute-start | bytes 2359304 | tf_op jit(solution)/shard_map/ppermute | solution.py:123
  900.5 28.7 %collective-permute-start.36 = (f32[256,768]{1,0:T(8,128)S(1)}, f32[256,768]{1,0:T(8,128)S(1)}, u32[]{:S(2)}, u32[]{:S(2)}) collective-permute-start(f32[256,768]{1,0:T(8,128)S(1)} %fusion.237), channel_id=1, source_target_pairs={{0,96},{4,100},{8,104},{12,108},{16,112},{20,116},{24,120},{28,124... | collective-permute-start | bytes 2359304 | tf_op jit(solution)/shard_map/ppermute | solution.py:123
  916.0 21.3 %collective-permute-start.39 = (f32[256,768]{1,0:T(8,128)S(1)}, f32[256,768]{1,0:T(8,128)S(1)}, u32[]{:S(2)}, u32[]{:S(2)}) collective-permute-start(f32[256,768]{1,0:T(8,128)S(1)} %fusion.231), channel_id=1, source_target_pairs={{0,32},{4,36},{8,40},{12,44},{16,48},{20,52},{24,56},{28,60},{32,6... | collective-permute-start | bytes 2359304 | tf_op jit(solution)/shard_map/ppermute | solution.py:122
  918.5 27.2 %collective-permute-start.38 = (f32[256,768]{1,0:T(8,128)S(1)}, f32[256,768]{1,0:T(8,128)S(1)}, u32[]{:S(2)}, u32[]{:S(2)}) collective-permute-start(f32[256,768]{1,0:T(8,128)S(1)} %convolution_add_fusion.18), channel_id=1, source_target_pairs={{0,32},{4,36},{8,40},{12,44},{16,48},{20,52},{24,56},{28,60},{32,6... | collective-permute-start | bytes 2359304 | tf_op jit(solution)/shard_map/ppermute | solution.py:122
  919.0 30.2 %collective-permute-start.41 = (f32[256,768]{1,0:T(8,128)S(1)}, f32[256,768]{1,0:T(8,128)S(1)}, u32[]{:S(2)}, u32[]{:S(2)}) collective-permute-start(f32[256,768]{1,0:T(8,128)S(1)} %convolution_add_fusion.16), channel_id=1, source_target_pairs={{0,96},{4,100},{8,104},{12,108},{16,112},{20,116},{24,120},{28,124... | collective-permute-start | bytes 2359304 | tf_op jit(solution)/shard_map/ppermute | solution.py:123
  929.2 20.6 %collective-permute-start.49 = (f32[256,768]{1,0:T(8,128)S(1)}, f32[256,768]{1,0:T(8,128)S(1)}, u32[]{:S(2)}, u32[]{:S(2)}) collective-permute-start(f32[256,768]{1,0:T(8,128)S(1)} %fusion.225), channel_id=1, source_target_pairs={{0,24},{4,28},{8,0},{12,4},{16,8},{20,12},{24,16},{28,20},{32,56},... | collective-permute-start | bytes 2359304 | tf_op jit(solution)/shard_map/ppermute | solution.py:123
  931.2 20.6 %collective-permute-start.51 = (f32[256,768]{1,0:T(8,128)S(1)}, f32[256,768]{1,0:T(8,128)S(1)}, u32[]{:S(2)}, u32[]{:S(2)}) collective-permute-start(f32[256,768]{1,0:T(8,128)S(1)} %convolution_add_fusion.14), channel_id=1, source_target_pairs={{0,8},{4,12},{8,16},{12,20},{16,24},{20,28},{24,0},{28,4},{32,40},... | collective-permute-start | bytes 2359304 | tf_op jit(solution)/shard_map/ppermute | solution.py:122
  937.3 23.7 %collective-permute-start.52 = (f32[256,768]{1,0:T(8,128)S(1)}, f32[256,768]{1,0:T(8,128)S(1)}, u32[]{:S(2)}, u32[]{:S(2)}) collective-permute-start(f32[256,768]{1,0:T(8,128)S(1)} %fusion.219), channel_id=1, source_target_pairs={{0,8},{4,12},{8,16},{12,20},{16,24},{20,28},{24,0},{28,4},{32,40},... | collective-permute-start | bytes 2359304 | tf_op jit(solution)/shard_map/ppermute | solution.py:122
  949.2 37.8 %collective-permute-start.34 = (f32[128,2048]{1,0:T(8,128)S(1)}, f32[128,2048]{1,0:T(8,128)S(1)}, u32[]{:S(2)}, u32[]{:S(2)}) collective-permute-start(f32[128,2048]{1,0:T(8,128)S(1)} %slice_add_fusion), channel_id=1, source_target_pairs={{0,2},{1,3},{2,0},{3,1},{4,6},{5,7},{6,4},{7,5},{8,10},{9,11},{10,... | collective-permute-start | bytes 3145736 | tf_op jit(solution)/shard_map/ppermute | solution.py:113
  989.1 26.2 %collective-permute-start.35 = (f32[128,2048]{1,0:T(8,128)S(1)}, f32[128,2048]{1,0:T(8,128)S(1)}, u32[]{:S(2)}, u32[]{:S(2)}) collective-permute-start(f32[128,2048]{1,0:T(8,128)S(1)} %select_multiply_fusion), channel_id=1, source_target_pairs={{0,1},{1,0},{2,3},{3,2},{4,5},{5,4},{6,7},{7,6},{8,9},{9,8},{10,11... | collective-permute-start | bytes 3145736 | tf_op jit(solution)/shard_map/ppermute | solution.py:107
  (306 other events, 2368.3 us)

commit v2 on v1

v2 whole, which is shorter than its diff:
```python
import functools

import jax
import jax.numpy as jnp
from jax import lax
from jax.experimental import pallas as pl
from jax.experimental.pallas import tpu as pltpu
from jax.sharding import PartitionSpec as P

HEAD = 128
EPS = 1e-05
MESH = pl.DeviceIdType.MESH
F32, BF16 = jnp.float32, jnp.bfloat16
CHUNK = 64
JOB = 512


def product(left, right):
    return jnp.dot(left, right, preferred_element_type=F32)


def outer_sum(left, right):
    return lax.dot_general(left, right, (((0,), (0,)), ((), ())), preferred_element_type=F32)


def back_product(left, right):
    return lax.dot_general(left, right, (((1,), (1,)), ((), ())), preferred_element_type=F32)


def low(value):
    return value.astype(BF16)


def layer_norm(rows, gain):
    mean = jnp.mean(rows, axis=-1, keepdims=True)
    centred = rows - mean
    spread = jnp.mean(centred * centred, axis=-1, keepdims=True)
    return centred * lax.rsqrt(spread + EPS) * gain


def norm_back(rows, gain, grad):
    mean = jnp.mean(rows, axis=-1, keepdims=True)
    centred = rows - mean
    spread = jnp.mean(centred * centred, axis=-1, keepdims=True)
    root = lax.rsqrt(spread + EPS)
    xhat = centred * root
    scaled = grad * gain
    row_grad = root * (
        scaled
        - jnp.mean(scaled, axis=-1, keepdims=True)
        - xhat * jnp.mean(scaled * xhat, axis=-1, keepdims=True)
    )
    return row_grad, grad * xhat


def attend_scores(query, keys, valid):
    scores = jnp.einsum("bqhd,bkhd->bhqk", query, keys, preferred_element_type=F32)
    scores = scores * HEAD ** (-0.5)
    if valid is None:
        return scores
    return jnp.where(valid[:, None, None, :], scores, -1e30)


def attend_forward(query, keys, values, valid):
    scores = attend_scores(query, keys, valid)
    total = jax.nn.logsumexp(scores, axis=-1, keepdims=True)
    weights_low = low(jnp.exp(scores - total))
    mixed = jnp.einsum("bhqk,bkhd->bqhd", weights_low, values, preferred_element_type=F32)
    return low(mixed), total


def attend_backward(query, keys, values, valid, total, upstream):
    scale = HEAD ** (-0.5)
    probs = jnp.exp(attend_scores(query, keys, valid) - total)
    grad_values = jnp.einsum("bhqk,bqhd->bkhd", low(probs), upstream, preferred_element_type=F32)
    grad_probs = jnp.einsum("bqhd,bkhd->bhqk", upstream, values, preferred_element_type=F32)
    inner = jnp.sum(grad_probs * probs, axis=-1, keepdims=True)
    grad_scores = low(probs * (grad_probs - inner))
    grad_query = jnp.einsum("bhqk,bkhd->bqhd", grad_scores, keys, preferred_element_type=F32)
    grad_keys = jnp.einsum("bhqk,bqhd->bkhd", grad_scores, query, preferred_element_type=F32)
    return low(grad_query * scale), low(grad_keys * scale), low(grad_values)


class Net:
    def __init__(self, send, recv, local):
        dp, tensor = lax.axis_index("dp"), lax.axis_index("tensor")
        self.x, self.y, self.z = dp // 8, (dp // 2) % 4, dp % 2
        self.tensor, self.core = tensor, tensor % 2
        self.send, self.recv, self.local = send, recv, local
        self.sent, self.loads = 0, 0

    def device(self, kind, step=1):
        x, y, z, tensor = self.x, self.y, self.z, self.tensor
        if kind == "x":
            x = (x + step + 4) % 4
        elif kind == "y":
            y = (y + step + 4) % 4
        elif kind == "zhi":
            z = 1 - z
        elif kind == "zlo":
            tensor = (tensor + 2) % 4
        else:
            tensor = tensor + 1 - 2 * self.core
        return (x * 8 + y * 2 + z, tensor)

    def greet(self, partners):
        barrier = pltpu.get_barrier_semaphore()
        for kind, step in partners:
            pl.semaphore_signal(
                barrier, inc=1, device_id=self.device(kind, step), device_id_type=MESH
            )
        pl.semaphore_wait(barrier, len(partners))

    def push(self, source, target, kind, step=1):
        copy = pltpu.make_async_remote_copy(
            src_ref=source,
            dst_ref=target,
            send_sem=self.send.at[self.sent],
            recv_sem=self.recv.at[self.sent],
            device_id=self.device(kind, step),
            device_id_type=MESH,
        )
        self.sent += 1
        copy.start()
        return copy

    def load(self, source, target):
        copy = pltpu.make_async_copy(source, target, self.local.at[self.loads])
        self.loads += 1
        copy.start()
        return copy


def add_rows(target, *sources):
    rows = target.shape[0]
    step = 16 if target.shape[1] > 1024 else 32

    def body(i, carry):
        at = pl.ds(pl.multiple_of(i * step, step), step)
        value = target[at, :]
        for source in sources:
            value = value + source[at, :]
        target[at, :] = value
        return carry

    lax.fori_loop(0, rows // step, body, 0)


class Ring:
    SCRATCH = (
        ((6, 2, 128, JOB), F32),
        ((2, 2, 128, JOB), F32),
        ((4, 128, JOB), F32),
        ((6, 64, JOB), F32),
        ((64, JOB), F32),
    )
    COPIES, LOADS = 13, 4

    def __init__(self, net, grad, column, x_first, out, scratch):
        self.net, self.grad, self.out = net, grad, out
        self.columns = pl.ds(column * JOB, JOB)
        self.x_first = x_first
        self.axes = ("x", "y") if x_first else ("y", "x")
        self.one, self.two = (net.x, net.y) if x_first else (net.y, net.x)
        self.got, self.turn, self.own, self.got_two, self.got_three = scratch

    def piece(self, step, half):
        at = (self.one + step) % 4
        pair = pl.ds(2 * half, 2)
        if self.x_first:
            return self.grad.at[at, pair, :, self.columns]
        return self.grad.at[pair, at, :, self.columns]

    def begin(self):
        net, axis = self.net, self.axes[0]
        self.far = [
            net.push(self.piece(2, 0), self.got.at[0], axis, 1),
            net.push(self.piece(2, 1), self.got.at[1], axis, -1),
        ]
        self.loading = [
            net.load(self.piece(1, 0), self.turn.at[0]),
            net.load(self.piece(3, 1), self.turn.at[1]),
            net.load(self.piece(0, 0), self.own.at[pl.ds(0, 2)]),
            net.load(self.piece(0, 1), self.own.at[pl.ds(2, 2)]),
        ]

    def relay(self):
        net, axis = self.net, self.axes[0]
        self.last = []
        for i, step in enumerate((1, -1)):
            self.loading[i].wait()
            self.far[i].wait_recv()
            for j in range(2):
                add_rows(self.turn.at[i, j], self.got.at[i, j])
            self.last.append(net.push(self.turn.at[i], self.got.at[2 + i], axis, step))
        self.near = [
            net.push(self.piece(1, 1), self.got.at[4], axis, 1),
            net.push(self.piece(3, 0), self.got.at[5], axis, -1),
        ]

    def second(self):
        net, axis, own = self.net, self.axes[1], self.own
        for copy in self.loading[2:]:
            copy.wait()
        for copy in self.last + self.near:
            copy.wait_recv()
        for j in range(2):
            add_rows(own.at[j], self.got.at[5, j], self.got.at[2, j])
            add_rows(own.at[2 + j], self.got.at[4, j], self.got.at[3, j])
        self.part = lambda k, h: own.at[(self.two + k) % 4, pl.ds(h * 64, 64), :]
        got = self.got_two
        self.far_two = [
            net.push(self.part(2, 0), got.at[0], axis, 1),
            net.push(self.part(2, 1), got.at[1], axis, -1),
        ]
        self.near_two = [
            net.push(self.part(1, 1), got.at[4], axis, 1),
            net.push(self.part(3, 0), got.at[5], axis, -1),
        ]

    def relay_two(self):
        net, axis = self.net, self.axes[1]
        self.last_two = []
        for i, (step, at) in enumerate(((1, (1, 0)), (-1, (3, 1)))):
            self.far_two[i].wait_recv()
            add_rows(self.part(*at), self.got_two.at[i])
            self.last_two.append(net.push(self.part(*at), self.got_two.at[2 + i], axis, step))

    def third(self):
        net, got = self.net, self.got_two
        for copy in self.near_two + self.last_two:
            copy.wait_recv()
        add_rows(self.part(0, 0), got.at[5], got.at[2])
        add_rows(self.part(0, 1), got.at[4], got.at[3])
        whole = self.own.at[self.two]
        self.other = whole.at[pl.ds(pl.multiple_of((1 - net.z) * 64, 64), 64)]
        self.mine = whole.at[pl.ds(pl.multiple_of(net.z * 64, 64), 64)]
        self.final = net.push(self.other, self.got_three, "zhi")

    def finish(self):
        self.final.wait_recv()
        self.out[...] = self.mine[...] + self.got_three[...]
        for copy in self.far + self.last + self.near:
            copy.wait_send()
        for copy in self.far_two + self.last_two + self.near_two + [self.final]:
            copy.wait_send()


class TensorSum:
    SCRATCH = tuple(((256 // CHUNK, CHUNK, 2048), F32) for _ in range(4))
    COPIES, LOADS = 3 * (256 // CHUNK), 256 // CHUNK

    def __init__(self, net, share, epilogue, whole, scratch):
        self.net, self.share, self.epilogue, self.whole = net, share, epilogue, whole
        self.mine, self.got_core, self.got_z, self.got_rows = scratch
        self.steps = range(256 // CHUNK)

    def rows(self, core, step):
        return pl.ds(pl.multiple_of(core * 256 + step * CHUNK, CHUNK), CHUNK)

    def begin(self):
        net = self.net
        self.swaps = [
            net.push(self.share.at[self.rows(1 - net.core, j)], self.got_core.at[j], "core")
            for j in self.steps
        ]
        self.loading = [
            net.load(self.share.at[self.rows(net.core, j)], self.mine.at[j]) for j in self.steps
        ]

    def exchange(self):
        self.over = []
        for j in self.steps:
            self.loading[j].wait()
            self.swaps[j].wait_recv()
            add_rows(self.mine.at[j], self.got_core.at[j])
            self.over.append(self.net.push(self.mine.at[j], self.got_z.at[j], "zlo"))

    def work(self):
        net = self.net
        self.spread = []
        for j in self.steps:
            self.over[j].wait_recv()

            def body(i, carry, j=j):
                at = pl.ds(pl.multiple_of(i * 8, 8), 8)
                rows = pl.ds(pl.multiple_of(j * CHUNK + i * 8, 8), 8)
                self.got_core[j, at, :] = self.epilogue(
                    rows, self.mine[j, at, :] + self.got_z[j, at, :]
                )
                return carry

            lax.fori_loop(0, CHUNK // 8, body, 0)
            self.spread.append(net.push(self.got_core.at[j], self.got_rows.at[j], "core"))
            self.round(self.got_core, j, net.core)

    def round(self, source, step, core):
        def body(i, carry):
            at = pl.ds(pl.multiple_of(i * 16, 16), 16)
            rows = pl.ds(pl.multiple_of(core * 256 + step * CHUNK + i * 16, 16), 16)
            self.whole[rows, :] = source[step, at, :].astype(BF16)
            return carry

        lax.fori_loop(0, CHUNK // 16, body, 0)

    def finish(self):
        for j in self.steps:
            self.spread[j].wait_recv()
            self.round(self.got_rows, j, 1 - self.net.core)
        for copy in self.swaps + self.over + self.spread:
            copy.wait_send()


NEAR = [("core", 1), ("zlo", 1)]
RING = [("x", 1), ("x", -1), ("y", 1), ("y", -1)]
ALL = [("x", 1), ("x", 2), ("x", 3), ("y", 1), ("y", 2), ("y", 3)]


def vmem(shapes):
    return [pltpu.VMEM(shape, kind) for shape, kind in shapes]


def call(body, ins, outs, scratch, copies, loads, number, name):
    spec = lambda inside: pl.BlockSpec(memory_space=pltpu.VMEM if inside else pl.ANY)
    return pl.pallas_call(
        body,
        name=name,
        out_shape=outs,
        in_specs=[spec(inside) for _, inside in ins],
        out_specs=[spec(True) for _ in outs],
        scratch_shapes=vmem(scratch)
        + [
            pltpu.SemaphoreType.DMA((copies,)),
            pltpu.SemaphoreType.DMA((copies,)),
            pltpu.SemaphoreType.DMA((max(loads, 1),)),
        ],
        compiler_params=pltpu.CompilerParams(
            collective_id=number, has_side_effects=True, vmem_limit_bytes=60 * 2**20
        ),
    )(*[array for array, _ in ins])


def shape(*dims, kind=F32):
    return jax.ShapeDtypeStruct(dims, kind)


def sum_and_norm(share, rows, gain, text_blocks, number):
    with_text = text_blocks is not None
    scratch = list(TensorSum.SCRATCH)
    ins = [(share, False), (rows, True), (gain, True)]
    outs = [shape(256, 2048), shape(512, 2048, kind=BF16)]
    copies, loads = TensorSum.COPIES, TensorSum.LOADS
    if with_text:
        ins.append((text_blocks, False))
        outs.append(shape(4, 4, 32, 256))
        scratch.append(((4, 32, 1024), F32))
        copies, loads = copies + 6, loads + 2

    def body(*refs):
        refs = list(refs)
        share_ref, rows_ref, gain_ref = refs[:3]
        text_ref = refs[3] if with_text else None
        outs_at = len(ins)
        total_ref, normed_ref = refs[outs_at : outs_at + 2]
        columns_ref = refs[outs_at + 2] if with_text else None
        scratch_at = outs_at + len(outs)
        net = Net(*refs[-3:])
        net.greet(NEAR + (ALL if with_text else []))

        def epilogue(at, total):
            total = rows_ref[at, :] + total
            total_ref[at, :] = total
            return layer_norm(total, gain_ref[...])

        work = TensorSum(net, share_ref, epilogue, normed_ref, refs[scratch_at : scratch_at + 4])
        work.begin()
        if with_text:
            got = refs[scratch_at + 4]
            own = net.load(text_ref.at[net.x], got.at[0])
            first = [
                net.push(text_ref.at[(net.x + k) % 4], got.at[k], "x", k) for k in (1, 2, 3)
            ]
        work.exchange()
        if with_text:
            own.wait()
            for copy in first:
                copy.wait_recv()
            cut = lambda y: pl.ds(pl.multiple_of(y * 256, 256), 256)
            kept = net.load(got.at[:, :, cut(net.y)], columns_ref.at[0])
            second = [
                net.push(got.at[:, :, cut((net.y + k) % 4)], columns_ref.at[k], "y", k)
                for k in (1, 2, 3)
            ]
        work.work()
        work.finish()
        if with_text:
            kept.wait()
            for copy in second:
                copy.wait_recv()
            for copy in first + second:
                copy.wait_send()

    return call(body, ins, outs, scratch, copies, loads, number, f"forward_sum_{number}")


def run_rings(rings, between):
    begin, first, second, third = between
    for ring in rings:
        ring.begin()
    begin()
    for ring in rings:
        ring.relay()
    first()
    for ring in rings:
        ring.second()
    second()
    for ring in rings:
        ring.relay_two()
    for ring in rings:
        ring.third()
    third()
    for ring in rings:
        ring.finish()


def ring_scratch(count):
    return [(s, k) for _ in range(count) for s, k in Ring.SCRATCH]


def take(refs, counts):
    out, at = [], 0
    for count in counts:
        out.append(refs[at : at + count])
        at += count
    return out


def backward_wide(share, x_rows, gain, extra, grad, number, more):
    grad = grad.reshape(4, 4, 128, 2048)
    ins = [(share, False), (x_rows, True), (gain, True), (extra, True), (grad, False)]
    outs = [shape(256, 2048), shape(512, 2048, kind=BF16), shape(8, 2048)]
    outs += [shape(64, JOB)] * 4
    scratch = ring_scratch(4) + list(TensorSum.SCRATCH)
    copies = 4 * Ring.COPIES + TensorSum.COPIES
    loads = 4 * Ring.LOADS + TensorSum.LOADS
    kind = more[0]
    if kind == "out":
        ins += [(more[1], False), (more[2], True)]
        outs.append(shape(512, 2048, kind=BF16))
        scratch += list(TensorSum.SCRATCH)
        copies, loads = copies + TensorSum.COPIES, loads + TensorSum.LOADS
        partners = NEAR + RING + [("zhi", 1)]
    else:
        ins += [(more[1], False)]
        outs.append(shape(4, 4, 32, 1024))
        copies, loads = copies + 6, loads + 1
        partners = NEAR + ALL + [("zhi", 1)]
    n_rings = len(ring_scratch(4))

    def body(*refs):
        refs = list(refs)
        n_in, n_out = len(ins), len(outs)
        in_refs, out_refs = refs[:n_in], refs[n_in : n_in + n_out]
        work_refs = refs[n_in + n_out : -3]
        net = Net(*refs[-3:])
        net.greet(partners)
        share_ref, x_ref, gain_ref, extra_ref, grad_ref = in_refs[:5]
        rows_ref, low_ref, gain_sum = out_refs[:3]
        gain_sum[...] = jnp.zeros_like(gain_sum)

        def epilogue(at, total):
            row_grad, terms = norm_back(x_ref[at, :], gain_ref[...], total)
            gain_sum[...] += terms
            result = extra_ref[at, :] + row_grad
            rows_ref[at, :] = result
            return result

        work = TensorSum(net, share_ref, epilogue, low_ref, work_refs[n_rings : n_rings + 4])
        sets = take(work_refs, [len(Ring.SCRATCH)] * 4)
        rings = [
            Ring(net, grad_ref, i, i % 2 == 0, out_refs[3 + i], sets[i]) for i in range(4)
        ]
        if kind == "out":
            more_ref, added_ref = in_refs[5:7]
            other = TensorSum(
                net,
                more_ref,
                lambda at, total: added_ref[at, :] + total,
                out_refs[-1],
                work_refs[n_rings + 4 : n_rings + 8],
            )

            def begin():
                work.exchange()
                other.begin()

            def first():
                work.work()
                other.exchange()
                work.finish()

            def second():
                pass

            def third():
                other.work()
                other.finish()

            work.begin()
            run_rings(rings, (begin, first, second, third))
            return
        small_ref, all_ref = in_refs[5], out_refs[-1]
        state = {}

        def begin():
            work.exchange()

        def first():
            state["own"].wait()
            for copy in state["x"]:
                copy.wait_recv()
            state["y"] = [net.push(all_ref.at[0], all_ref.at[k], "y", k) for k in (1, 2, 3)]
            work.work()

        def second():
            work.finish()

        def third():
            for copy in state["y"]:
                copy.wait_recv()
            for copy in state["x"] + state["y"]:
                copy.wait_send()

        work.begin()
        state["own"] = net.load(small_ref, all_ref.at[0, 0])
        state["x"] = [net.push(small_ref, all_ref.at[0, k], "x", k) for k in (1, 2, 3)]
        run_rings(rings, (begin, first, second, third))

    name = f"backward_sum_{number}"
    return call(body, ins, outs, scratch, copies, loads, number, name)


def backward_last(share, x_rows, gain, extra, keep, grads, text_grad, sums, number):
    grads = [grad.reshape(4, 4, 128, -1) for grad in grads]
    jobs = [(i, c) for i, grad in enumerate(grads) for c in range(grad.shape[3] // JOB)]
    count = len(jobs)
    ins = [(share, False), (x_rows, True), (gain, True), (extra, True), (keep, True)]
    ins += [(text_grad, True), (sums, True)]
    ins += [(grad, False) for grad in grads]
    outs = [shape(512, 2048, kind=BF16), shape(8, 2048), shape(128, 1024)]
    outs += [shape(64, JOB)] * count
    scratch = ring_scratch(count) + list(TensorSum.SCRATCH)
    n_rings = len(ring_scratch(count))
    scratch += [((16, 2048), F32), ((128, 1024), F32), ((9, 8, 2048), F32)]
    copies = count * Ring.COPIES + TensorSum.COPIES + 9
    loads = count * Ring.LOADS + TensorSum.LOADS
    partners = NEAR + ALL + [("zhi", 1)]

    def body(*refs):
        refs = list(refs)
        n_in, n_out = len(ins), len(outs)
        in_refs, out_refs = refs[:n_in], refs[n_in : n_in + n_out]
        work_refs = refs[n_in + n_out : -3]
        net = Net(*refs[-3:])
        net.greet(partners)
        share_ref, x_ref, gain_ref, extra_ref, keep_ref, text_ref, sums_ref = in_refs[:7]
        image_ref, small_ref, text_out = out_refs[:3]
        acc_ref, got_text, got_small = work_refs[n_rings + 4 :]
        acc_ref[...] = jnp.zeros_like(acc_ref)

        def epilogue(at, total):
            row_grad, terms = norm_back(x_ref[at, :], gain_ref[...], total)
            result = extra_ref[at, :] + row_grad
            kept = keep_ref[at, :] > 0.5
            acc_ref[0:8, :] += terms
            acc_ref[8:16, :] += jnp.where(kept, 0.0, result)
            return jnp.where(kept, result, 0.0)

        work = TensorSum(net, share_ref, epilogue, image_ref, work_refs[n_rings : n_rings + 4])
        sets = take(work_refs, [len(Ring.SCRATCH)] * count)
        rings = [
            Ring(net, in_refs[7 + g], c, i % 2 == 0, out_refs[3 + i], sets[i])
            for i, (g, c) in enumerate(jobs)
        ]
        state = {}

        def begin():
            work.exchange()

        def first():
            work.work()

        def second():
            small_ref[...] = sums_ref[...]
            small_ref[0:1, :] = jnp.sum(acc_ref[0:8, :], axis=0, keepdims=True)
            small_ref[3:4, :] = jnp.sum(acc_ref[8:16, :], axis=0, keepdims=True)
            got_small[0] = small_ref[...]
            state["core"] = net.push(got_small.at[0], got_small.at[1], "core")
            state["text"] = net.push(
                text_ref.at[pl.ds(pl.multiple_of((1 - net.z) * 128, 128), 128)], got_text, "zhi"
            )
            work.finish()
            state["core"].wait()
            got_small[0] += got_small[1]
            state["x"] = [net.push(got_small.at[0], got_small.at[1 + k], "x", k) for k in (1, 2, 3)]

        def third():
            for copy in state["x"]:
                copy.wait()
            got_small[0] += got_small[2] + got_small[3] + got_small[4]
            state["y"] = [net.push(got_small.at[0], got_small.at[4 + k], "y", k) for k in (1, 2, 3)]
            for copy in state["y"]:
                copy.wait()
            got_small[0] += got_small[5] + got_small[6] + got_small[7]
            final = net.push(got_small.at[0], got_small.at[8], "zhi")
            final.wait()
            small_ref[...] = got_small[0] + got_small[8]
            state["text"].wait()
            mine = text_ref[pl.ds(pl.multiple_of(net.z * 128, 128), 128), :]
            text_out[...] = mine + got_text[...]

        work.begin()
        run_rings(rings, (begin, first, second, third))

    return call(body, ins, outs, scratch, copies, loads, number, "backward_last")


def shards(
    image,
    text,
    masked,
    text_len,
    cotangent,
    self_query,
    self_key,
    self_value,
    self_output,
    text_query,
    text_key,
    text_value,
    text_output,
    expand,
    contract,
    first_gain,
    second_gain,
    third_gain,
    mask_token,
):
    items, length, width = image.shape
    words = text.shape[1]
    count = items * length
    core = lax.axis_index("tensor") % 2
    heads = self_query.shape[1] // HEAD
    split = lambda rows: rows.reshape(items, -1, heads, HEAD)
    flat = lambda value: value.reshape(-1, heads * HEAD)
    gains = [g.reshape(1, width) for g in (first_gain, second_gain, third_gain)]
    own = lambda rows: lax.dynamic_slice_in_dim(rows, core * length, length, axis=0)

    text_rows = text.reshape(items * words, text.shape[2])
    cross_keys = split(low(product(text_rows, text_key)))
    cross_values = split(low(product(text_rows, text_value)))
    text_blocks = text_rows.astype(F32).reshape(items * words, 4, -1).transpose(1, 0, 2)

    hidden = masked.reshape(count, 1) == 1
    start = jnp.where(hidden, mask_token[None, :], image.reshape(count, width).astype(F32))
    normed_one = low(layer_norm(start, first_gain))
    query = split(low(product(normed_one, self_query)))
    keys = split(low(product(normed_one, self_key)))
    values = split(low(product(normed_one, self_value)))
    self_mixed, self_total = attend_forward(query, keys, values, None)
    self_rows = flat(self_mixed)
    start_own = own(start)
    first, normed_two, text_columns = sum_and_norm(
        product(self_rows, self_output), start_own, gains[1], text_blocks, 0
    )
    text_columns = low(text_columns.reshape(-1, text_columns.shape[-1]))

    cross_query = split(low(product(normed_two, text_query)))
    present = jnp.arange(words)[None, :] < text_len[:, None]
    cross_mixed, cross_total = attend_forward(cross_query, cross_keys, cross_values, present)
    cross_rows = flat(cross_mixed)
    second, normed_three = sum_and_norm(
        product(cross_rows, text_output), first, gains[2], None, 1
    )

    upstream = cotangent.reshape(count, width)
    raised = product(normed_three, expand)
    gelu, pull = jax.vjp(jax.nn.gelu, raised)
    active = low(gelu)
    grad_raised = low(pull(back_product(upstream, contract))[0])
    grad_second, cross_out_grad, third_sum, *contract_t, layer_out = backward_wide(
        back_product(grad_raised, expand),
        second,
        gains[2],
        own(upstream).astype(F32),
        outer_sum(upstream, active),
        2,
        ("out", product(active, contract), second),
    )

    grad_mixed = split(low(back_product(cross_out_grad, text_output)))
    grad_q, grad_k, grad_v = attend_backward(
        cross_query, cross_keys, cross_values, present, cross_total, grad_mixed
    )
    grad_cq = flat(grad_q)
    text_kv = jnp.concatenate([flat(grad_k), flat(grad_v)], axis=1).astype(F32)
    grad_first, self_out_grad, second_sum, *expand_grad, gathered = backward_wide(
        back_product(grad_cq, text_query),
        first,
        gains[1],
        grad_second,
        outer_sum(normed_three, grad_raised),
        3,
        ("text", text_kv),
    )
    gathered = low(gathered.reshape(-1, gathered.shape[-1]))
    text_grads = outer_sum(text_columns, gathered)

    grad_mixed = split(low(back_product(self_out_grad, self_output)))
    grad_q, grad_k, grad_v = map(
        flat, attend_backward(query, keys, values, None, self_total, grad_mixed)
    )
    shares = (
        back_product(grad_q, self_query)
        + back_product(grad_k, self_key)
        + back_product(grad_v, self_value)
    )
    sums = jnp.zeros((8, width), F32)
    sums = sums.at[1].set(jnp.sum(second_sum, axis=0)).at[2].set(jnp.sum(third_sum, axis=0))
    grads = [
        outer_sum(cross_out_grad, cross_rows),
        outer_sum(normed_two, grad_cq),
        outer_sum(self_out_grad, self_rows),
        outer_sum(normed_one, grad_q),
        outer_sum(normed_one, grad_k),
        outer_sum(normed_one, grad_v),
    ]
    keep = 1.0 - own(masked.reshape(count, 1)).astype(F32)
    image_grad, small, text_grads, to, tq, so, sq, sk, sv = backward_last(
        shares, start_own, gains[0], grad_first, keep, grads, text_grads, sums, 4
    )

    share = width // 32
    small = lax.dynamic_slice_in_dim(small, lax.axis_index("dp") * share, share, axis=1)
    cut = text_grads.shape[1] // 2
    joined = lambda parts: jnp.concatenate(parts, axis=1)
    return (
        layer_out.reshape(image.shape),
        image_grad.reshape(image.shape),
        sq,
        sk,
        sv,
        so.T,
        tq,
        text_grads[:, :cut],
        text_grads[:, cut:],
        to.T,
        joined(expand_grad),
        joined(contract_t).T,
        small[0],
        small[1],
        small[2],
        small[3],
    )


def solution(mesh):
    rows, split = P("dp", None, None), P(None, "tensor")
    turned, grads, grads_t = P("tensor", None), P("dp", "tensor"), P("tensor", "dp")
    ins = (rows, rows, P("dp", None), P("dp"), rows, split, split, split, turned)
    ins += (split, split, split, turned, split, turned, P(), P(), P(), P())
    outs = (rows, rows, grads, grads, grads, grads_t, grads, grads, grads, grads_t)
    outs += (grads, grads_t, P("dp"), P("dp"), P("dp"), P("dp"))
    return jax.shard_map(shards, mesh=mesh, in_specs=ins, out_specs=outs, check_vma=False)
```

time: 1030 us -> 739 us (0.72)
  Pallas kernels: 0 us -> 515 us
  waiting for transfers between devices: 502 us -> 0 us
  starting transfers between devices: 175 us -> 0 us
  local copies, waits for them, and re-layouts: 133 us -> 56.9 us
  other arithmetic: 81.1 us -> 14.4 us
  matrix products: 121 us -> 143 us
    pallas_call x0 -> x5, Pallas kernels: none -> 515 us  [call(): pl.pallas_call(body, name=name, out_shape=outs, in_specs=[spec(inside) fo...]
    ppermute x148 -> x0, waiting for transfers between devices: 502 us -> none  [the longest x42 147 us: ring_sum(): right = lambda v: lax.ppermute(v, 'dp', along(1))]
    ppermute x148 -> x0, starting transfers between devices: 175 us -> none  [the longest x42 87.2 us: ring_sum(): left = lambda v: lax.ppermute(v, 'dp', along(-1))]
    select_n x20 -> x0, local copies, waits for them, and re-layouts: 39.3 us -> none  [the longest x10 19.7 us: mine_first(): jnp.where(odd, first, second)]
    unnamed x474 -> x112, local copies, waits for them, and re-layouts: 43.4 us -> 14.4 us
    concatenate x17 -> x0, local copies, waits for them, and re-layouts: 24 us -> none  [the longest x8 17.8 us: whole(): return jnp.concatenate([mine, other], axis=0)]
    dot_general x0 -> x4, local copies, waits for them, and re-layouts: none -> 14 us  [outer_sum(): lax.dot_general(left, right, (((0,), (0,)), ((), ())), preferred_element_...]
    add x25 -> x0, other arithmetic: 13.7 us -> none  [the longest x12 11.8 us: half_sum(): mine = part[:half] + core_swap(part[half:])]
  transfers between devices with their start and end apart: 148 -> 0, of which waited for: 68 -> 0; matrix products, arithmetic and copies ran while one was open for 27% -> 0% of each run, Pallas kernels for 0% -> 0%
where the time goes in v2:
time: 739 us; the launch traced here: 731 us
  Pallas kernels  515 us (70%)
  matrix products  143 us (19%)
  local copies, waits for them, and re-layouts  56.9 us (8%)
  other arithmetic  14.4 us (2%)
    pallas_call x5, Pallas kernels, call(): pl.pallas_call(body, name=name, out_shape=outs, in_specs=[spec(inside) fo...  515 us
    dot_general x10, matrix products, product(): return jnp.dot(left, right, preferred_element_type=F32)  46.6 us
    dot_general x9, matrix products, outer_sum(): lax.dot_general(left, right, (((0,), (0,)), ((), ())), preferred_element_...  46.1 us
    dot_general x8, matrix products, back_product(): lax.dot_general(left, right, (((1,), (1,)), ((), ())), preferred_element_...  39.7 us

profile of v2, /device:TPU:0, one launch (start us, length us, event | category | flops | bytes accessed | tf_op | source)
XLA Modules:
  0.0 731.0 jit_solution(14470879829699281846)
XLA Ops:
  1.5 2.3 select_reduce_fusion
  4.8 2.5 bitcast_select_fusion
  7.3 1.5 constant_dynamic-slice_fusion.1.refs_1_
  10.4 1.3 convolution_convert_fusion.3
  12.1 3.7 convolution_convert_fusion.4
  16.7 1.3 copy.86
  18.5 1.3 copy-done.2
  21.2 1.2 convolution_convert_fusion.5
  22.5 2.9 fusion.12
  25.4 1.3 copy.67
  26.8 5.0 fusion.36.refs_0_
  32.3 1.1 copy.183
  33.4 60.3 %forward_sum_0.1 = (f32[256,2048]{1,0:T(8,128)}, bf16[512,2048]{1,0:T(8,128)(2,1)}, f32[4,4,32,256]{3,2,1,0:T(8,128)}) custom-call(f32[512,2048]{1,0:T(8,128)} %fusion.36.refs_0_, f32[256,2048]{1,0:T(8,128)} %constant_dynamic-slice_fusion.1.refs_1_, f32[1,2048]{1,0:T(1,128)} %bitcast.207, f32[4,32,1024]{2,1,0:T(8,128)} %bitcast.196), custom_call_target="tpu_custom_call" | custom-call | tf_op jit(solution)/shard_map/forward_sum_0/pallas_call | solution.py:325
  93.6 4.3 convolution_convert_fusion.2
  97.9 1.2 reshape.304
  99.1 3.2 convolution_convert_fusion.10
  103.0 1.0 fusion.75
  104.1 3.0 convolution_convert_fusion.11
  107.1 1.1 fusion.11
  108.3 1.3 copy.72
  109.6 3.2 fusion.33.refs_0_
  112.9 57.0 %forward_sum_1.1 = (f32[256,2048]{1,0:T(8,128)}, bf16[512,2048]{1,0:T(8,128)(2,1)}) custom-call(f32[512,2048]{1,0:T(8,128)} %fusion.33.refs_0_, f32[256,2048]{1,0:T(8,128)} %get-tuple-element.71.refs_1_, f32[1,2048]{1,0:T(1,128)} %bitcast.205), custom_call_target="tpu_custom_call" | custom-call | tf_op jit(solution)/shard_map/forward_sum_1/pallas_call | solution.py:325
  169.9 10.7 %fusion.76 = f32[512,2048]{1,0:T(8,128)} fusion(bf16[512,2048]{1,0:T(8,128)(2,1)} %bitcast.198, bf16[2048,2048]{1,0:T(8,128)(2,1)} %param.37), kind=kOutput, calls=%fused_computation.129 | convolution fusion | flops 4294967296 | bytes 14680064 | tf_op jit(solution)/shard_map/dot_general | solution.py:27
  180.6 12.5 %fusion.6 = (bf16[512,2048]{1,0:T(8,128)(2,1)}, f32[512,2048]{1,0:T(8,128)S(1)}) fusion(f32[512,2048]{1,0:T(8,128)} %fusion.76, bf16[512,2048]{1,0:T(8,128)(2,1)S(1)} %copy-done.42, bf16[2048,2048]{1,0:T(8,128)(2,1)} %param.36), kind=kOutput, calls=%fused_computation.8 | convolution fusion | flops 4315938816 | bytes 20971520 | tf_op jit(solution)/shard_map/dot_general | solution.py:19
  193.1 8.6 %fusion.73 = f32[2048,2048]{0,1:T(8,128)} fusion(bf16[512,2048]{1,0:T(8,128)(2,1)S(1)} %bitcast.199, f32[512,2048]{1,0:T(8,128)S(1)} %get-tuple-element.115), kind=kOutput, calls=%fused_computation.126 | convolution fusion | flops 4304404480 | bytes 23068672 | tf_op jit(solution)/shard_map/dot_general | solution.py:23
  201.8 9.2 %fusion.72.refs_5_ = f32[512,2048]{1,0:T(8,128)} fusion(bf16[2048,2048]{1,0:T(8,128)(2,1)S(1)} %bitcast.217, f32[512,2048]{1,0:T(8,128)} %copy-done.45), kind=kOutput, calls=%fused_computation.125 | convolution fusion | flops 4304404480 | bytes 16777216 | tf_op jit(solution)/shard_map/dot_general | solution.py:19
  211.0 8.0 %fusion.77.refs_0_ = f32[512,2048]{1,0:T(8,128)} fusion(bf16[512,2048]{1,0:T(8,128)(2,1)} %get-tuple-element.114, bf16[2048,2048]{1,0:T(8,128)(2,1)S(1)} %bitcast.219), kind=kOutput, calls=%fused_computation.130 | convolution fusion | flops 4294967296 | bytes 14680064 | tf_op jit(solution)/shard_map/dot_general | solution.py:27
  218.9 1.6 dynamic-slice_convert_fusion.refs_3_
  220.5 121.4 %backward_sum_2.1 = (f32[256,2048]{1,0:T(8,128)}, bf16[512,2048]{1,0:T(8,128)(2,1)}, f32[8,2048]{1,0:T(8,128)}, f32[64,512]{1,0:T(8,128)}, f32[64,512]{1,0:T(8,1...) custom-call(f32[512,2048]{1,0:T(8,128)} %fusion.77.refs_0_, ...), custom_call_target="tpu_custom_call" | custom-call | tf_op jit(solution)/shard_map/backward_sum_2/pallas_call | solution.py:325
  342.0 1.9 maximum_bitcast_fusion
  343.9 2.9 convolution_convert_fusion.1
  349.0 10.1 %fusion.78 = f32[2048,2048]{1,0:T(8,128)} fusion(bf16[512,2048]{1,0:T(8,128)(2,1)S(1)} %copy-done.43, bf16[512,2048]{1,0:T(8,128)(2,1)} %get-tuple-element.114), kind=kOutput, calls=%fused_computation.131 | convolution fusion | flops 4294967296 | bytes 20971520 | tf_op jit(solution)/shard_map/dot_general | solution.py:23
  359.7 5.1 fusion.30.refs_0_
  364.8 126.6 %backward_sum_3.1 = (f32[256,2048]{1,0:T(8,128)}, bf16[512,2048]{1,0:T(8,128)(2,1)}, f32[8,2048]{1,0:T(8,128)}, f32[64,512]{1,0:T(8,128)}, f32[64,512]{1,0:T(8,1...) custom-call(f32[512,2048]{1,0:T(8,128)} %fusion.30.refs_0_, ...), custom_call_target="tpu_custom_call" | custom-call | tf_op jit(solution)/shard_map/backward_sum_3/pallas_call | solution.py:325
  491.4 1.9 pad_maximum_fusion
  493.3 3.6 convolution_convert_fusion
  497.9 1.3 copy.89
  499.1 1.3 fusion.13
  500.5 2.1 copy.91
  502.5 2.1 reshape.331
  504.6 3.9 copy.113
  508.5 4.9 fusion.39.refs_12_
  513.4 4.1 copy.112
  517.5 2.1 reshape.328
  519.6 4.9 fusion.45.refs_9_
  526.2 1.3 fusion.14
  527.4 2.1 copy.88
  529.6 2.0 reshape.330
  531.6 4.3 fusion.41.refs_11_
  536.3 3.3 convolution_bitcast_fusion.refs_5_
  539.6 3.2 fusion.24
  542.9 1.1 fusion.15
  544.0 1.3 copy.85
  545.3 3.0 fusion.27
  549.0 3.2 add_add_fusion.refs_0_
  552.4 3.2 fusion.43.refs_10_
  555.8 3.1 copy.111
  558.9 3.3 fusion.47.refs_8_
  562.2 2.9 copy.110
  565.4 3.3 fusion.49.refs_7_
  569.5 149.5 %backward_last.1 = (bf16[512,2048]{1,0:T(8,128)(2,1)}, f32[8,2048]{1,0:T(8,128)}, f32[128,1024]{1,0:T(8,128)}, f32[64,512]{1,0:T(8,128)}, f32[64,512]{1,0:T(8,12...) custom-call(f32[512,2048]{1,0:T(8,128)} %add_add_fusion.refs_0_, ...), custom_call_target="tpu_custom_call" | custom-call | tf_op jit(solution)/shard_map/backward_last/pallas_call | solution.py:325
  719.0 1.9 fusion.74
  722.1 3.3 copy.193
  725.5 1.3 copy.194
  (155 shorter events, 20.7 us)
Async XLA Ops:
  0.6 109.0 %copy-start = (bf16[512,2048]{1,0:T(8,128)(2,1)S(1)}, bf16[512,2048]{1,0:T(8,128)(2,1)}, u32[]{:S(2)}) copy-start(bf16[512,2048]{1,0:T(8,128)(2,1)} %param.35) | copy-start | bytes 6291460
  0.7 3.2 copy-start.37
  0.7 3.2 copy-start.6
  1.5 3.2 copy-start.40
  7.3 2.1 copy-start.7
  7.3 3.1 copy-start.24
  12.1 5.9 copy-start.12
  18.0 2.2 copy-start.14
  18.0 2.5 copy-start.8
  18.0 3.2 copy-start.26
  18.5 1.3 copy-start.2
  26.8 5.1 copy-start.18
  26.8 5.0 copy-start.20
  99.1 3.9 copy-start.22
  99.1 3.9 copy-start.44
  109.6 3.3 copy-start.16
  169.9 10.7 %copy-start.42 = (bf16[512,2048]{1,0:T(8,128)(2,1)S(1)}, bf16[512,2048]{1,0:T(8,128)(2,1)}, u32[]{:S(2)}) copy-start(bf16[512,2048]{1,0:T(8,128)(2,1)} %get-tuple-element.72) | copy-start | bytes 6291460
  169.9 31.8 %slice-start = ((s8[8388608]{0:T(1024)(128)(4,1)}), s8[4194304]{0:T(1024)(128)(4,1)S(1)}, s32[]{:S(2)}) async-start(s8[8388608]{0:T(1024)(128)(4,1)} %bitcast.216), calls=%async_computation | async-start | bytes 8388608
  180.6 12.5 %copy-start.28 = (bf16[2,256,2048]{2,1,0:T(8,128)(2,1)S(1)}, bf16[2,256,2048]{2,1,0:T(8,128)(2,1)}, u32[]{:S(2)}) copy-start(bf16[2,256,2048]{2,1,0:T(8,128)(2,1)} %param.27) | copy-start | bytes 6291460
  180.6 21.2 %slice-start.1 = ((s8[8388608]{0:T(1024)(128)(4,1)}), s8[4194304]{0:T(1024)(128)(4,1)S(1)}, s32[]{:S(2)}) async-start(s8[8388608]{0:T(1024)(128)(4,1)} %bitcast.216), calls=%async_computation.1 | async-start | bytes 8388608
  193.1 8.6 %copy-start.45 = (f32[512,2048]{1,0:T(8,128)}, f32[512,2048]{1,0:T(8,128)S(1)}, u32[]{:S(2)}) copy-start(f32[512,2048]{1,0:T(8,128)S(1)} %get-tuple-element.115) | copy-start | bytes 12582916
  193.1 17.9 %slice-start.2 = ((s8[8388608]{0:T(1024)(128)(4,1)}), s8[4194304]{0:T(1024)(128)(4,1)S(1)}, s32[]{:S(2)}) async-start(s8[8388608]{0:T(1024)(128)(4,1)} %bitcast.218), calls=%async_computation.2 | async-start | bytes 8388608
  201.7 9.2 %slice-start.3 = ((s8[8388608]{0:T(1024)(128)(4,1)}), s8[4194304]{0:T(1024)(128)(4,1)S(1)}, s32[]{:S(2)}) async-start(s8[8388608]{0:T(1024)(128)(4,1)} %bitcast.218), calls=%async_computation.3 | async-start | bytes 8388608
  346.8 1.0 copy-start.23
  346.9 2.0 copy-start.43
  348.9 10.1 %copy-start.30 = (bf16[2,16,4,128]{3,2,1,0:T(4,128)(2,1)S(1)}, bf16[2,16,4,128]{3,2,1,0:T(4,128)(2,1)}, u32[]{:S(2)}) copy-start(bf16[2,16,4,128]{3,2,1,0:T(4,128)(2,1)} %reshape.305) | copy-start | bytes 98308
  359.7 5.1 copy-start.9
  493.3 5.8 copy-start.3
  525.1 1.0 copy-start.15
  526.2 5.4 copy-start.4
  531.6 4.3 copy-start.39
  531.6 4.4 copy-start.38
  536.2 3.4 copy-start.29
  536.2 3.4 copy-start.11
  536.3 3.4 copy-start.25
  539.6 3.2 copy-start.13
  545.3 3.1 copy-start.5
  545.3 3.1 copy-start.19
  545.3 3.6 copy-start.27
  552.4 3.2 copy-start.10
  562.2 2.9 copy-start.17
  565.4 3.3 copy-start.41
  722.1 3.3 copy-start.21
  722.1 8.6 %copy-start.1 = (bf16[512,2048]{1,0:T(8,128)(2,1)S(1)}, bf16[512,2048]{1,0:T(8,128)(2,1)}, u32[]{:S(2)}) copy-start(bf16[512,2048]{1,0:T(8,128)(2,1)} %param.35) | copy-start | bytes 6291460
  725.4 1.4 copy-start.36
  725.5 2.0 copy-start.35
  725.5 2.7 copy-start.34
  725.5 3.3 copy-start.33
  725.5 4.0 copy-start.32
  725.5 4.6 copy-start.31

commit v3 on v2

--- a/solution.py
+++ b/solution.py
@@ -148,65 +148,66 @@
 
 class Ring:
     SCRATCH = (
-        ((6, 2, 128, JOB), F32),
+        ((2, 2, 128, JOB), F32),
+        ((2, 2, 128, JOB), F32),
         ((2, 2, 128, JOB), F32),
         ((4, 128, JOB), F32),
         ((6, 64, JOB), F32),
         ((64, JOB), F32),
     )
-    COPIES, LOADS = 13, 4
-
-    def __init__(self, net, grad, column, x_first, out, scratch):
-        self.net, self.grad, self.out = net, grad, out
-        self.columns = pl.ds(column * JOB, JOB)
+    COPIES = 13
+
+    def __init__(self, net, left, right, column, x_first, out, scratch):
+        self.net, self.left, self.right, self.out = net, left, right, out
+        self.column = column * JOB
         self.x_first = x_first
         self.axes = ("x", "y") if x_first else ("y", "x")
         self.one, self.two = (net.x, net.y) if x_first else (net.y, net.x)
-        self.got, self.turn, self.own, self.got_two, self.got_three = scratch
-
-    def piece(self, step, half):
+        self.sending, self.got, self.beside, self.own, self.got_two, self.got_three = scratch
+
+    def piece(self, step, half, target, add=False):
         at = (self.one + step) % 4
-        pair = pl.ds(2 * half, 2)
         if self.x_first:
-            return self.grad.at[at, pair, :, self.columns]
-        return self.grad.at[pair, at, :, self.columns]
+            left = self.left[:, pl.ds(pl.multiple_of(at * 512 + half * 256, 256), 256)]
+        else:
+            cut = lambda x: self.left[:, pl.ds(pl.multiple_of(x * 512 + at * 128, 128), 128)]
+            left = jnp.concatenate([cut(2 * half), cut(2 * half + 1)], axis=1)
+        for n in range(JOB // 256):
+            value = outer_sum(left, self.right[:, pl.ds(self.column + n * 256, 256)])
+            for j in range(2):
+                part = value[j * 128 : (j + 1) * 128]
+                if add:
+                    part = part + target[j, :, pl.ds(n * 256, 256)]
+                target[j, :, pl.ds(n * 256, 256)] = part
 
     def begin(self):
         net, axis = self.net, self.axes[0]
-        self.far = [
-            net.push(self.piece(2, 0), self.got.at[0], axis, 1),
-            net.push(self.piece(2, 1), self.got.at[1], axis, -1),
-        ]
-        self.loading = [
-            net.load(self.piece(1, 0), self.turn.at[0]),
-            net.load(self.piece(3, 1), self.turn.at[1]),
-            net.load(self.piece(0, 0), self.own.at[pl.ds(0, 2)]),
-            net.load(self.piece(0, 1), self.own.at[pl.ds(2, 2)]),
-        ]
+        self.far = []
+        for half, step in enumerate((1, -1)):
+            self.piece(2, half, self.sending.at[half])
+            self.far.append(net.push(self.sending.at[half], self.got.at[half], axis, step))
 
     def relay(self):
         net, axis = self.net, self.axes[0]
-        self.last = []
-        for i, step in enumerate((1, -1)):
-            self.loading[i].wait()
+        self.last, self.near = [], []
+        for i, (step, at) in enumerate(((1, 1), (-1, 3))):
             self.far[i].wait_recv()
-            for j in range(2):
-                add_rows(self.turn.at[i, j], self.got.at[i, j])
-            self.last.append(net.push(self.turn.at[i], self.got.at[2 + i], axis, step))
-        self.near = [
-            net.push(self.piece(1, 1), self.got.at[4], axis, 1),
-            net.push(self.piece(3, 0), self.got.at[5], axis, -1),
-        ]
+            self.piece(at, i, self.got.at[i], True)
+            self.last.append(net.push(self.got.at[i], self.own.at[pl.ds(2 * i, 2)], axis, step))
+        for i, (step, at) in enumerate(((1, 1), (-1, 3))):
+            self.far[i].wait_send()
+            self.piece(at, 1 - i, self.sending.at[i])
+            self.near.append(net.push(self.sending.at[i], self.beside.at[1 - i], axis, step))
 
     def second(self):
         net, axis, own = self.net, self.axes[1], self.own
-        for copy in self.loading[2:]:
-            copy.wait()
-        for copy in self.last + self.near:
-            copy.wait_recv()
-        for j in range(2):
-            add_rows(own.at[j], self.got.at[5, j], self.got.at[2, j])
-            add_rows(own.at[2 + j], self.got.at[4, j], self.got.at[3, j])
+        for half in range(2):
+            self.near[1 - half].wait_recv()
+            self.piece(0, half, self.beside.at[half], True)
+        for half in range(2):
+            self.last[half].wait_recv()
+            for j in range(2):
+                add_rows(own.at[2 * half + j], self.beside.at[half, j])
         self.part = lambda k, h: own.at[(self.two + k) % 4, pl.ds(h * 64, 64), :]
         got = self.got_two
         self.far_two = [
@@ -240,7 +241,7 @@
     def finish(self):
         self.final.wait_recv()
         self.out[...] = self.mine[...] + self.got_three[...]
-        for copy in self.far + self.last + self.near:
+        for copy in self.last + self.near:
             copy.wait_send()
         for copy in self.far_two + self.last_two + self.near_two + [self.final]:
             copy.wait_send()
@@ -435,14 +436,14 @@
     return out
 
 
-def backward_wide(share, x_rows, gain, extra, grad, number, more):
-    grad = grad.reshape(4, 4, 128, 2048)
-    ins = [(share, False), (x_rows, True), (gain, True), (extra, True), (grad, False)]
+def backward_wide(share, x_rows, gain, extra, left, right, number, more):
+    ins = [(share, False), (x_rows, True), (gain, True), (extra, True)]
+    ins += [(left, True), (right, True)]
     outs = [shape(256, 2048), shape(512, 2048, kind=BF16), shape(8, 2048)]
     outs += [shape(64, JOB)] * 4
     scratch = ring_scratch(4) + list(TensorSum.SCRATCH)
     copies = 4 * Ring.COPIES + TensorSum.COPIES
-    loads = 4 * Ring.LOADS + TensorSum.LOADS
+    loads = TensorSum.LOADS
     kind = more[0]
     if kind == "out":
         ins += [(more[1], False), (more[2], True)]
@@ -464,7 +465,7 @@
         work_refs = refs[n_in + n_out : -3]
         net = Net(*refs[-3:])
         net.greet(partners)
-        share_ref, x_ref, gain_ref, extra_ref, grad_ref = in_refs[:5]
+        share_ref, x_ref, gain_ref, extra_ref, left_ref, right_ref = in_refs[:6]
         rows_ref, low_ref, gain_sum = out_refs[:3]
         gain_sum[...] = jnp.zeros_like(gain_sum)
 
@@ -478,10 +479,11 @@
         work = TensorSum(net, share_ref, epilogue, low_ref, work_refs[n_rings : n_rings + 4])
         sets = take(work_refs, [len(Ring.SCRATCH)] * 4)
         rings = [
-            Ring(net, grad_ref, i, i % 2 == 0, out_refs[3 + i], sets[i]) for i in range(4)
+            Ring(net, left_ref, right_ref, i, i % 2 == 0, out_refs[3 + i], sets[i])
+            for i in range(4)
         ]
         if kind == "out":
-            more_ref, added_ref = in_refs[5:7]
+            more_ref, added_ref = in_refs[6:8]
             other = TensorSum(
                 net,
                 more_ref,
@@ -509,7 +511,7 @@
             work.begin()
             run_rings(rings, (begin, first, second, third))
             return
-        small_ref, all_ref = in_refs[5], out_refs[-1]
+        small_ref, all_ref = in_refs[6], out_refs[-1]
         state = {}
 
         def begin():
@@ -541,19 +543,22 @@
 
 
 def backward_last(share, x_rows, gain, extra, keep, grads, text_grad, sums, number):
-    grads = [grad.reshape(4, 4, 128, -1) for grad in grads]
-    jobs = [(i, c) for i, grad in enumerate(grads) for c in range(grad.shape[3] // JOB)]
-    count = len(jobs)
+    lefts = []
+    for left, _ in grads:
+        if not any(left is other for other in lefts):
+            lefts.append(left)
+    where = [[left is other for other in lefts].index(True) for left, _ in grads]
+    count = len(grads)
     ins = [(share, False), (x_rows, True), (gain, True), (extra, True), (keep, True)]
     ins += [(text_grad, True), (sums, True)]
-    ins += [(grad, False) for grad in grads]
+    ins += [(left, True) for left in lefts] + [(right, True) for _, right in grads]
     outs = [shape(512, 2048, kind=BF16), shape(8, 2048), shape(128, 1024)]
     outs += [shape(64, JOB)] * count
     scratch = ring_scratch(count) + list(TensorSum.SCRATCH)
     n_rings = len(ring_scratch(count))
     scratch += [((16, 2048), F32), ((128, 1024), F32), ((9, 8, 2048), F32)]
     copies = count * Ring.COPIES + TensorSum.COPIES + 9
-    loads = count * Ring.LOADS + TensorSum.LOADS
+    loads = TensorSum.LOADS
     partners = NEAR + ALL + [("zhi", 1)]
 
     def body(*refs):
@@ -579,8 +584,16 @@
         work = TensorSum(net, share_ref, epilogue, image_ref, work_refs[n_rings : n_rings + 4])
         sets = take(work_refs, [len(Ring.SCRATCH)] * count)
         rings = [
-            Ring(net, in_refs[7 + g], c, i % 2 == 0, out_refs[3 + i], sets[i])
-            for i, (g, c) in enumerate(jobs)
+            Ring(
+                net,
+                in_refs[7 + where[i]],
+                in_refs[7 + len(lefts) + i],
+                0,
+                i % 2 == 0,
+                out_refs[3 + i],
+                sets[i],
+            )
+            for i in range(count)
         ]
         state = {}
 
@@ -693,7 +706,8 @@
         second,
         gains[2],
         own(upstream).astype(F32),
-        outer_sum(upstream, active),
+        upstream,
+        active,
         2,
         ("out", product(active, contract), second),
     )
@@ -709,7 +723,8 @@
         first,
         gains[1],
         grad_second,
-        outer_sum(normed_three, grad_raised),
+        normed_three,
+        grad_raised,
         3,
         ("text", text_kv),
     )
@@ -728,12 +743,12 @@
     sums = jnp.zeros((8, width), F32)
     sums = sums.at[1].set(jnp.sum(second_sum, axis=0)).at[2].set(jnp.sum(third_sum, axis=0))
     grads = [
-        outer_sum(cross_out_grad, cross_rows),
-        outer_sum(normed_two, grad_cq),
-        outer_sum(self_out_grad, self_rows),
-        outer_sum(normed_one, grad_q),
-        outer_sum(normed_one, grad_k),
-        outer_sum(normed_one, grad_v),
+        (cross_out_grad, cross_rows),
+        (normed_two, grad_cq),
+        (self_out_grad, self_rows),
+        (normed_one, grad_q),
+        (normed_one, grad_k),
+        (normed_one, grad_v),
     ]
     keep = 1.0 - own(masked.reshape(count, 1)).astype(F32)
     image_grad, small, text_grads, to, tq, so, sq, sk, sv = backward_last(

time: 739 us -> 692 us (0.936)
  matrix products: 143 us -> 100 us
  local copies, waits for them, and re-layouts: 56.9 us -> 44.6 us
  Pallas kernels: 515 us -> 523 us
    dot_general x9 -> x1, matrix products: 46.1 us -> 2.66 us  [outer_sum(): lax.dot_general(left, right, (((0,), (0,)), ((), ())), preferred_element_...]
    dot_general x4 -> x0, local copies, waits for them, and re-layouts: 14 us -> none  [outer_sum(): lax.dot_general(left, right, (((0,), (0,)), ((), ())), preferred_element_...]
    pallas_call x5, Pallas kernels: 515 us -> 523 us  [call(): pl.pallas_call(body, name=name, out_shape=outs, in_specs=[spec(inside) fo...]
    unnamed x112 -> x106, local copies, waits for them, and re-layouts: 14.4 us -> 17.3 us
where the time goes in v3:
time: 692 us; the launch traced here: 684 us
  Pallas kernels  523 us (76%)
  matrix products  100 us (14%)
  local copies, waits for them, and re-layouts  44.6 us (6%)
  other arithmetic  15.3 us (2%)
    pallas_call x5, Pallas kernels, call(): pl.pallas_call(body, name=name, out_shape=outs, in_specs=[spec(inside) fo...  523 us
    dot_general x10, matrix products, product(): return jnp.dot(left, right, preferred_element_type=F32)  45.3 us
    dot_general x8, matrix products, back_product(): lax.dot_general(left, right, (((1,), (1,)), ((), ())), preferred_element_...  35.3 us
    unnamed x106, local copies, waits for them, and re-layouts  17.3 us

profile of v3, /device:TPU:0, one launch (start us, length us, event | category | flops | bytes accessed | tf_op | source)
XLA Modules:
  0.0 684.4 jit_solution(12634618440506481)
XLA Ops:
  1.5 2.3 select_reduce_fusion
  4.8 2.5 bitcast_select_fusion
  7.3 1.6 constant_dynamic-slice_fusion.1.refs_1_
  9.4 1.0 copy-done.24
  10.4 1.3 convolution_convert_fusion.3
  12.1 3.7 convolution_convert_fusion.4
  15.8 0.9 reshape.282
  16.7 1.3 copy.86
  18.5 1.3 copy-done.1
  21.2 1.2 convolution_convert_fusion.5
  22.5 2.9 fusion.12
  25.5 1.3 copy.67
  26.8 5.0 fusion.43.refs_0_
  32.2 1.1 copy.159
  33.3 60.6 %forward_sum_0.1 = (f32[256,2048]{1,0:T(8,128)}, bf16[512,2048]{1,0:T(8,128)(2,1)}, f32[4,4,32,256]{3,2,1,0:T(8,128)}) custom-call(f32[512,2048]{1,0:T(8,128)} %fusion.43.refs_0_, f32[256,2048]{1,0:T(8,128)} %constant_dynamic-slice_fusion.1.refs_1_, f32[1,2048]{1,0:T(1,128)} %bitcast.173, f32[4,32,1024]{2,1,0:T(8,128)} %bitcast.163), custom_call_target="tpu_custom_call" | custom-call | tf_op jit(solution)/shard_map/forward_sum_0/pallas_call | solution.py:326
  93.9 4.3 convolution_convert_fusion.2
  98.2 1.2 reshape.286
  99.4 3.2 convolution_convert_fusion.10
  103.3 1.0 fusion.49
  104.4 3.0 convolution_convert_fusion.11
  107.4 1.1 fusion.11
  108.6 1.3 copy.72
  109.9 3.2 fusion.44.refs_0_
  113.1 57.1 %forward_sum_1.1 = (f32[256,2048]{1,0:T(8,128)}, bf16[512,2048]{1,0:T(8,128)(2,1)}) custom-call(f32[512,2048]{1,0:T(8,128)} %fusion.44.refs_0_, f32[256,2048]{1,0:T(8,128)} %get-tuple-element.71.refs_1_, f32[1,2048]{1,0:T(1,128)} %bitcast.169), custom_call_target="tpu_custom_call" | custom-call | tf_op jit(solution)/shard_map/forward_sum_1/pallas_call | solution.py:326
  170.2 7.9 %fusion.50 = f32[512,2048]{1,0:T(8,128)S(1)} fusion(bf16[512,2048]{1,0:T(8,128)(2,1)} %bitcast.146, bf16[2048,2048]{1,0:T(8,128)(2,1)} %param.37), kind=kOutput, calls=%fused_computation.109 | convolution fusion | flops 4294967296 | bytes 14680064 | tf_op jit(solution)/shard_map/dot_general | solution.py:27
  178.2 10.7 %multiply_convert_fusion = (bf16[512,2048]{1,0:T(8,128)(2,1)S(1)}, bf16[512,2048]{1,0:T(8,128)(2,1)S(1)}) fusion(f32[512,2048]{1,0:T(8,128)S(1)} %fusion.50, bf16[512,2048]{1,0:T(8,128)(2,1)S(1)} %copy-done.25, bf16[2048,2048]{1,0:T(8,128)(2,1)} %param.36), kind=kOutput, calls=%fused_computation.11 | convolution fusion | flops 4318035968 | bytes 18874368 | tf_op jit(solution)/shard_map/dot_general | solution.py:19
  189.0 6.2 fusion.51.refs_0_
  195.2 9.7 %fusion.52.refs_6_ = f32[512,2048]{1,0:T(8,128)} fusion(bf16[512,2048]{1,0:T(8,128)(2,1)S(1)} %get-tuple-element.100.refs_5_, bf16[2048,2048]{1,0:T(8,128)(2,1)} %param.37), kind=kOutput, calls=%fused_computation.111 | convolution fusion | flops 4294967296 | bytes 14680064 | tf_op jit(solution)/shard_map/dot_general | solution.py:19
  204.9 1.6 dynamic-slice_convert_fusion.refs_3_
  206.5 123.2 %backward_sum_2.1 = (f32[256,2048]{1,0:T(8,128)}, bf16[512,2048]{1,0:T(8,128)(2,1)}, f32[8,2048]{1,0:T(8,128)}, f32[64,512]{1,0:T(8,128)}, f32[64,512]{1,0:T(8,1...) custom-call(f32[512,2048]{1,0:T(8,128)} %fusion.51.refs_0_, ...), custom_call_target="tpu_custom_call" | custom-call | tf_op jit(solution)/shard_map/backward_sum_2/pallas_call | solution.py:326
  329.7 1.9 maximum_bitcast_fusion
  331.6 3.7 convolution_convert_fusion.1
  335.3 2.1 reshape.291
  337.4 1.3 multiply_reduce_fusion.3
  339.0 1.2 fusion.20
  340.9 1.1 fusion.16
  342.0 1.3 copy.76
  343.4 4.8 fusion.45.refs_0_
  348.2 128.4 %backward_sum_3.1 = (f32[256,2048]{1,0:T(8,128)}, bf16[512,2048]{1,0:T(8,128)(2,1)}, f32[8,2048]{1,0:T(8,128)}, f32[64,512]{1,0:T(8,128)}, f32[64,512]{1,0:T(8,1...) custom-call(f32[512,2048]{1,0:T(8,128)} %fusion.45.refs_0_, ...), custom_call_target="tpu_custom_call" | custom-call | tf_op jit(solution)/shard_map/backward_sum_3/pallas_call | solution.py:326
  476.6 1.9 pad_maximum_fusion
  478.5 0.9 reduce_sum.78
  479.8 2.3 copy_bitcast_fusion.3
  482.2 2.7 convolution_bitcast_fusion.refs_5_
  484.9 1.3 convolution_convert_fusion
  486.1 0.9 reshape.295
  487.1 1.3 copy.89
  488.3 2.9 fusion.13
  491.2 2.1 copy.91
  493.3 2.3 multiply_reduce_fusion.1
  496.7 1.3 fusion.14
  498.0 2.1 copy.88
  500.1 5.1 fusion.47
  505.1 1.1 fusion.15
  506.2 1.3 copy.85
  507.6 3.0 fusion.46
  511.2 3.3 add_add_fusion.refs_0_
  514.5 0.9 copy.155
  515.4 0.9 copy.156
  516.3 0.9 copy.157
  518.1 0.9 copy.158
  518.9 153.4 %backward_last.1 = (bf16[512,2048]{1,0:T(8,128)(2,1)}, f32[8,2048]{1,0:T(8,128)}, f32[128,1024]{1,0:T(8,128)}, f32[64,512]{1,0:T(8,128)}, f32[64,512]{1,0:T(8,12...) custom-call(f32[512,2048]{1,0:T(8,128)} %add_add_fusion.refs_0_, ...), custom_call_target="tpu_custom_call" | custom-call | tf_op jit(solution)/shard_map/backward_last/pallas_call | solution.py:326
  672.4 1.9 fusion.48
  675.5 3.3 copy.169
  678.9 1.3 copy.170
  (131 shorter events, 15.0 us)
Async XLA Ops:
  0.6 109.3 %copy-start = (bf16[512,2048]{1,0:T(8,128)(2,1)S(1)}, bf16[512,2048]{1,0:T(8,128)(2,1)}, u32[]{:S(2)}) copy-start(bf16[512,2048]{1,0:T(8,128)(2,1)} %param.35) | copy-start | bytes 6291460
  0.7 3.2 copy-start.37
  0.7 3.2 copy-start.4
  1.5 3.2 copy-start.39
  7.3 2.1 copy-start.5
  7.3 3.1 copy-start.24
  12.1 5.9 copy-start.9
  18.0 2.2 copy-start.11
  18.0 2.5 copy-start.6
  18.0 3.2 copy-start.27
  18.5 1.3 copy-start.1
  26.8 5.0 copy-start.13
  26.8 5.0 copy-start.17
  99.4 3.9 copy-start.22
  99.4 3.9 copy-start.42
  109.9 3.2 copy-start.15
  170.2 8.0 %copy-start.25 = (bf16[512,2048]{1,0:T(8,128)(2,1)S(1)}, bf16[512,2048]{1,0:T(8,128)(2,1)}, u32[]{:S(2)}) copy-start(bf16[512,2048]{1,0:T(8,128)(2,1)} %get-tuple-element.72.refs_4_) | copy-start | bytes 6291460
  170.2 18.7 %slice-start = ((s8[8388608]{0:T(1024)(128)(4,1)}), s8[4194304]{0:T(1024)(128)(4,1)S(1)}, s32[]{:S(2)}) async-start(s8[8388608]{0:T(1024)(128)(4,1)} %bitcast.180), calls=%async_computation | async-start | bytes 8388608
  178.2 10.8 %slice-start.1 = ((s8[8388608]{0:T(1024)(128)(4,1)}), s8[4194304]{0:T(1024)(128)(4,1)S(1)}, s32[]{:S(2)}) async-start(s8[8388608]{0:T(1024)(128)(4,1)} %bitcast.180), calls=%async_computation.1 | async-start | bytes 8388608
  188.9 6.2 copy-start.26
  189.0 6.2 copy-start.19
  195.2 9.7 %copy-start.8 = (bf16[2,256,2048]{2,1,0:T(8,128)(2,1)S(1)}, bf16[2,256,2048]{2,1,0:T(8,128)(2,1)}, u32[]{:S(2)}) copy-start(bf16[2,256,2048]{2,1,0:T(8,128)(2,1)} %param.27) | copy-start | bytes 6291460
  335.3 3.4 copy-start.23
  335.3 5.6 copy-start.30
  348.2 131.2 %copy-start.38 = (f32[8,2048]{1,0:T(8,128)S(1)}, f32[8,2048]{1,0:T(8,128)}, u32[]{:S(2)}) copy-start(f32[8,2048]{1,0:T(8,128)} %get-tuple-element.82) | copy-start | bytes 196612
  479.8 5.0 copy-start.29
  479.8 2.3 copy-start.41
  482.2 2.7 copy-start.18
  482.2 2.7 copy-start.20
  493.3 2.3 copy-start.2
  495.7 1.0 copy-start.12
  500.1 5.1 copy-start.10
  507.6 3.1 copy-start.3
  507.6 3.1 copy-start.16
  507.6 3.6 copy-start.28
  511.2 4.2 copy-start.7
  514.5 2.7 copy-start.40
  514.5 3.6 copy-start.14
  675.5 3.3 copy-start.21
  678.8 1.4 copy-start.36
  678.8 2.0 copy-start.35
  678.8 2.7 copy-start.34
  678.8 3.3 copy-start.33
  678.8 4.0 copy-start.32
  678.8 4.6 copy-start.31

commit v4 on v3

v4 whole, which is shorter than its diff:
```python
import functools

import jax
import jax.numpy as jnp
from jax import lax
from jax.experimental import pallas as pl
from jax.experimental.pallas import tpu as pltpu
from jax.sharding import PartitionSpec as P

HEAD = 128
EPS = 1e-05
MESH = pl.DeviceIdType.MESH
F32, BF16 = jnp.float32, jnp.bfloat16
CHUNK = 64
JOB = 512


def product(left, right):
    return jnp.dot(left, right, preferred_element_type=F32)


def outer_sum(left, right):
    return lax.dot_general(left, right, (((0,), (0,)), ((), ())), preferred_element_type=F32)


def back_product(left, right):
    return lax.dot_general(left, right, (((1,), (1,)), ((), ())), preferred_element_type=F32)


def low(value):
    return value.astype(BF16)


def layer_norm(rows, gain):
    mean = jnp.mean(rows, axis=-1, keepdims=True)
    centred = rows - mean
    spread = jnp.mean(centred * centred, axis=-1, keepdims=True)
    return centred * lax.rsqrt(spread + EPS) * gain


def norm_back(rows, gain, grad):
    mean = jnp.mean(rows, axis=-1, keepdims=True)
    centred = rows - mean
    spread = jnp.mean(centred * centred, axis=-1, keepdims=True)
    root = lax.rsqrt(spread + EPS)
    xhat = centred * root
    scaled = grad * gain
    row_grad = root * (
        scaled
        - jnp.mean(scaled, axis=-1, keepdims=True)
        - xhat * jnp.mean(scaled * xhat, axis=-1, keepdims=True)
    )
    return row_grad, grad * xhat


def attend_scores(query, keys, valid):
    scores = jnp.einsum("bqhd,bkhd->bhqk", query, keys, preferred_element_type=F32)
    scores = scores * HEAD ** (-0.5)
    if valid is None:
        return scores
    return jnp.where(valid[:, None, None, :], scores, -1e30)


def attend_forward(query, keys, values, valid):
    scores = attend_scores(query, keys, valid)
    total = jax.nn.logsumexp(scores, axis=-1, keepdims=True)
    weights_low = low(jnp.exp(scores - total))
    mixed = jnp.einsum("bhqk,bkhd->bqhd", weights_low, values, preferred_element_type=F32)
    return low(mixed), total


def attend_backward(query, keys, values, valid, total, upstream):
    scale = HEAD ** (-0.5)
    probs = jnp.exp(attend_scores(query, keys, valid) - total)
    grad_values = jnp.einsum("bhqk,bqhd->bkhd", low(probs), upstream, preferred_element_type=F32)
    grad_probs = jnp.einsum("bqhd,bkhd->bhqk", upstream, values, preferred_element_type=F32)
    inner = jnp.sum(grad_probs * probs, axis=-1, keepdims=True)
    grad_scores = low(probs * (grad_probs - inner))
    grad_query = jnp.einsum("bhqk,bkhd->bqhd", grad_scores, keys, preferred_element_type=F32)
    grad_keys = jnp.einsum("bhqk,bqhd->bkhd", grad_scores, query, preferred_element_type=F32)
    return low(grad_query * scale), low(grad_keys * scale), low(grad_values)


class Net:
    def __init__(self, send, recv, local, free):
        dp, tensor = lax.axis_index("dp"), lax.axis_index("tensor")
        self.x, self.y, self.z = dp // 8, (dp // 2) % 4, dp % 2
        self.tensor, self.core = tensor, tensor % 2
        self.send, self.recv, self.local, self.free = send, recv, local, free
        self.sent, self.loads, self.stores = 0, 0, []

    def device(self, kind, step=1):
        x, y, z, tensor = self.x, self.y, self.z, self.tensor
        if kind == "x":
            x = (x + step + 4) % 4
        elif kind == "y":
            y = (y + step + 4) % 4
        elif kind == "zhi":
            z = 1 - z
        elif kind == "zlo":
            tensor = (tensor + 2) % 4
        else:
            tensor = tensor + 1 - 2 * self.core
        return (x * 8 + y * 2 + z, tensor)

    def greet(self, partners):
        barrier = pltpu.get_barrier_semaphore()
        for kind, step in partners:
            pl.semaphore_signal(
                barrier, inc=1, device_id=self.device(kind, step), device_id_type=MESH
            )
        pl.semaphore_wait(barrier, len(partners))

    def release(self, kind):
        pl.semaphore_signal(self.free, inc=1, device_id=self.device(kind), device_id_type=MESH)

    def await_release(self):
        pl.semaphore_wait(self.free, 1)

    def push(self, source, target, kind, step=1):
        copy = pltpu.make_async_remote_copy(
            src_ref=source,
            dst_ref=target,
            send_sem=self.send.at[self.sent],
            recv_sem=self.recv.at[self.sent],
            device_id=self.device(kind, step),
            device_id_type=MESH,
        )
        self.sent += 1
        copy.start()
        return copy

    def load(self, source, target):
        copy = pltpu.make_async_copy(source, target, self.local.at[self.loads])
        self.loads += 1
        copy.start()
        return copy

    def store(self, out):
        self.stores.append(self.load(out.vmem, out.hbm))


class Late:
    def __init__(self, net, hbm, vmem):
        self.net, self.hbm, self.vmem, self.copy, self.here = net, hbm, vmem, None, False

    def start(self):
        self.copy = self.net.load(self.hbm, self.vmem)

    def ref(self):
        if self.copy is None:
            self.start()
        if not self.here:
            self.copy.wait()
            self.here = True
        return self.vmem


class Out:
    def __init__(self, hbm, vmem):
        self.hbm, self.vmem = hbm, vmem


def add_rows(target, *sources):
    rows = target.shape[0]
    step = 16 if target.shape[1] > 1024 else 32

    def body(i, carry):
        at = pl.ds(pl.multiple_of(i * step, step), step)
        value = target[at, :]
        for source in sources:
            value = value + source[at, :]
        target[at, :] = value
        return carry

    lax.fori_loop(0, rows // step, body, 0)


class RingOne:
    SCRATCH = (
        ((2, 2, 128, JOB), F32),
        ((2, 2, 128, JOB), F32),
        ((2, 2, 128, JOB), F32),
    )
    COPIES = 6

    def __init__(self, net, left, right, column, x_first, own, scratch):
        self.net, self.left, self.right, self.own = net, left, right, own
        self.column = column * JOB
        self.x_first = x_first
        self.axis, self.one = ("x", net.x) if x_first else ("y", net.y)
        self.sending, self.got, self.beside = scratch

    def piece(self, step, half, target, add=False):
        at = (self.one + step) % 4
        if self.x_first:
            left = self.left[:, pl.ds(pl.multiple_of(at * 512 + half * 256, 256), 256)]
        else:
            cut = lambda x: self.left[:, pl.ds(pl.multiple_of(x * 512 + at * 128, 128), 128)]
            left = jnp.concatenate([cut(2 * half), cut(2 * half + 1)], axis=1)
        for n in range(JOB // 256):
            value = outer_sum(left, self.right[:, pl.ds(self.column + n * 256, 256)])
            for j in range(2):
                part = value[j * 128 : (j + 1) * 128]
                if add:
                    part = part + target[j, :, pl.ds(n * 256, 256)]
                target[j, :, pl.ds(n * 256, 256)] = part

    def begin(self):
        self.far = []
        for half, step in enumerate((1, -1)):
            self.piece(2, half, self.sending.at[half])
            self.far.append(
                self.net.push(self.sending.at[half], self.got.at[half], self.axis, step)
            )

    def relay(self):
        net, axis = self.net, self.axis
        self.last, self.near = [], []
        for i, (step, at) in enumerate(((1, 1), (-1, 3))):
            self.far[i].wait_recv()
            self.piece(at, i, self.got.at[i], True)
            self.last.append(net.push(self.got.at[i], self.own.at[pl.ds(2 * i, 2)], axis, step))
        for i, (step, at) in enumerate(((1, 1), (-1, 3))):
            self.far[i].wait_send()
            self.piece(at, 1 - i, self.sending.at[i])
            self.near.append(net.push(self.sending.at[i], self.beside.at[1 - i], axis, step))

    def close(self):
        for half in range(2):
            self.near[1 - half].wait_recv()
            self.piece(0, half, self.beside.at[half], True)
        for half in range(2):
            self.last[half].wait_recv()
            for j in range(2):
                add_rows(self.own.at[2 * half + j], self.beside.at[half, j])

    def done(self):
        for copy in self.last + self.near:
            copy.wait_send()


class RingTwo:
    SCRATCH = (((6, 64, JOB), F32), ((64, JOB), F32))
    PARTS = (((4, 64, JOB), F32),)
    COPIES, LOADS = 7, 4

    def __init__(self, net, own, x_first, out, scratch, parts=None):
        self.net, self.own, self.out, self.parts = net, own, out, parts
        self.axis, self.two = ("y", net.y) if x_first else ("x", net.x)
        self.got, self.got_last = scratch

    def part(self, step, half):
        return self.own.at[(self.two + step) % 4, pl.ds(half * 64, 64), :]

    def begin(self):
        net, axis, got = self.net, self.axis, self.got
        self.far = [
            net.push(self.part(2, 0), got.at[0], axis, 1),
            net.push(self.part(2, 1), got.at[1], axis, -1),
        ]
        self.near = [
            net.push(self.part(1, 1), got.at[4], axis, 1),
            net.push(self.part(3, 0), got.at[5], axis, -1),
        ]
        self.read = [self.part(*at) for at in ((1, 0), (3, 1), (0, 0), (0, 1))]
        self.loading = []
        if self.parts is not None:
            self.loading = [net.load(ref, self.parts.at[i]) for i, ref in enumerate(self.read)]
            self.read = [self.parts.at[i] for i in range(4)]

    def relay(self):
        net, axis, got = self.net, self.axis, self.got
        self.last = []
        for copy in self.loading:
            copy.wait()
        for i, step in enumerate((1, -1)):
            self.far[i].wait_recv()
            add_rows(got.at[i], self.read[i])
            self.last.append(net.push(got.at[i], got.at[2 + i], axis, step))

    def third(self):
        net, got = self.net, self.got
        for copy in self.near + self.last:
            copy.wait_recv()
        add_rows(got.at[5], got.at[2], self.read[2])
        add_rows(got.at[4], got.at[3], self.read[3])
        self.final = net.push(got.at[4 + net.z], self.got_last, "zhi")

    def finish(self):
        self.final.wait_recv()
        self.out[...] = self.got[5 - self.net.z] + self.got_last[...]
        for copy in self.far + self.near + self.last + [self.final]:
            copy.wait_send()


class TensorSum:
    SCRATCH = tuple(((256 // CHUNK, CHUNK, 2048), F32) for _ in range(4))
    COPIES, LOADS = 3 * (256 // CHUNK), 256 // CHUNK

    def __init__(self, net, share, epilogue, whole, scratch):
        self.net, self.share, self.epilogue, self.whole = net, share, epilogue, whole
        self.mine, self.got_core, self.got_z, self.got_rows = scratch
        self.steps = range(256 // CHUNK)

    def rows(self, core, step):
        return pl.ds(pl.multiple_of(core * 256 + step * CHUNK, CHUNK), CHUNK)

    def begin(self):
        net = self.net
        self.swaps = [
            net.push(self.share.at[self.rows(1 - net.core, j)], self.got_core.at[j], "core")
            for j in self.steps
        ]
        self.loading = [
            net.load(self.share.at[self.rows(net.core, j)], self.mine.at[j]) for j in self.steps
        ]

    def exchange(self):
        self.over = []
        for j in self.steps:
            self.loading[j].wait()
            self.swaps[j].wait_recv()
            add_rows(self.mine.at[j], self.got_core.at[j])
            self.over.append(self.net.push(self.mine.at[j], self.got_z.at[j], "zlo"))

    def work(self):
        net = self.net
        self.spread = []
        for j in self.steps:
            self.over[j].wait_recv()

            def body(i, carry, j=j):
                at = pl.ds(pl.multiple_of(i * 8, 8), 8)
                rows = pl.ds(pl.multiple_of(j * CHUNK + i * 8, 8), 8)
                self.got_core[j, at, :] = self.epilogue(
                    rows, self.mine[j, at, :] + self.got_z[j, at, :]
                )
                return carry

            lax.fori_loop(0, CHUNK // 8, body, 0)
            self.spread.append(net.push(self.got_core.at[j], self.got_rows.at[j], "core"))
            self.round(self.got_core, j, net.core)

    def round(self, source, step, core):
        def body(i, carry):
            at = pl.ds(pl.multiple_of(i * 16, 16), 16)
            rows = pl.ds(pl.multiple_of(core * 256 + step * CHUNK + i * 16, 16), 16)
            self.whole[rows, :] = source[step, at, :].astype(BF16)
            return carry

        lax.fori_loop(0, CHUNK // 16, body, 0)

    def finish(self):
        for j in self.steps:
            self.spread[j].wait_recv()
            self.round(self.got_rows, j, 1 - self.net.core)
        for copy in self.swaps + self.over + self.spread:
            copy.wait_send()


NEAR = [("core", 1), ("zlo", 1)]
RING = [("x", 1), ("x", -1), ("y", 1), ("y", -1)]
ALL = [("x", 1), ("x", 2), ("x", 3), ("y", 1), ("y", 2), ("y", 3)]


def vmem(shapes):
    return [pltpu.VMEM(shape, kind) for shape, kind in shapes]


def call(body, ins, outs, scratch, copies, loads, number, name):
    spec = lambda how: pl.BlockSpec(memory_space=pltpu.VMEM if how == "vmem" else pl.ANY)
    late = [(a.shape, a.dtype) for a, how in ins if how == "load"]
    kept = [(o.shape, o.dtype) for o, how in outs if how == "store"]

    def kernel(*refs):
        refs, net = Refs(refs[:-4]), Net(*refs[-4:])
        in_refs, out_refs = refs.some(len(ins)), refs.some(len(outs))
        late_refs, kept_refs = refs.some(len(late)), refs.some(len(kept))
        in_refs = [
            Late(net, ref, late_refs.pop(0)) if how == "load" else ref
            for ref, (_, how) in zip(in_refs, ins)
        ]
        out_refs = [
            Out(ref, kept_refs.pop(0)) if how == "store" else ref
            for ref, (_, how) in zip(out_refs, outs)
        ]
        body(net, Refs(in_refs), Refs(out_refs), refs)
        for copy in net.stores:
            copy.wait()

    return pl.pallas_call(
        kernel,
        name=name,
        out_shape=[o for o, _ in outs],
        in_specs=[spec(how) for _, how in ins],
        out_specs=[spec(how) for _, how in outs],
        scratch_shapes=vmem(late + kept + list(scratch))
        + [
            pltpu.SemaphoreType.DMA((copies,)),
            pltpu.SemaphoreType.DMA((copies,)),
            pltpu.SemaphoreType.DMA((loads + len(late) + len(kept),)),
            pltpu.SemaphoreType.REGULAR,
        ],
        compiler_params=pltpu.CompilerParams(
            collective_id=number, has_side_effects=True, vmem_limit_bytes=60 * 2**20
        ),
    )(*[array for array, _ in ins])


def shape(*dims, kind=F32):
    return jax.ShapeDtypeStruct(dims, kind)


def blocks(count, width, body):
    def step(i, carry):
        body(pl.ds(pl.multiple_of(i * width, width), width))
        return carry

    lax.fori_loop(0, count, step, 0)


class Refs:
    def __init__(self, refs):
        self.refs = list(refs)

    def one(self):
        return self.refs.pop(0)

    def some(self, count):
        return [self.refs.pop(0) for _ in range(count)]


def forward_self(share, rows, gain, text_blocks, text_rows, text_key, text_value):
    ins = [(share, "hbm"), (rows, "load"), (gain, "vmem"), (text_blocks, "hbm")]
    ins += [(text_rows, "load"), (text_key, "load"), (text_value, "load")]
    outs = [(shape(256, 2048), "store"), (shape(512, 2048, kind=BF16), "store")]
    outs += [(shape(4, 4, 32, 256), "vmem")] + [(shape(32, 512, kind=BF16), "vmem")] * 2
    scratch = list(TensorSum.SCRATCH) + [((4, 32, 1024), F32)]

    def body(net, in_refs, out_refs, refs):
        share_ref, late_rows, gain_ref, text_ref, *late_text = in_refs.some(7)
        total, normed, columns_ref, *text_outs = out_refs.some(5)
        sum_scratch, got = refs.some(4), refs.one()
        net.greet(NEAR + ALL)
        rows_ref, total_ref = late_rows.vmem, total.vmem

        def epilogue(at, value):
            value = rows_ref[at, :] + value
            total_ref[at, :] = value
            return layer_norm(value, gain_ref[...])

        work = TensorSum(net, share_ref, epilogue, normed.vmem, sum_scratch)
        work.begin()
        own = net.load(text_ref.at[net.x], got.at[0])
        first = [net.push(text_ref.at[(net.x + k) % 4], got.at[k], "x", k) for k in (1, 2, 3)]
        late_rows.start()
        every(late_text, "start")
        work.exchange()
        own.wait()
        for copy in first:
            copy.wait_recv()
        cut = lambda y: pl.ds(pl.multiple_of(y * 256, 256), 256)
        kept = net.load(got.at[:, :, cut(net.y)], columns_ref.at[0])
        second = [
            net.push(got.at[:, :, cut((net.y + k) % 4)], columns_ref.at[k], "y", k)
            for k in (1, 2, 3)
        ]
        text_rows_ref = late_text[0].ref()
        for weight, out in zip(late_text[1:], text_outs):
            out[...] = low(product(text_rows_ref[...], weight.ref()[...]))
        late_rows.ref()
        work.work()
        net.store(total)
        work.finish()
        net.store(normed)
        kept.wait()
        for copy in second:
            copy.wait_recv()
        for copy in first + second:
            copy.wait_send()

    copies, loads = TensorSum.COPIES + 6, TensorSum.LOADS + 2
    return call(body, ins, outs, scratch, copies, loads, 0, "forward_self")


def forward_cross(share, rows, gain, upstream, contract):
    ins = [(share, "hbm"), (rows, "load"), (gain, "vmem"), (upstream, "load"), (contract, "load")]
    outs = [(shape(256, 2048), "store"), (shape(512, 2048, kind=BF16), "store")]
    outs += [(shape(512, 2048), "store")]
    scratch = list(TensorSum.SCRATCH)

    def body(net, in_refs, out_refs, refs):
        share_ref, late_rows, gain_ref, late_upstream, late_contract = in_refs.some(5)
        total, normed, grad = out_refs.some(3)
        net.greet(NEAR)
        rows_ref, total_ref = late_rows.vmem, total.vmem

        def epilogue(at, value):
            value = rows_ref[at, :] + value
            total_ref[at, :] = value
            return layer_norm(value, gain_ref[...])

        work = TensorSum(net, share_ref, epilogue, normed.vmem, refs.some(4))
        work.begin()
        every([late_upstream, late_contract, late_rows], "start")
        work.exchange()
        upstream_ref, contract_ref = late_upstream.ref(), late_contract.ref()

        def part(at):
            grad.vmem[:, at] = back_product(upstream_ref[...], contract_ref[at, :])

        blocks(8, 256, part)
        net.store(grad)
        late_rows.ref()
        work.work()
        net.store(total)
        work.finish()
        net.store(normed)

    return call(
        body, ins, outs, scratch, TensorSum.COPIES, TensorSum.LOADS, 1, "forward_cross"
    )


def norm_back_sum(net, share_ref, x_ref, gain_ref, extra_ref, rows_ref, low_ref, gain_sum, scratch):
    gain_sum[...] = jnp.zeros_like(gain_sum)

    def epilogue(at, total):
        row_grad, terms = norm_back(x_ref[at, :], gain_ref[...], total)
        gain_sum[...] += terms
        result = extra_ref[at, :] + row_grad
        rows_ref[at, :] = result
        return result

    return TensorSum(net, share_ref, epilogue, low_ref, scratch)


def every(parts, step):
    for part in parts:
        getattr(part, step)()


def backward_first(share, x_rows, gain, extra, left, right, contract):
    ins = [(share, "hbm"), (x_rows, "load"), (gain, "vmem"), (extra, "load"), (left, "load")]
    ins += [(right, "load"), (contract, "load")]
    outs = [(shape(256, 2048), "store"), (shape(512, 2048, kind=BF16), "store")]
    outs += [(shape(8, 2048), "vmem"), (shape(512, 2048), "store")]
    outs += [(shape(4, 128, JOB), "store")] * 4
    scratch = list(TensorSum.SCRATCH) + list(RingOne.SCRATCH) * 4

    def body(net, in_refs, out_refs, refs):
        share_ref, late_x, gain_ref, late_extra, late_left, late_right = in_refs.some(6)
        late_contract = in_refs.one()
        rows, lows, gain_sum, out_share, *owns = out_refs.some(8)
        sum_scratch = refs.some(4)
        rings = [
            RingOne(net, late_left.vmem, late_right.vmem, i, i % 2 == 0, owns[i].vmem, refs.some(3))
            for i in range(4)
        ]
        every([late_left, late_right], "start")
        net.greet(NEAR + RING)
        x_ref = late_x.vmem
        work = norm_back_sum(
            net, share_ref, x_ref, gain_ref, late_extra.vmem, rows.vmem, lows.vmem, gain_sum, sum_scratch
        )
        work.begin()
        every([late_contract, late_x, late_extra], "start")
        late_left.ref(), late_right.ref()
        every(rings, "begin")
        work.exchange()
        every(rings, "relay")
        right_ref, contract_ref = late_right.ref(), late_contract.ref()

        def part(at):
            out_share.vmem[:, at] = product(right_ref[...], contract_ref[:, at])

        blocks(8, 256, part)
        late_x.ref(), late_extra.ref()
        joins = jnp.where(net.tensor < 2, 1.0, 0.0)

        def join(i, carry):
            at = pl.ds(pl.multiple_of(i * 16, 16), 16)
            to = pl.ds(pl.multiple_of(net.core * 256 + i * 16, 16), 16)
            out_share.vmem[to, :] += x_ref[at, :] * joins
            return carry

        lax.fori_loop(0, 16, join, 0)
        net.store(out_share)
        work.work()
        net.store(rows)
        work.finish()
        net.store(lows)
        for ring, own in zip(rings, owns):
            ring.close()
            net.store(own)
        every(rings, "done")

    copies, loads = TensorSum.COPIES + 4 * RingOne.COPIES, TensorSum.LOADS
    return call(body, ins, outs, scratch, copies, loads, 2, "backward_first")


def grouped(pairs):
    lefts = []
    for left, _ in pairs:
        if not any(left is other for other in lefts):
            lefts.append(left)
    return lefts, [[left is other for other in lefts].index(True) for left, _ in pairs]


def backward_second(share, x_rows, gain, extra, owns, wide, narrow, text, out_share):
    pairs = [wide] + narrow
    ones = [(0, i, i % 2 == 0) for i in range(4)]
    ones += [(1 + i, 0, i % 2 == 0) for i in range(len(narrow))]
    ins = [(share, "hbm"), (x_rows, "load"), (gain, "vmem"), (extra, "load"), (text, "hbm")]
    ins += [(out_share, "hbm")] + [(own, "hbm") for own in owns]
    ins += [(array, "load") for pair in pairs for array in pair]
    outs = [(shape(256, 2048), "store"), (shape(512, 2048, kind=BF16), "store")]
    outs += [(shape(8, 2048), "vmem"), (shape(4, 4, 32, 1024), "vmem")]
    outs += [(shape(512, 2048, kind=BF16), "hbm")]
    outs += [(shape(64, JOB), "vmem")] * len(owns)
    outs += [(shape(4, 128, JOB), "store")] * len(ones)
    scratch = list(TensorSum.SCRATCH) + [TensorSum.SCRATCH[0]]
    scratch += list(RingTwo.SCRATCH + RingTwo.PARTS) * len(owns)
    scratch += list(RingOne.SCRATCH) * len(ones)

    def body(net, in_refs, out_refs, refs):
        share_ref, late_x, gain_ref, late_extra, text_ref, out_share_ref = in_refs.some(6)
        own_refs, late_pairs = in_refs.some(len(owns)), [in_refs.some(2) for _ in pairs]
        rows, lows, gain_sum, all_ref, layer_out = out_refs.some(5)
        final_refs, nexts = out_refs.some(len(owns)), out_refs.some(len(ones))
        mine, got_core, got_z, got_rows = refs.some(4)
        got_z_two = refs.one()
        twos = [
            RingTwo(net, own, i % 2 == 0, final_refs[i], refs.some(2), refs.one())
            for i, own in enumerate(own_refs)
        ]
        rings = [
            RingOne(
                net, *[late.vmem for late in late_pairs[p]], c, x_first, nexts[i].vmem, refs.some(3)
            )
            for i, (p, c, x_first) in enumerate(ones)
        ]
        for pair in late_pairs:
            every(pair, "start")
        net.greet(NEAR + ALL + [("zhi", 1)])
        work = norm_back_sum(
            net,
            share_ref,
            late_x.vmem,
            gain_ref,
            late_extra.vmem,
            rows.vmem,
            lows.vmem,
            gain_sum,
            (mine, got_core, got_z, got_rows),
        )
        layer = TensorSum(
            net,
            out_share_ref,
            lambda at, total: total,
            lows.vmem,
            (mine, got_core, got_z_two, got_rows),
        )
        work.begin()
        kept = net.load(text_ref, all_ref.at[0, 0])
        by_x = [net.push(text_ref, all_ref.at[0, k], "x", k) for k in (1, 2, 3)]
        every([late_x, late_extra], "start")
        for pair in late_pairs:
            every(pair, "ref")
        every(twos, "begin")
        every(rings, "begin")
        work.exchange()
        every(twos, "relay")
        every(rings, "relay")
        kept.wait()
        for copy in by_x:
            copy.wait_recv()
        by_y = [net.push(all_ref.at[0], all_ref.at[k], "y", k) for k in (1, 2, 3)]
        every([late_x, late_extra], "ref")
        work.work()
        net.store(rows)
        work.finish()
        net.release("core")
        lows_copy = net.load(lows.vmem, lows.hbm)
        net.await_release()
        layer.begin()
        layer.exchange()
        every(twos, "third")
        for ring, own in zip(rings[:2] + rings[4:], nexts[:2] + nexts[4:]):
            ring.close()
            net.store(own)
        every(twos, "finish")
        lows_copy.wait()
        layer.work()
        layer.finish()
        net.stores.append(net.load(lows.vmem, layer_out))
        for ring, own in zip(rings[2:4], nexts[2:4]):
            ring.close()
            net.store(own)
        for copy in by_y:
            copy.wait_recv()
        for copy in by_x + by_y:
            copy.wait_send()
        every(rings, "done")

    copies = 2 * TensorSum.COPIES + 6 + len(owns) * RingTwo.COPIES + len(ones) * RingOne.COPIES
    loads = 2 * TensorSum.LOADS + 2 + len(owns) * RingTwo.LOADS
    return call(body, ins, outs, scratch, copies, loads, 3, "backward_second")


def backward_last(share, x_rows, gain, extra, keep, owns, narrow, text_grad, sums):
    lefts, where = grouped(narrow)
    count = len(narrow)
    ins = [(share, "hbm"), (x_rows, "load"), (gain, "vmem"), (extra, "load"), (keep, "vmem")]
    ins += [(text_grad, "vmem"), (sums, "vmem")] + [(own, "hbm") for own in owns]
    ins += [(left, "load") for left in lefts] + [(right, "load") for _, right in narrow]
    outs = [(shape(512, 2048, kind=BF16), "store"), (shape(8, 2048), "vmem")]
    outs += [(shape(128, 1024), "vmem")] + [(shape(64, JOB), "vmem")] * (len(owns) + count)
    scratch = list(TensorSum.SCRATCH)
    scratch += [((16, 2048), F32), ((128, 1024), F32), ((9, 8, 2048), F32)]
    scratch += list(RingTwo.SCRATCH + RingTwo.PARTS) * len(owns)
    scratch += (list(RingTwo.SCRATCH + RingOne.SCRATCH) + [((4, 128, JOB), F32)]) * count

    def body(net, in_refs, out_refs, refs):
        share_ref, late_x, gain_ref, late_extra, keep_ref, text_ref, sums_ref = in_refs.some(7)
        own_refs = in_refs.some(len(owns))
        late_lefts, late_rights = in_refs.some(len(lefts)), in_refs.some(count)
        image, small_ref, text_out = out_refs.some(3)
        old_refs, new_refs = out_refs.some(len(owns)), out_refs.some(count)
        sum_scratch = refs.some(4)
        acc_ref, got_text, got_small = refs.some(3)
        old = [
            RingTwo(net, own, i % 2 == 0, old_refs[i], refs.some(2), refs.one())
            for i, own in enumerate(own_refs)
        ]
        ones, twos = [], []
        for i in range(count):
            two_scratch, one_scratch, own = refs.some(2), refs.some(3), refs.one()
            left, right = late_lefts[where[i]].vmem, late_rights[i].vmem
            ones.append(RingOne(net, left, right, 0, i % 2 == 0, own, one_scratch))
            twos.append(RingTwo(net, own, i % 2 == 0, new_refs[i], two_scratch))
        every(late_lefts + late_rights, "start")
        net.greet(NEAR + ALL + [("zhi", 1)])
        acc_ref[...] = jnp.zeros_like(acc_ref)
        x_ref, extra_ref = late_x.vmem, late_extra.vmem

        def epilogue(at, total):
            row_grad, terms = norm_back(x_ref[at, :], gain_ref[...], total)
            result = extra_ref[at, :] + row_grad
            kept = keep_ref[at, :] > 0.5
            acc_ref[0:8, :] += terms
            acc_ref[8:16, :] += jnp.where(kept, 0.0, result)
            return jnp.where(kept, result, 0.0)

        work = TensorSum(net, share_ref, epilogue, image.vmem, sum_scratch)
        work.begin()
        every([late_x, late_extra], "start")
        every(late_lefts + late_rights, "ref")
        every(old, "begin")
        every(ones, "begin")
        work.exchange()
        every(old, "relay")
        every(ones, "relay")
        every([late_x, late_extra], "ref")
        work.work()
        got_small[0] = sums_ref[...]
        got_small[0, 0:1, :] = jnp.sum(acc_ref[0:8, :], axis=0, keepdims=True)
        got_small[0, 3:4, :] = jnp.sum(acc_ref[8:16, :], axis=0, keepdims=True)
        by_core = net.push(got_small.at[0], got_small.at[1], "core")
        text_copy = net.push(
            text_ref.at[pl.ds(pl.multiple_of((1 - net.z) * 128, 128), 128)], got_text, "zhi"
        )
        work.finish()
        net.store(image)
        by_core.wait()
        got_small[0] += got_small[1]
        by_x = [net.push(got_small.at[0], got_small.at[1 + k], "x", k) for k in (1, 2, 3)]
        every(old, "third")
        for one, two in zip(ones, twos):
            one.close()
            two.begin()
        every(old, "finish")
        for copy in by_x:
            copy.wait()
        got_small[0] += got_small[2] + got_small[3] + got_small[4]
        by_y = [net.push(got_small.at[0], got_small.at[4 + k], "y", k) for k in (1, 2, 3)]
        every(twos, "relay")
        for copy in by_y:
            copy.wait()
        got_small[0] += got_small[5] + got_small[6] + got_small[7]
        by_z = net.push(got_small.at[0], got_small.at[8], "zhi")
        every(twos, "third")
        text_copy.wait()
        mine_text = text_ref[pl.ds(pl.multiple_of(net.z * 128, 128), 128), :]
        text_out[...] = mine_text + got_text[...]
        by_z.wait()
        small_ref[...] = got_small[0] + got_small[8]
        every(twos, "finish")
        every(ones, "done")

    copies = TensorSum.COPIES + 9 + (len(owns) + count) * RingTwo.COPIES + count * RingOne.COPIES
    loads = TensorSum.LOADS + len(owns) * RingTwo.LOADS
    return call(body, ins, outs, scratch, copies, loads, 4, "backward_last")


def shards(
    image,
    text,
    masked,
    text_len,
    cotangent,
    self_query,
    self_key,
    self_value,
    self_output,
    text_query,
    text_key,
    text_value,
    text_output,
    expand,
    contract,
    first_gain,
    second_gain,
    third_gain,
    mask_token,
):
    items, length, width = image.shape
    words = text.shape[1]
    count = items * length
    core = lax.axis_index("tensor") % 2
    heads = self_query.shape[1] // HEAD
    split = lambda rows: rows.reshape(items, -1, heads, HEAD)
    flat = lambda value: value.reshape(-1, heads * HEAD)
    gains = [g.reshape(1, width) for g in (first_gain, second_gain, third_gain)]
    own = lambda rows: lax.dynamic_slice_in_dim(rows, core * length, length, axis=0)

    text_rows = text.reshape(items * words, text.shape[2])
    text_blocks = text_rows.astype(F32).reshape(items * words, 4, -1).transpose(1, 0, 2)
    upstream = cotangent.reshape(count, width)

    hidden = masked.reshape(count, 1) == 1
    start = jnp.where(hidden, mask_token[None, :], image.reshape(count, width).astype(F32))
    normed_one = low(layer_norm(start, first_gain))
    query = split(low(product(normed_one, self_query)))
    keys = split(low(product(normed_one, self_key)))
    values = split(low(product(normed_one, self_value)))
    self_mixed, self_total = attend_forward(query, keys, values, None)
    self_rows = flat(self_mixed)
    start_own = own(start)
    first, normed_two, text_columns, cross_keys, cross_values = forward_self(
        product(self_rows, self_output),
        start_own,
        gains[1],
        text_blocks,
        text_rows,
        text_key,
        text_value,
    )
    cross_keys, cross_values = split(cross_keys), split(cross_values)
    text_columns = low(text_columns.reshape(-1, text_columns.shape[-1]))

    cross_query = split(low(product(normed_two, text_query)))
    present = jnp.arange(words)[None, :] < text_len[:, None]
    cross_mixed, cross_total = attend_forward(cross_query, cross_keys, cross_values, present)
    cross_rows = flat(cross_mixed)
    second, normed_three, grad_active = forward_cross(
        product(cross_rows, text_output), first, gains[2], upstream, contract
    )

    raised = product(normed_three, expand)
    gelu, pull = jax.vjp(jax.nn.gelu, raised)
    active = low(gelu)
    grad_raised = low(pull(grad_active)[0])
    grad_second, cross_out_grad, third_sum, out_share, *owns = backward_first(
        back_product(grad_raised, expand),
        second,
        gains[2],
        own(upstream).astype(F32),
        upstream,
        active,
        contract,
    )

    grad_mixed = split(low(back_product(cross_out_grad, text_output)))
    grad_q, grad_k, grad_v = attend_backward(
        cross_query, cross_keys, cross_values, present, cross_total, grad_mixed
    )
    grad_cq = flat(grad_q)
    text_kv = jnp.concatenate([flat(grad_k), flat(grad_v)], axis=1).astype(F32)
    grad_first, self_out_grad, second_sum, gathered, layer_out, *rest = backward_second(
        back_product(grad_cq, text_query),
        first,
        gains[1],
        grad_second,
        owns,
        (normed_three, grad_raised),
        [(cross_out_grad, cross_rows), (normed_two, grad_cq)],
        text_kv,
        out_share,
    )
    contract_t, owns = rest[:4], rest[4:]
    gathered = low(gathered.reshape(-1, gathered.shape[-1]))
    text_grads = outer_sum(text_columns, gathered)

    grad_mixed = split(low(back_product(self_out_grad, self_output)))
    grad_q, grad_k, grad_v = map(
        flat, attend_backward(query, keys, values, None, self_total, grad_mixed)
    )
    shares = (
        back_product(grad_q, self_query)
        + back_product(grad_k, self_key)
        + back_product(grad_v, self_value)
    )
    sums = jnp.zeros((8, width), F32)
    sums = sums.at[1].set(jnp.sum(second_sum, axis=0)).at[2].set(jnp.sum(third_sum, axis=0))
    keep = 1.0 - own(masked.reshape(count, 1)).astype(F32)
    image_grad, small, text_grads, *rest = backward_last(
        shares,
        start_own,
        gains[0],
        grad_first,
        keep,
        owns,
        [
            (self_out_grad, self_rows),
            (normed_one, grad_q),
            (normed_one, grad_k),
            (normed_one, grad_v),
        ],
        text_grads,
        sums,
    )
    expand_grad, (to, tq, so, sq, sk, sv) = rest[:4], rest[4:]

    share = width // 32
    small = lax.dynamic_slice_in_dim(small, lax.axis_index("dp") * share, share, axis=1)
    cut = text_grads.shape[1] // 2
    joined = lambda parts: jnp.concatenate(parts, axis=1)
    return (
        layer_out.reshape(image.shape),
        image_grad.reshape(image.shape),
        sq,
        sk,
        sv,
        so.T,
        tq,
        text_grads[:, :cut],
        text_grads[:, cut:],
        to.T,
        joined(expand_grad),
        joined(contract_t).T,
        small[0],
        small[1],
        small[2],
        small[3],
    )


def solution(mesh):
    rows, split = P("dp", None, None), P(None, "tensor")
    turned, grads, grads_t = P("tensor", None), P("dp", "tensor"), P("tensor", "dp")
    ins = (rows, rows, P("dp", None), P("dp"), rows, split, split, split, turned)
    ins += (split, split, split, turned, split, turned, P(), P(), P(), P())
    outs = (rows, rows, grads, grads, grads, grads_t, grads, grads, grads, grads_t)
    outs += (grads, grads_t, P("dp"), P("dp"), P("dp"), P("dp"))
    return jax.shard_map(shards, mesh=mesh, in_specs=ins, out_specs=outs, check_vma=False)
```

time: 692 us -> 616 us (0.89)
  Pallas kernels: 523 us -> 479 us
  matrix products: 100 us -> 74.3 us
    pallas_call x5, Pallas kernels: 523 us -> 479 us  [call(): pl.pallas_call(kernel, name=name, out_shape=[o for o, _ in outs], in_spec...]
    dot_general x10 -> x7, matrix products: 45.3 us -> 32.3 us  [product(): return jnp.dot(left, right, preferred_element_type=F32)]
    dot_general x8 -> x7, matrix products: 35.3 us -> 30.3 us  [back_product(): lax.dot_general(left, right, (((1,), (1,)), ((), ())), preferred_element_...]
    unnamed x106 -> x100, local copies, waits for them, and re-layouts: 17.3 us -> 17.6 us
where the time goes in v4:
time: 616 us; the launch traced here: 608 us
  Pallas kernels  479 us (78%)
  matrix products  74.3 us (12%)
  local copies, waits for them, and re-layouts  38 us (6%)
  other arithmetic  15.2 us (2%)
    pallas_call x5, Pallas kernels, call(): pl.pallas_call(kernel, name=name, out_shape=[o for o, _ in outs], in_spec...  479 us
    dot_general x7, matrix products, product(): return jnp.dot(left, right, preferred_element_type=F32)  32.3 us
    dot_general x7, matrix products, back_product(): lax.dot_general(left, right, (((1,), (1,)), ((), ())), preferred_element_...  30.3 us
    unnamed x100, local copies, waits for them, and re-layouts  17.6 us

profile of v4, /device:TPU:0, one launch (start us, length us, event | category | flops | bytes accessed | tf_op | source)
XLA Modules:
  0.0 608.0 jit_solution(9954723347928555574)
XLA Ops:
  0.7 0.8 broadcast_compare_fusion
  1.5 2.3 select_reduce_fusion
  3.9 0.9 multiply_reduce_fusion
  4.8 2.5 bitcast_select_fusion
  7.3 1.6 constant_dynamic-slice_fusion.1.refs_1_
  9.4 1.0 copy-done.23
  10.4 1.3 convolution_convert_fusion.3
  12.1 3.7 convolution_convert_fusion.4
  15.8 0.9 reshape.279
  16.7 1.3 copy.86
  18.5 1.3 copy-done.2
  20.5 0.7 copy-done.24
  21.2 1.2 convolution_convert_fusion.5
  22.5 2.9 fusion.12
  25.5 1.3 copy.67
  26.8 5.0 fusion.43.refs_0_
  32.2 1.1 copy.159
  33.3 59.3 %forward_self.1 = (f32[256,2048]{1,0:T(8,128)}, bf16[512,2048]{1,0:T(8,128)(2,1)}, f32[4,4,32,256]{3,2,1,0:T(8,128)}, bf16[32,512]{1,0:T(8,128)(2,1)}, bf16[32,512]{1,0:T(8,128)(2,1)}) custom-call(f32[512,2048]{1,0:T(8,128)} %fusion.43.refs_0_, f32[256,2048]{1,0:T(8,128)} %constant_dynamic-slice_fusion.1.refs_1_, f32[1,2048]{1,0:T(1,128)} %bitcast.160, ...), custom_call_target="tpu_custom_call" | custom-call | tf_op jit(solution)/shard_map/forward_self/pallas_call | solution.py:392
  92.7 4.3 convolution_convert_fusion.2
  97.0 1.2 reshape.285
  98.9 1.1 fusion.11
  100.1 1.3 copy.72
  101.4 3.3 fusion.44.refs_0_
  104.7 55.6 %forward_cross.1 = (f32[256,2048]{1,0:T(8,128)}, bf16[512,2048]{1,0:T(8,128)(2,1)}, f32[512,2048]{1,0:T(8,128)}) custom-call(f32[512,2048]{1,0:T(8,128)} %fusion.44.refs_0_, f32[256,2048]{1,0:T(8,128)} %get-tuple-element.87.refs_1_, f32[1,2048]{1,0:T(1,128)} %bitcast.163, bf16[512,2048]{1,0:T(8,128)(2,1)} %bitcast.132, bf16[2048,2048]{1,0:T(8,128)(2,1)} %refs_6_.3), custom_call_target="tpu_custom_call" | custom-call | tf_op jit(solution)/shard_map/forward_cross/pallas_call | solution.py:392
  160.3 13.6 %multiply_convert_fusion = (bf16[512,2048]{1,0:T(8,128)(2,1)}, bf16[512,2048]{1,0:T(8,128)(2,1)S(1)}) fusion(f32[512,2048]{1,0:T(8,128)} %get-tuple-element.88, bf16[512,2048]{1,0:T(8,128)(2,1)} %get-tuple-element.89.refs_10_, bf16[2048,2048]{1,0:T(8,128)(2,1)} %param.36), kind=kOutput, calls=%fused_computation.11 | convolution fusion | flops 4318035968 | bytes 18874368 | tf_op jit(solution)/shard_map/dot_general | solution.py:19
  173.9 10.9 %fusion.50.refs_0_ = f32[512,2048]{1,0:T(8,128)} fusion(bf16[512,2048]{1,0:T(8,128)(2,1)S(1)} %get-tuple-element.129.refs_11_, bf16[2048,2048]{1,0:T(8,128)(2,1)} %param.36), kind=kOutput, calls=%fused_computation.107 | convolution fusion | flops 4294967296 | bytes 14680064 | tf_op jit(solution)/shard_map/dot_general | solution.py:27
  184.8 1.6 dynamic-slice_convert_fusion.refs_3_
  186.3 78.7 %backward_first.1 = (f32[256,2048]{1,0:T(8,128)}, bf16[512,2048]{1,0:T(8,128)(2,1)}, f32[8,2048]{1,0:T(8,128)}, f32[512,2048]{1,0:T(8,128)}, f32[4,128,512]{2,1,...) custom-call(f32[512,2048]{1,0:T(8,128)} %fusion.50.refs_0_, ...), custom_call_target="tpu_custom_call" | custom-call | tf_op jit(solution)/shard_map/backward_first/pallas_call | solution.py:392
  265.0 3.7 convolution_convert_fusion.1
  268.7 1.2 reshape.290
  270.9 1.1 copy_bitcast_fusion.3
  272.4 0.7 maximum_convert_fusion.refs_4_
  273.1 3.3 fusion.45.refs_0_
  276.4 151.4 %backward_second.1 = (f32[256,2048]{1,0:T(8,128)}, bf16[512,2048]{1,0:T(8,128)(2,1)}, f32[8,2048]{1,0:T(8,128)}, f32[4,4,32,1024]{3,2,1,0:T(8,128)}, bf16[512,20...) custom-call(f32[512,2048]{1,0:T(8,128)} %fusion.45.refs_0_, ...), custom_call_target="tpu_custom_call" | custom-call | tf_op jit(solution)/shard_map/backward_second/pallas_call | solution.py:392
  427.8 1.9 maximum_bitcast_fusion
  429.8 0.9 reduce_sum.78
  430.9 3.2 convolution_bitcast_fusion.refs_5_
  434.1 1.3 convolution_convert_fusion
  435.4 0.9 reshape.295
  436.3 1.3 copy.89
  437.6 1.3 fusion.13
  439.0 2.1 copy.91
  441.0 0.6 multiply_reduce_fusion.1
  443.4 4.9 fusion.47
  449.0 3.0 fusion.46
  452.0 0.6 copy-done.25
  452.6 3.3 add_add_fusion.refs_0_
  455.9 0.9 copy.155
  456.8 0.9 copy.156
  457.7 0.9 copy.157
  458.7 0.7 convert_subtract_fusion.refs_4_
  459.4 0.9 copy.158
  460.3 133.6 %backward_last.1 = (bf16[512,2048]{1,0:T(8,128)(2,1)}, f32[8,2048]{1,0:T(8,128)}, f32[128,1024]{1,0:T(8,128)}, f32[64,512]{1,0:T(8,128)}, f32[64,512]{1,0:T(8,12...) custom-call(f32[512,2048]{1,0:T(8,128)} %add_add_fusion.refs_0_, ...), custom_call_target="tpu_custom_call" | custom-call | tf_op jit(solution)/shard_map/backward_last/pallas_call | solution.py:392
  593.9 1.9 pad_maximum_fusion
  595.8 1.9 fusion.48
  597.7 0.7 constant_dynamic-slice_fusion
  598.9 3.3 copy.169
  602.3 1.3 copy.170
  603.6 0.7 copy.171
  604.3 0.7 copy.172
  604.9 0.7 copy.173
  605.6 0.7 copy.174
  606.2 0.7 copy.175
  606.9 0.7 copy.176
  (120 shorter events, 8.1 us)
Async XLA Ops:
  0.6 100.7 %copy-start = (bf16[512,2048]{1,0:T(8,128)(2,1)S(1)}, bf16[512,2048]{1,0:T(8,128)(2,1)}, u32[]{:S(2)}) copy-start(bf16[512,2048]{1,0:T(8,128)(2,1)} %param.35) | copy-start | bytes 6291460
  0.7 3.2 copy-start.34
  0.7 3.2 copy-start.5
  1.5 3.2 copy-start.36
  7.3 2.1 copy-start.7
  7.3 3.1 copy-start.23
  12.1 5.9 copy-start.9
  18.0 2.2 copy-start.11
  18.0 2.5 copy-start.8
  18.0 3.2 copy-start.24
  18.5 1.3 copy-start.2
  26.8 5.0 copy-start.13
  26.8 5.0 copy-start.26
  92.7 5.5 copy-start.38
  92.7 5.5 copy-start.41
  97.0 1.7 copy-start.37
  98.1 0.8 copy-start.20
  173.9 10.9 %copy-start.17 = (bf16[512,2048]{1,0:T(8,128)(2,1)}, bf16[512,2048]{1,0:T(8,128)(2,1)S(1)}, u32[]{:S(2)}) copy-start(bf16[512,2048]{1,0:T(8,128)(2,1)S(1)} %get-tuple-element.129.refs_11_) | copy-start | bytes 6291460
  173.9 10.9 %copy-start.6 = (bf16[2,256,2048]{2,1,0:T(8,128)(2,1)S(1)}, bf16[2,256,2048]{2,1,0:T(8,128)(2,1)}, u32[]{:S(2)}) copy-start(bf16[2,256,2048]{2,1,0:T(8,128)(2,1)} %param.27) | copy-start | bytes 6291460
  270.1 1.8 copy-start.21
  270.8 2.2 copy-start.22
  276.4 154.2 %copy-start.35 = (f32[8,2048]{1,0:T(8,128)S(1)}, f32[8,2048]{1,0:T(8,128)}, u32[]{:S(2)}) copy-start(f32[8,2048]{1,0:T(8,128)} %get-tuple-element.104) | copy-start | bytes 196612
  276.4 154.5 %copy-start.40 = (f32[4,4,32,256]{3,2,1,0:T(8,128)S(1)}, f32[4,4,32,256]{3,2,1,0:T(8,128)}, u32[]{:S(2)}) copy-start(f32[4,4,32,256]{3,2,1,0:T(8,128)} %get-tuple-element.101) | copy-start | bytes 1572868
  430.9 3.2 copy-start.27
  430.9 3.2 copy-start.16
  430.9 3.2 copy-start.18
  434.1 3.5 copy-start.3
  441.6 1.0 copy-start.12
  443.4 4.9 copy-start.10
  448.9 3.1 copy-start.4
  448.9 3.1 copy-start.15
  449.0 3.6 copy-start.25
  455.9 2.7 copy-start.39
  455.9 3.6 copy-start.14
  598.9 3.3 copy-start.19
  598.9 8.6 %copy-start.1 = (bf16[512,2048]{1,0:T(8,128)(2,1)S(1)}, bf16[512,2048]{1,0:T(8,128)(2,1)}, u32[]{:S(2)}) copy-start(bf16[512,2048]{1,0:T(8,128)(2,1)} %param.35) | copy-start | bytes 6291460
  602.2 1.4 copy-start.33
  602.2 2.0 copy-start.32
  602.2 2.7 copy-start.31
  602.2 3.3 copy-start.30
  602.3 4.0 copy-start.29
  602.3 4.6 copy-start.28

commit v5 on v4

--- a/solution.py
+++ b/solution.py
@@ -53,32 +53,24 @@
     return row_grad, grad * xhat
 
 
-def attend_scores(query, keys, valid):
-    scores = jnp.einsum("bqhd,bkhd->bhqk", query, keys, preferred_element_type=F32)
-    scores = scores * HEAD ** (-0.5)
-    if valid is None:
-        return scores
-    return jnp.where(valid[:, None, None, :], scores, -1e30)
-
-
-def attend_forward(query, keys, values, valid):
-    scores = attend_scores(query, keys, valid)
-    total = jax.nn.logsumexp(scores, axis=-1, keepdims=True)
-    weights_low = low(jnp.exp(scores - total))
-    mixed = jnp.einsum("bhqk,bkhd->bqhd", weights_low, values, preferred_element_type=F32)
-    return low(mixed), total
-
-
-def attend_backward(query, keys, values, valid, total, upstream):
+def attend_probs(query, keys, valid):
+    scores = back_product(query, keys) * HEAD ** (-0.5)
+    if valid is not None:
+        scores = jnp.where(valid > 0.5, scores, -1e30)
+    raised = jnp.exp(scores - jnp.max(scores, axis=-1, keepdims=True))
+    return raised / jnp.sum(raised, axis=-1, keepdims=True)
+
+
+def attend_backward(query, keys, values, valid, upstream):
     scale = HEAD ** (-0.5)
-    probs = jnp.exp(attend_scores(query, keys, valid) - total)
-    grad_values = jnp.einsum("bhqk,bqhd->bkhd", low(probs), upstream, preferred_element_type=F32)
-    grad_probs = jnp.einsum("bqhd,bkhd->bhqk", upstream, values, preferred_element_type=F32)
+    probs = attend_probs(query, keys, valid)
+    grad_values = outer_sum(low(probs), upstream)
+    grad_probs = back_product(upstream, values)
     inner = jnp.sum(grad_probs * probs, axis=-1, keepdims=True)
     grad_scores = low(probs * (grad_probs - inner))
-    grad_query = jnp.einsum("bhqk,bkhd->bqhd", grad_scores, keys, preferred_element_type=F32)
-    grad_keys = jnp.einsum("bhqk,bqhd->bkhd", grad_scores, query, preferred_element_type=F32)
-    return low(grad_query * scale), low(grad_keys * scale), low(grad_values)
+    grad_query = product(grad_scores, keys) * scale
+    grad_keys = outer_sum(grad_scores, query) * scale
+    return low(grad_query), low(grad_keys), low(grad_values)
 
 
 class Net:
@@ -174,6 +166,17 @@
         return carry
 
     lax.fori_loop(0, rows // step, body, 0)
+
+
+def each_head(rows, other_rows):
+    for item in range(2):
+        for head in range(4):
+            columns = pl.ds(head * HEAD, HEAD)
+            yield (
+                item,
+                (pl.ds(item * rows, rows), columns),
+                (pl.ds(item * other_rows, other_rows), columns),
+            )
 
 
 class RingOne:
@@ -298,16 +301,38 @@
     SCRATCH = tuple(((256 // CHUNK, CHUNK, 2048), F32) for _ in range(4))
     COPIES, LOADS = 3 * (256 // CHUNK), 256 // CHUNK
 
-    def __init__(self, net, share, epilogue, whole, scratch):
+    HALF = (((256, 2048), F32),)
+
+    def __init__(self, net, share, epilogue, whole, scratch, half=None):
         self.net, self.share, self.epilogue, self.whole = net, share, epilogue, whole
+        self.half = half
         self.mine, self.got_core, self.got_z, self.got_rows = scratch
         self.steps = range(256 // CHUNK)
 
     def rows(self, core, step):
         return pl.ds(pl.multiple_of(core * 256 + step * CHUNK, CHUNK), CHUNK)
 
+    def free_half(self):
+        for copy in self.swaps:
+            copy.wait_send()
+        self.swaps_sent = True
+
     def begin(self):
         net = self.net
+        self.loading, self.swaps_sent = [], False
+        if self.half is not None:
+            for n in range(4):
+                self.half[:, pl.ds(n * 512, 512)] = self.share(1 - net.core, n)
+            self.swaps = [
+                net.push(self.half.at[pl.ds(j * CHUNK, CHUNK)], self.got_core.at[j], "core")
+                for j in self.steps
+            ]
+            for n in range(4):
+                value = self.share(net.core, n)
+                for j in self.steps:
+                    rows = value[j * CHUNK : (j + 1) * CHUNK]
+                    self.mine[j, :, pl.ds(n * 512, 512)] = rows
+            return
         self.swaps = [
             net.push(self.share.at[self.rows(1 - net.core, j)], self.got_core.at[j], "core")
             for j in self.steps
@@ -318,8 +343,9 @@
 
     def exchange(self):
         self.over = []
+        for copy in self.loading:
+            copy.wait()
         for j in self.steps:
-            self.loading[j].wait()
             self.swaps[j].wait_recv()
             add_rows(self.mine.at[j], self.got_core.at[j])
             self.over.append(self.net.push(self.mine.at[j], self.got_z.at[j], "zlo"))
@@ -355,7 +381,7 @@
         for j in self.steps:
             self.spread[j].wait_recv()
             self.round(self.got_rows, j, 1 - self.net.core)
-        for copy in self.swaps + self.over + self.spread:
+        for copy in ([] if self.swaps_sent else self.swaps) + self.over + self.spread:
             copy.wait_send()
 
 
@@ -431,18 +457,42 @@
         return [self.refs.pop(0) for _ in range(count)]
 
 
-def forward_self(share, rows, gain, text_blocks, text_rows, text_key, text_value):
-    ins = [(share, "hbm"), (rows, "load"), (gain, "vmem"), (text_blocks, "hbm")]
+def own_rows(core):
+    return pl.ds(pl.multiple_of(core * 256, 256), 256)
+
+
+def forward_self(normed, weights, rows, gain, text_blocks, text_rows, text_key, text_value):
+    ins = [(normed, "load")] + [(weight, "load") for weight in weights]
+    ins += [(rows, "load"), (gain, "vmem"), (text_blocks, "hbm")]
     ins += [(text_rows, "load"), (text_key, "load"), (text_value, "load")]
     outs = [(shape(256, 2048), "store"), (shape(512, 2048, kind=BF16), "store")]
     outs += [(shape(4, 4, 32, 256), "vmem")] + [(shape(32, 512, kind=BF16), "vmem")] * 2
-    scratch = list(TensorSum.SCRATCH) + [((4, 32, 1024), F32)]
+    outs += [(shape(512, 512, kind=BF16), "store")] * 4
+    scratch = list(TensorSum.SCRATCH + TensorSum.HALF) + [((4, 32, 1024), F32)]
 
     def body(net, in_refs, out_refs, refs):
-        share_ref, late_rows, gain_ref, text_ref, *late_text = in_refs.some(7)
+        late_normed, late_weights = in_refs.one(), in_refs.some(4)
+        late_rows, gain_ref, text_ref, *late_text = in_refs.some(6)
         total, normed, columns_ref, *text_outs = out_refs.some(5)
-        sum_scratch, got = refs.some(4), refs.one()
+        attention = out_refs.some(4)
+        sum_scratch, half, got = refs.some(4), refs.one(), refs.one()
+        every([late_normed] + late_weights, "start")
         net.greet(NEAR + ALL)
+        own = net.load(text_ref.at[net.x], got.at[0])
+        first = [net.push(text_ref.at[(net.x + k) % 4], got.at[k], "x", k) for k in (1, 2, 3)]
+        normed_in = late_normed.ref()
+        for late, out in zip(late_weights[:3], attention):
+            out.vmem[...] = low(product(normed_in[...], late.ref()[...]))
+        query_ref, keys_ref, values_ref, mixed_ref = [out.vmem for out in attention]
+        for _, at, to in each_head(256, 256):
+            probs = attend_probs(query_ref[at], keys_ref[to], None)
+            mixed_ref[at] = low(product(low(probs), values_ref[to]))
+        for out in attention:
+            net.store(out)
+        output_ref = late_weights[3].ref()
+        share = lambda core, n: product(
+            mixed_ref[own_rows(core), :], output_ref[:, pl.ds(n * 512, 512)]
+        )
         rows_ref, total_ref = late_rows.vmem, total.vmem
 
         def epilogue(at, value):
@@ -450,10 +500,8 @@
             total_ref[at, :] = value
             return layer_norm(value, gain_ref[...])
 
-        work = TensorSum(net, share_ref, epilogue, normed.vmem, sum_scratch)
+        work = TensorSum(net, share, epilogue, normed.vmem, sum_scratch, half)
         work.begin()
-        own = net.load(text_ref.at[net.x], got.at[0])
-        first = [net.push(text_ref.at[(net.x + k) % 4], got.at[k], "x", k) for k in (1, 2, 3)]
         late_rows.start()
         every(late_text, "start")
         work.exchange()
@@ -484,16 +532,32 @@
     return call(body, ins, outs, scratch, copies, loads, 0, "forward_self")
 
 
-def forward_cross(share, rows, gain, upstream, contract):
-    ins = [(share, "hbm"), (rows, "load"), (gain, "vmem"), (upstream, "load"), (contract, "load")]
+def forward_cross(normed, weights, keys, values, present, rows, gain, upstream, contract):
+    ins = [(normed, "load")] + [(weight, "load") for weight in weights]
+    ins += [(keys, "vmem"), (values, "vmem"), (present, "vmem")]
+    ins += [(rows, "load"), (gain, "vmem"), (upstream, "load"), (contract, "load")]
     outs = [(shape(256, 2048), "store"), (shape(512, 2048, kind=BF16), "store")]
-    outs += [(shape(512, 2048), "store")]
-    scratch = list(TensorSum.SCRATCH)
+    outs += [(shape(512, 2048), "store")] + [(shape(512, 512, kind=BF16), "store")] * 2
+    scratch = list(TensorSum.SCRATCH + TensorSum.HALF)
 
     def body(net, in_refs, out_refs, refs):
-        share_ref, late_rows, gain_ref, late_upstream, late_contract = in_refs.some(5)
-        total, normed, grad = out_refs.some(3)
+        late_normed, late_query, late_output = in_refs.some(3)
+        keys_ref, values_ref, present_ref = in_refs.some(3)
+        late_rows, gain_ref, late_upstream, late_contract = in_refs.some(4)
+        total, normed, grad, query, mixed = out_refs.some(5)
+        every([late_normed, late_query, late_output], "start")
         net.greet(NEAR)
+        query_ref, mixed_ref = query.vmem, mixed.vmem
+        query_ref[...] = low(product(late_normed.ref()[...], late_query.ref()[...]))
+        for item, at, to in each_head(256, 16):
+            probs = attend_probs(query_ref[at], keys_ref[to], present_ref[pl.ds(item, 1), :])
+            mixed_ref[at] = low(product(low(probs), values_ref[to]))
+        net.store(query)
+        net.store(mixed)
+        output_ref = late_output.ref()
+        share = lambda core, n: product(
+            mixed_ref[own_rows(core), :], output_ref[:, pl.ds(n * 512, 512)]
+        )
         rows_ref, total_ref = late_rows.vmem, total.vmem
 
         def epilogue(at, value):
@@ -501,7 +565,7 @@
             total_ref[at, :] = value
             return layer_norm(value, gain_ref[...])
 
-        work = TensorSum(net, share_ref, epilogue, normed.vmem, refs.some(4))
+        work = TensorSum(net, share, epilogue, normed.vmem, refs.some(4), refs.one())
         work.begin()
         every([late_upstream, late_contract, late_rows], "start")
         work.exchange()
@@ -598,14 +662,6 @@
 
     copies, loads = TensorSum.COPIES + 4 * RingOne.COPIES, TensorSum.LOADS
     return call(body, ins, outs, scratch, copies, loads, 2, "backward_first")
-
-
-def grouped(pairs):
-    lefts = []
-    for left, _ in pairs:
-        if not any(left is other for other in lefts):
-            lefts.append(left)
-    return lefts, [[left is other for other in lefts].index(True) for left, _ in pairs]
 
 
 def backward_second(share, x_rows, gain, extra, owns, wide, narrow, text, out_share):
@@ -709,26 +765,29 @@
     return call(body, ins, outs, scratch, copies, loads, 3, "backward_second")
 
 
-def backward_last(share, x_rows, gain, extra, keep, owns, narrow, text_grad, sums):
-    lefts, where = grouped(narrow)
-    count = len(narrow)
-    ins = [(share, "hbm"), (x_rows, "load"), (gain, "vmem"), (extra, "load"), (keep, "vmem")]
-    ins += [(text_grad, "vmem"), (sums, "vmem")] + [(own, "hbm") for own in owns]
-    ins += [(left, "load") for left in lefts] + [(right, "load") for _, right in narrow]
+def backward_last(
+    attention, weights, upstream, normed, x_rows, gain, extra, keep, owns, text_grad, sums
+):
+    count = 4
+    ins = [(array, "load") for array in attention] + [(weights[3], "hbm")]
+    ins += [(weight, "load") for weight in weights[:3]]
+    ins += [(upstream, "load"), (normed, "load"), (x_rows, "load"), (gain, "vmem"), (extra, "hbm"), (keep, "vmem")]
+    ins += [(text_grad, "hbm"), (sums, "vmem")] + [(own, "hbm") for own in owns]
     outs = [(shape(512, 2048, kind=BF16), "store"), (shape(8, 2048), "vmem")]
     outs += [(shape(128, 1024), "vmem")] + [(shape(64, JOB), "vmem")] * (len(owns) + count)
-    scratch = list(TensorSum.SCRATCH)
+    scratch = list(TensorSum.SCRATCH + TensorSum.HALF) + [((512, 512), BF16)] * 4
     scratch += [((16, 2048), F32), ((128, 1024), F32), ((9, 8, 2048), F32)]
     scratch += list(RingTwo.SCRATCH + RingTwo.PARTS) * len(owns)
     scratch += (list(RingTwo.SCRATCH + RingOne.SCRATCH) + [((4, 128, JOB), F32)]) * count
 
     def body(net, in_refs, out_refs, refs):
-        share_ref, late_x, gain_ref, late_extra, keep_ref, text_ref, sums_ref = in_refs.some(7)
+        late_attention, late_output, late_weights = in_refs.some(4), in_refs.one(), in_refs.some(3)
+        late_upstream, late_normed = in_refs.some(2)
+        late_x, gain_ref, extra_hbm, keep_ref, text_ref, sums_ref = in_refs.some(6)
         own_refs = in_refs.some(len(owns))
-        late_lefts, late_rights = in_refs.some(len(lefts)), in_refs.some(count)
         image, small_ref, text_out = out_refs.some(3)
         old_refs, new_refs = out_refs.some(len(owns)), out_refs.some(count)
-        sum_scratch = refs.some(4)
+        sum_scratch, half, grad_mixed, grads = refs.some(4), refs.one(), refs.one(), refs.some(3)
         acc_ref, got_text, got_small = refs.some(3)
         old = [
             RingTwo(net, own, i % 2 == 0, old_refs[i], refs.some(2), refs.one())
@@ -737,13 +796,16 @@
         ones, twos = [], []
         for i in range(count):
             two_scratch, one_scratch, own = refs.some(2), refs.some(3), refs.one()
-            left, right = late_lefts[where[i]].vmem, late_rights[i].vmem
+            left = (late_normed if i else late_upstream).vmem
+            right = grads[i - 1] if i else late_attention[3].vmem
             ones.append(RingOne(net, left, right, 0, i % 2 == 0, own, one_scratch))
             twos.append(RingTwo(net, own, i % 2 == 0, new_refs[i], two_scratch))
-        every(late_lefts + late_rights, "start")
+        output_copy = net.load(late_output, image.vmem)
+        every([late_upstream, late_attention[3]] + late_attention[:3], "start")
+        every(late_weights + [late_normed], "start")
         net.greet(NEAR + ALL + [("zhi", 1)])
         acc_ref[...] = jnp.zeros_like(acc_ref)
-        x_ref, extra_ref = late_x.vmem, late_extra.vmem
+        x_ref, extra_ref = late_x.vmem, half
 
         def epilogue(at, total):
             row_grad, terms = norm_back(x_ref[at, :], gain_ref[...], total)
@@ -753,24 +815,46 @@
             acc_ref[8:16, :] += jnp.where(kept, 0.0, result)
             return jnp.where(kept, result, 0.0)
 
-        work = TensorSum(net, share_ref, epilogue, image.vmem, sum_scratch)
+        every(old, "begin")
+        every([late_upstream, late_attention[3]], "ref")
+        ones[0].begin()
+        output_copy.wait()
+        grad_mixed[...] = low(back_product(late_upstream.vmem[...], image.vmem[...]))
+        late_x.start()
+        text_rows = lambda z: pl.ds(pl.multiple_of(z * 128, 128), 128)
+        text_copy = net.load(text_ref.at[text_rows(net.z)], text_out)
+        query_ref, keys_ref, values_ref = [late.ref() for late in late_attention[:3]]
+        every(old, "relay")
+        for _, at, to in each_head(256, 256):
+            found = attend_backward(
+                query_ref[at], keys_ref[to], values_ref[to], None, grad_mixed[at]
+            )
+            for ref, value in zip(grads, found):
+                ref[at] = value
+        weight_refs = [late.ref() for late in late_weights]
+
+        def share(core, n):
+            block, total = pl.ds(n * 512, 512), 0.0
+            for ref, weight in zip(grads, weight_refs):
+                total = total + back_product(ref[own_rows(core), :], weight[block, :])
+            return total
+
+        work = TensorSum(net, share, epilogue, image.vmem, sum_scratch, half)
         work.begin()
-        every([late_x, late_extra], "start")
-        every(late_lefts + late_rights, "ref")
-        every(old, "begin")
-        every(ones, "begin")
+        late_normed.ref()
+        every(ones[1:], "begin")
         work.exchange()
-        every(old, "relay")
+        work.free_half()
+        extra_copy = net.load(extra_hbm, half)
         every(ones, "relay")
-        every([late_x, late_extra], "ref")
+        late_x.ref()
+        extra_copy.wait()
         work.work()
         got_small[0] = sums_ref[...]
         got_small[0, 0:1, :] = jnp.sum(acc_ref[0:8, :], axis=0, keepdims=True)
         got_small[0, 3:4, :] = jnp.sum(acc_ref[8:16, :], axis=0, keepdims=True)
         by_core = net.push(got_small.at[0], got_small.at[1], "core")
-        text_copy = net.push(
-            text_ref.at[pl.ds(pl.multiple_of((1 - net.z) * 128, 128), 128)], got_text, "zhi"
-        )
+        text_push = net.push(text_ref.at[text_rows(1 - net.z)], got_text, "zhi")
         work.finish()
         net.store(image)
         by_core.wait()
@@ -792,15 +876,15 @@
         by_z = net.push(got_small.at[0], got_small.at[8], "zhi")
         every(twos, "third")
         text_copy.wait()
-        mine_text = text_ref[pl.ds(pl.multiple_of(net.z * 128, 128), 128), :]
-        text_out[...] = mine_text + got_text[...]
+        text_push.wait()
+        text_out[...] += got_text[...]
         by_z.wait()
         small_ref[...] = got_small[0] + got_small[8]
         every(twos, "finish")
         every(ones, "done")
 
     copies = TensorSum.COPIES + 9 + (len(owns) + count) * RingTwo.COPIES + count * RingOne.COPIES
-    loads = TensorSum.LOADS + len(owns) * RingTwo.LOADS
+    loads = 3 + len(owns) * RingTwo.LOADS
     return call(body, ins, outs, scratch, copies, loads, 4, "backward_last")
 
 
@@ -842,30 +926,24 @@
     hidden = masked.reshape(count, 1) == 1
     start = jnp.where(hidden, mask_token[None, :], image.reshape(count, width).astype(F32))
     normed_one = low(layer_norm(start, first_gain))
-    query = split(low(product(normed_one, self_query)))
-    keys = split(low(product(normed_one, self_key)))
-    values = split(low(product(normed_one, self_value)))
-    self_mixed, self_total = attend_forward(query, keys, values, None)
-    self_rows = flat(self_mixed)
+    weights = (self_query, self_key, self_value, self_output)
     start_own = own(start)
-    first, normed_two, text_columns, cross_keys, cross_values = forward_self(
-        product(self_rows, self_output),
-        start_own,
-        gains[1],
-        text_blocks,
-        text_rows,
-        text_key,
-        text_value,
+    first, normed_two, text_columns, cross_keys, cross_values, *attention = forward_self(
+        normed_one, weights, start_own, gains[1], text_blocks, text_rows, text_key, text_value
     )
-    cross_keys, cross_values = split(cross_keys), split(cross_values)
     text_columns = low(text_columns.reshape(-1, text_columns.shape[-1]))
 
-    cross_query = split(low(product(normed_two, text_query)))
-    present = jnp.arange(words)[None, :] < text_len[:, None]
-    cross_mixed, cross_total = attend_forward(cross_query, cross_keys, cross_values, present)
-    cross_rows = flat(cross_mixed)
-    second, normed_three, grad_active = forward_cross(
-        product(cross_rows, text_output), first, gains[2], upstream, contract
+    present = (jnp.arange(words)[None, :] < text_len[:, None]).astype(F32)
+    second, normed_three, grad_active, cross_query, cross_rows = forward_cross(
+        normed_two,
+        (text_query, text_output),
+        cross_keys,
+        cross_values,
+        present,
+        first,
+        gains[2],
+        upstream,
+        contract,
     )
 
     raised = product(normed_three, expand)
@@ -883,8 +961,9 @@
     )
 
     grad_mixed = split(low(back_product(cross_out_grad, text_output)))
-    grad_q, grad_k, grad_v = attend_backward(
-        cross_query, cross_keys, cross_values, present, cross_total, grad_mixed
+    over = jax.vmap(jax.vmap(attend_backward, (1, 1, 1, None, 1), 1), (0, 0, 0, 0, 0))
+    grad_q, grad_k, grad_v = over(
+        split(cross_query), split(cross_keys), split(cross_values), present[:, None, :], grad_mixed
     )
     grad_cq = flat(grad_q)
     text_kv = jnp.concatenate([flat(grad_k), flat(grad_v)], axis=1).astype(F32)
@@ -903,31 +982,19 @@
     gathered = low(gathered.reshape(-1, gathered.shape[-1]))
     text_grads = outer_sum(text_columns, gathered)
 
-    grad_mixed = split(low(back_product(self_out_grad, self_output)))
-    grad_q, grad_k, grad_v = map(
-        flat, attend_backward(query, keys, values, None, self_total, grad_mixed)
-    )
-    shares = (
-        back_product(grad_q, self_query)
-        + back_product(grad_k, self_key)
-        + back_product(grad_v, self_value)
-    )
     sums = jnp.zeros((8, width), F32)
     sums = sums.at[1].set(jnp.sum(second_sum, axis=0)).at[2].set(jnp.sum(third_sum, axis=0))
     keep = 1.0 - own(masked.reshape(count, 1)).astype(F32)
     image_grad, small, text_grads, *rest = backward_last(
-        shares,
+        attention,
+        weights,
+        self_out_grad,
+        normed_one,
         start_own,
         gains[0],
         grad_first,
         keep,
         owns,
-        [
-            (self_out_grad, self_rows),
-            (normed_one, grad_q),
-            (normed_one, grad_k),
-            (normed_one, grad_v),
-        ],
         text_grads,
         sums,
     )

time: 616 us -> 567 us (0.920)
  matrix products: 74.3 us -> 37.1 us
  local copies, waits for them, and re-layouts: 38 us -> 15.8 us
  Pallas kernels: 479 us -> 486 us
    dot_general x7 -> x2, matrix products: 32.3 us -> 13.9 us  [product(): return jnp.dot(left, right, preferred_element_type=F32)]
    dot_general x7 -> x5, matrix products: 30.3 us -> 18.6 us  [back_product(): lax.dot_general(left, right, (((1,), (1,)), ((), ())), preferred_element_...]
    unnamed x100 -> x61, local copies, waits for them, and re-layouts: 17.6 us -> 7.71 us
    dot_general x12 -> x0, matrix products: 8.48 us -> none  [the longest x2 4.05 us: attend_forward(): jnp.einsum('bhqk,bkhd->bqhd', weights_low, values, preferred_element_type...]
    pallas_call x5, Pallas kernels: 479 us -> 486 us  [call(): pl.pallas_call(kernel, name=name, out_shape=[o for o, _ in outs], in_spec...]
    reshape x11 -> x4, local copies, waits for them, and re-layouts: 7.25 us -> 1.07 us  [shards(): split = lambda rows: rows.reshape(items, -1, heads, HEAD)]
where the time goes in v5:
time: 567 us; the launch traced here: 559 us
  Pallas kernels  486 us (86%)
  matrix products  37.1 us (7%)
  other arithmetic  18.5 us (3%)
  local copies, waits for them, and re-layouts  15.8 us (3%)
    pallas_call x5, Pallas kernels, call(): pl.pallas_call(kernel, name=name, out_shape=[o for o, _ in outs], in_spec...  486 us
    dot_general x5, matrix products, back_product(): lax.dot_general(left, right, (((1,), (1,)), ((), ())), preferred_element_...  18.6 us
    dot_general x2, matrix products, product(): return jnp.dot(left, right, preferred_element_type=F32)  13.9 us

profile of v5, /device:TPU:0, one launch (start us, length us, event | category | flops | bytes accessed | tf_op | source)
XLA Modules:
  0.0 559.4 jit_solution(2681112519839556228)
XLA Ops:
  0.6 0.0 copy-start
  0.7 0.0 copy-start.18
  0.7 0.0 copy-start.20
  0.7 0.8 broadcast_compare_fusion
  1.5 2.2 select_reduce_fusion
  3.7 2.4 multiply_reduce_fusion
  6.2 0.0 copy-done
  6.2 0.0 copy-done.18
  6.2 0.0 copy-done.20
  6.2 3.9 bitcast_select_fusion
  10.1 1.5 constant_dynamic-slice_fusion.1.refs_5_.refs_10_
  11.7 0.0 copy-done.7
  11.7 0.4 reshape.233
  12.1 1.1 copy.89
  13.2 65.4 %forward_self.1 = (f32[256,2048]{1,0:T(8,128)}, bf16[512,2048]{1,0:T(8,128)(2,1)}, f32[4,4,32,256]{3,2,1,0:T(8,128)}, bf16[32,512]{1,0:T(8,128)(2,1)}, bf16[32,5...) custom-call(bf16[512,2048]{1,0:T(8,128)(2,1)} %get-tuple-element.143, ...), custom_call_target="tpu_custom_call" | custom-call | tf_op jit(solution)/shard_map/forward_self/pallas_call | solution.py:418
  78.7 0.6 broadcast_compare_fusion.1
  79.3 58.5 %forward_cross.1 = (f32[256,2048]{1,0:T(8,128)}, bf16[512,2048]{1,0:T(8,128)(2,1)}, f32[512,2048]{1,0:T(8,128)}, bf16[512,512]{1,0:T(8,128)(2,1)}, bf16[512,512]{1,0:T(8,128)(2,1)}) custom-call(bf16[512,2048]{1,0:T(8,128)(2,1)} %get-tuple-element.90.refs_0_.refs_14_, bf16[2048,512]{1,0:T(8,128)(2,1)} %refs_1_.3, bf16[512,2048]{1,0:T(8,128)(2,1)} %refs_2_.3, ...), custom_call_target="tpu_custom_call" | custom-call | tf_op jit(solution)/shard_map/forward_cross/pallas_call | solution.py:418
  137.8 13.6 %multiply_convert_fusion = (bf16[512,2048]{1,0:T(8,128)(2,1)}, bf16[512,2048]{1,0:T(8,128)(2,1)S(1)}) fusion(f32[512,2048]{1,0:T(8,128)} %get-tuple-element.95, bf16[512,2048]{1,0:T(8,128)(2,1)} %get-tuple-element.96.refs_10_, bf16[2048,2048]{1,0:T(8,128)(2,1)} %param.36), kind=kOutput, calls=%fused_computation.11 | convolution fusion | flops 4318035968 | bytes 18874368 | tf_op jit(solution)/shard_map/dot_general | solution.py:19
  151.4 10.8 %fusion.31.refs_0_ = f32[512,2048]{1,0:T(8,128)} fusion(bf16[512,2048]{1,0:T(8,128)(2,1)S(1)} %get-tuple-element.141.refs_11_, bf16[2048,2048]{1,0:T(8,128)(2,1)} %param.36), kind=kOutput, calls=%fused_computation.67 | convolution fusion | flops 4294967296 | bytes 14680064 | tf_op jit(solution)/shard_map/dot_general | solution.py:27
  162.3 1.6 dynamic-slice_convert_fusion.refs_3_
  163.8 78.6 %backward_first.1 = (f32[256,2048]{1,0:T(8,128)}, bf16[512,2048]{1,0:T(8,128)(2,1)}, f32[8,2048]{1,0:T(8,128)}, f32[512,2048]{1,0:T(8,128)}, f32[4,128,512]{2,1,...) custom-call(f32[512,2048]{1,0:T(8,128)} %fusion.31.refs_0_, ...), custom_call_target="tpu_custom_call" | custom-call | tf_op jit(solution)/shard_map/backward_first/pallas_call | solution.py:418
  242.5 2.9 convolution_convert_fusion
  245.4 0.0 copy-start.2
  245.4 0.9 reshape.222
  246.3 0.1 reshape.220
  246.5 0.2 fusion.11
  246.7 0.9 fusion.30
  247.6 1.3 multiply_reduce_fusion.1
  249.0 0.2 fusion.14
  249.2 1.3 fusion.15
  250.5 0.7 maximum_convert_fusion.refs_4_
  251.2 0.4 fusion.9
  251.5 0.4 copy.51
  252.0 3.3 fusion.28.refs_0_
  255.2 0.9 copy.88
  256.1 152.0 %backward_second.1 = (f32[256,2048]{1,0:T(8,128)}, bf16[512,2048]{1,0:T(8,128)(2,1)}, f32[8,2048]{1,0:T(8,128)}, f32[4,4,32,1024]{3,2,1,0:T(8,128)}, bf16[512,20...) custom-call(f32[512,2048]{1,0:T(8,128)} %fusion.28.refs_0_, ...), custom_call_target="tpu_custom_call" | custom-call | tf_op jit(solution)/shard_map/backward_second/pallas_call | solution.py:418
  408.1 0.0 copy-start.21
  408.1 1.9 maximum_bitcast_fusion
  410.1 0.9 reduce_sum.58
  411.0 0.2 scatter.9.refs_15_
  411.2 0.0 copy-start.9
  411.2 0.0 copy-done.23
  411.2 3.2 convolution_bitcast_fusion.refs_14_
  414.4 0.1 copy.64
  414.5 0.7 convert_subtract_fusion.refs_13_
  415.2 131.9 %backward_last.1 = (bf16[512,2048]{1,0:T(8,128)(2,1)}, f32[8,2048]{1,0:T(8,128)}, f32[128,1024]{1,0:T(8,128)}, f32[64,512]{1,0:T(8,128)}, f32[64,512]{1,0:T(8,12...) custom-call(bf16[512,512]{1,0:T(8,128)(2,1)} %get-tuple-element.107., ...), custom_call_target="tpu_custom_call" | custom-call | tf_op jit(solution)/shard_map/backward_last/pallas_call | solution.py:418
  547.1 1.9 pad_maximum_fusion
  549.1 1.9 fusion.29
  550.9 0.9 constant_dynamic-slice_fusion
  551.8 0.5 slice_bitcast_fusion
  552.3 0.0 copy-done.5
  552.3 0.0 copy-start.15
  552.3 0.0 copy-start.14
  552.4 0.0 copy-start.13
  552.4 0.0 copy-start.12
  552.4 1.3 copy.99
  553.7 1.3 copy.100
  555.0 0.7 copy.101
  555.7 0.7 copy.102
  556.3 0.7 copy.103
  557.0 0.7 copy.104
  557.7 0.7 copy.105
  558.3 0.0 copy-done.12
  558.3 0.7 copy.106
  (45 shorter events, 0.3 us)
Async XLA Ops:
  0.6 5.5 copy-start
  0.7 5.5 copy-start.18
  0.7 5.5 copy-start.20
  10.1 1.5 copy-start.7
  13.2 65.5 %copy-start.22 = (s32[2]{0:T(128)S(1)}, s32[2]{0:T(128)}, u32[]{:S(2)}) copy-start(s32[2]{0:T(128)} %param.26) | copy-start | bytes 28
  151.4 10.8 %copy-start.4 = (bf16[512,2048]{1,0:T(8,128)(2,1)}, bf16[512,2048]{1,0:T(8,128)(2,1)S(1)}, u32[]{:S(2)}) copy-start(bf16[512,2048]{1,0:T(8,128)(2,1)S(1)} %get-tuple-element.141.refs_11_) | copy-start | bytes 6291460
  151.4 10.8 %copy-start.1 = (bf16[2,256,2048]{2,1,0:T(8,128)(2,1)S(1)}, bf16[2,256,2048]{2,1,0:T(8,128)(2,1)}, u32[]{:S(2)}) copy-start(bf16[2,256,2048]{2,1,0:T(8,128)(2,1)} %param.27) | copy-start | bytes 6291460
  163.8 78.6 %copy-start.3 = (bf16[512,2048]{1,0:T(8,128)(2,1)S(1)}, bf16[512,2048]{1,0:T(8,128)(2,1)}, u32[]{:S(2)}) copy-start(bf16[512,2048]{1,0:T(8,128)(2,1)} %refs_2_.3) | copy-start | bytes 6291460
  242.4 3.9 copy-start.8
  242.5 4.0 copy-start.11
  242.5 5.1 copy-start.10
  245.4 6.5 %copy-start.2 = (bf16[2048,512]{1,0:T(8,128)(2,1)S(1)}, bf16[2048,512]{1,0:T(8,128)(2,1)}, u32[]{:S(2)}) copy-start(bf16[2048,512]{1,0:T(8,128)(2,1)} %refs_1_.3) | copy-start | bytes 6291460
  256.1 154.8 %copy-start.19 = (f32[8,2048]{1,0:T(8,128)S(1)}, f32[8,2048]{1,0:T(8,128)}, u32[]{:S(2)}) copy-start(f32[8,2048]{1,0:T(8,128)} %get-tuple-element.116) | copy-start | bytes 196612
  256.1 155.1 %copy-start.23 = (f32[4,4,32,256]{3,2,1,0:T(8,128)S(1)}, f32[4,4,32,256]{3,2,1,0:T(8,128)}, u32[]{:S(2)}) copy-start(f32[4,4,32,256]{3,2,1,0:T(8,128)} %get-tuple-element.113) | copy-start | bytes 1572868
  408.1 6.2 %copy-start.21 = (s32[2,256]{1,0:T(2,128)S(1)}, s32[2,256]{1,0:T(2,128)}, u32[]{:S(2)}) copy-start(s32[2,256]{1,0:T(2,128)} %param.25) | copy-start | bytes 6148
  411.2 4.0 copy-start.9
  415.2 137.1 %copy-start.5 = (bf16[512,2048]{1,0:T(8,128)(2,1)S(1)}, bf16[512,2048]{1,0:T(8,128)(2,1)}, u32[]{:S(2)}) copy-start(bf16[512,2048]{1,0:T(8,128)(2,1)} %get-tuple-element.106) | copy-start | bytes 6291460
  550.9 2.8 copy-start.6
  552.3 2.7 copy-start.17
  552.3 3.3 copy-start.16
  552.3 4.0 copy-start.15
  552.3 4.7 copy-start.14
  552.4 5.3 copy-start.13
  552.4 5.9 %copy-start.12 = (f32[64,512]{1,0:T(8,128)S(1)}, f32[64,512]{1,0:T(8,128)}, u32[]{:S(2)}) copy-start(f32[64,512]{1,0:T(8,128)} %get-tuple-element.130) | copy-start | bytes 393220

commit v6 on v5

--- a/solution.py
+++ b/solution.py
@@ -532,19 +532,21 @@
     return call(body, ins, outs, scratch, copies, loads, 0, "forward_self")
 
 
-def forward_cross(normed, weights, keys, values, present, rows, gain, upstream, contract):
+def forward_cross(normed, weights, keys, values, present, rows, gain, upstream, contract, expand):
     ins = [(normed, "load")] + [(weight, "load") for weight in weights]
     ins += [(keys, "vmem"), (values, "vmem"), (present, "vmem")]
     ins += [(rows, "load"), (gain, "vmem"), (upstream, "load"), (contract, "load")]
+    ins += [(expand, "load")]
     outs = [(shape(256, 2048), "store"), (shape(512, 2048, kind=BF16), "store")]
-    outs += [(shape(512, 2048), "store")] + [(shape(512, 512, kind=BF16), "store")] * 2
-    scratch = list(TensorSum.SCRATCH + TensorSum.HALF)
+    outs += [(shape(512, 2048, kind=BF16), "store")] * 2
+    outs += [(shape(512, 512, kind=BF16), "store")] * 2
+    scratch = list(TensorSum.SCRATCH + TensorSum.HALF) + [((512, 2048), F32)]
 
     def body(net, in_refs, out_refs, refs):
         late_normed, late_query, late_output = in_refs.some(3)
         keys_ref, values_ref, present_ref = in_refs.some(3)
-        late_rows, gain_ref, late_upstream, late_contract = in_refs.some(4)
-        total, normed, grad, query, mixed = out_refs.some(5)
+        late_rows, gain_ref, late_upstream, late_contract, late_expand = in_refs.some(5)
+        total, normed, active, grad_raised, query, mixed = out_refs.some(6)
         every([late_normed, late_query, late_output], "start")
         net.greet(NEAR)
         query_ref, mixed_ref = query.vmem, mixed.vmem
@@ -566,38 +568,58 @@
             return layer_norm(value, gain_ref[...])
 
         work = TensorSum(net, share, epilogue, normed.vmem, refs.some(4), refs.one())
+        grad_ref = refs.one()
         work.begin()
-        every([late_upstream, late_contract, late_rows], "start")
+        every([late_upstream, late_contract, late_rows, late_expand], "start")
         work.exchange()
         upstream_ref, contract_ref = late_upstream.ref(), late_contract.ref()
 
         def part(at):
-            grad.vmem[:, at] = back_product(upstream_ref[...], contract_ref[at, :])
+            grad_ref[:, at] = back_product(upstream_ref[...], contract_ref[at, :])
 
         blocks(8, 256, part)
-        net.store(grad)
         late_rows.ref()
+        expand_ref = late_expand.ref()
+
+        def hidden(core):
+            rows = own_rows(core)
+
+            def part(at):
+                raised = product(normed.vmem[rows, :], expand_ref[:, at])
+                inner = raised * (0.7978845608028654 + 0.035677408136300125 * raised * raised)
+                bend = jnp.tanh(inner)
+                active.vmem[rows, at] = low(0.5 * raised * (1.0 + bend))
+                slope = 0.7978845608028654 + 0.10703222440890037 * raised * raised
+                slope = 0.5 * (1.0 + bend) + 0.5 * raised * (1.0 - bend * bend) * slope
+                grad_raised.vmem[rows, at] = low(grad_ref[rows, at] * slope)
+
+            blocks(8, 256, part)
+
         work.work()
         net.store(total)
+        hidden(net.core)
         work.finish()
         net.store(normed)
+        hidden(1 - net.core)
+        net.store(active)
+        net.store(grad_raised)
 
     return call(
         body, ins, outs, scratch, TensorSum.COPIES, TensorSum.LOADS, 1, "forward_cross"
     )
 
 
-def norm_back_sum(net, share_ref, x_ref, gain_ref, extra_ref, rows_ref, low_ref, gain_sum, scratch):
+def norm_back_sum(net, share, x_ref, gain_ref, rows_ref, low_ref, gain_sum, scratch, half):
     gain_sum[...] = jnp.zeros_like(gain_sum)
 
     def epilogue(at, total):
         row_grad, terms = norm_back(x_ref[at, :], gain_ref[...], total)
         gain_sum[...] += terms
-        result = extra_ref[at, :] + row_grad
+        result = rows_ref[at, :] + row_grad
         rows_ref[at, :] = result
         return result
 
-    return TensorSum(net, share_ref, epilogue, low_ref, scratch)
+    return TensorSum(net, share, epilogue, low_ref, scratch, half)
 
 
 def every(parts, step):
@@ -605,34 +627,42 @@
         getattr(part, step)()
 
 
-def backward_first(share, x_rows, gain, extra, left, right, contract):
-    ins = [(share, "hbm"), (x_rows, "load"), (gain, "vmem"), (extra, "load"), (left, "load")]
+def backward_first(grad_raised, expand, x_rows, gain, extra, left, right, contract):
+    ins = [(grad_raised, "load"), (expand, "load"), (x_rows, "load"), (gain, "vmem")]
+    ins += [(extra, "hbm"), (left, "load")]
     ins += [(right, "load"), (contract, "load")]
-    outs = [(shape(256, 2048), "store"), (shape(512, 2048, kind=BF16), "store")]
+    outs = [(shape(256, 2048), "hbm"), (shape(512, 2048, kind=BF16), "store")]
     outs += [(shape(8, 2048), "vmem"), (shape(512, 2048), "store")]
     outs += [(shape(4, 128, JOB), "store")] * 4
-    scratch = list(TensorSum.SCRATCH) + list(RingOne.SCRATCH) * 4
+    scratch = list(TensorSum.SCRATCH + TensorSum.HALF) + list(RingOne.SCRATCH) * 4
 
     def body(net, in_refs, out_refs, refs):
-        share_ref, late_x, gain_ref, late_extra, late_left, late_right = in_refs.some(6)
+        late_raised, late_expand, late_x, gain_ref = in_refs.some(4)
+        extra_hbm, late_left, late_right = in_refs.some(3)
         late_contract = in_refs.one()
         rows, lows, gain_sum, out_share, *owns = out_refs.some(8)
-        sum_scratch = refs.some(4)
+        sum_scratch, half = refs.some(4), refs.one()
         rings = [
             RingOne(net, late_left.vmem, late_right.vmem, i, i % 2 == 0, owns[i].vmem, refs.some(3))
             for i in range(4)
         ]
-        every([late_left, late_right], "start")
+        every([late_left, late_right, late_raised, late_expand], "start")
         net.greet(NEAR + RING)
-        x_ref = late_x.vmem
+        x_ref, raised_ref, expand_ref = late_x.vmem, late_raised.vmem, late_expand.vmem
+        share = lambda core, n: back_product(
+            raised_ref[own_rows(core), :], expand_ref[pl.ds(n * 512, 512), :]
+        )
         work = norm_back_sum(
-            net, share_ref, x_ref, gain_ref, late_extra.vmem, rows.vmem, lows.vmem, gain_sum, sum_scratch
+            net, share, x_ref, gain_ref, half, lows.vmem, gain_sum, sum_scratch, half
         )
-        work.begin()
-        every([late_contract, late_x, late_extra], "start")
         late_left.ref(), late_right.ref()
         every(rings, "begin")
+        late_raised.ref(), late_expand.ref()
+        work.begin()
+        every([late_contract, late_x], "start")
         work.exchange()
+        work.free_half()
+        extra_copy = net.load(extra_hbm, half)
         every(rings, "relay")
         right_ref, contract_ref = late_right.ref(), late_contract.ref()
 
@@ -640,7 +670,7 @@
             out_share.vmem[:, at] = product(right_ref[...], contract_ref[:, at])
 
         blocks(8, 256, part)
-        late_x.ref(), late_extra.ref()
+        late_x.ref()
         joins = jnp.where(net.tensor < 2, 1.0, 0.0)
 
         def join(i, carry):
@@ -651,8 +681,9 @@
 
         lax.fori_loop(0, 16, join, 0)
         net.store(out_share)
+        extra_copy.wait()
         work.work()
-        net.store(rows)
+        net.stores.append(net.load(half, rows))
         work.finish()
         net.store(lows)
         for ring, own in zip(rings, owns):
@@ -660,56 +691,66 @@
             net.store(own)
         every(rings, "done")
 
-    copies, loads = TensorSum.COPIES + 4 * RingOne.COPIES, TensorSum.LOADS
+    copies, loads = TensorSum.COPIES + 4 * RingOne.COPIES, 2
     return call(body, ins, outs, scratch, copies, loads, 2, "backward_first")
 
 
-def backward_second(share, x_rows, gain, extra, owns, wide, narrow, text, out_share):
-    pairs = [wide] + narrow
-    ones = [(0, i, i % 2 == 0) for i in range(4)]
-    ones += [(1 + i, 0, i % 2 == 0) for i in range(len(narrow))]
-    ins = [(share, "hbm"), (x_rows, "load"), (gain, "vmem"), (extra, "load"), (text, "hbm")]
-    ins += [(out_share, "hbm")] + [(own, "hbm") for own in owns]
-    ins += [(array, "load") for pair in pairs for array in pair]
-    outs = [(shape(256, 2048), "store"), (shape(512, 2048, kind=BF16), "store")]
-    outs += [(shape(8, 2048), "vmem"), (shape(4, 4, 32, 1024), "vmem")]
+def backward_second(
+    attention, weights, present, x_rows, gain, extra, owns, wide, upstream, mixed, normed, out_share
+):
+    ones = [(0, i, i % 2 == 0) for i in range(4)] + [(1, 0, True), (2, 0, False)]
+    query, keys, values = attention
+    ins = [(query, "load"), (keys, "vmem"), (values, "vmem"), (present, "vmem")]
+    ins += [(weights[0], "load"), (weights[1], "hbm"), (x_rows, "load"), (gain, "vmem")]
+    ins += [(extra, "hbm"), (out_share, "hbm")] + [(own, "hbm") for own in owns]
+    ins += [(array, "load") for array in (*wide, upstream, mixed, normed)]
+    outs = [(shape(256, 2048), "hbm"), (shape(512, 2048, kind=BF16), "store")]
+    outs += [(shape(8, 2048), "vmem")] + [(shape(4, 4, 32, 512), "vmem")] * 2
     outs += [(shape(512, 2048, kind=BF16), "hbm")]
     outs += [(shape(64, JOB), "vmem")] * len(owns)
     outs += [(shape(4, 128, JOB), "store")] * len(ones)
-    scratch = list(TensorSum.SCRATCH) + [TensorSum.SCRATCH[0]]
+    scratch = list(TensorSum.SCRATCH + TensorSum.HALF) + [TensorSum.SCRATCH[0]]
+    scratch += [((512, 512), BF16)]
     scratch += list(RingTwo.SCRATCH + RingTwo.PARTS) * len(owns)
     scratch += list(RingOne.SCRATCH) * len(ones)
 
     def body(net, in_refs, out_refs, refs):
-        share_ref, late_x, gain_ref, late_extra, text_ref, out_share_ref = in_refs.some(6)
-        own_refs, late_pairs = in_refs.some(len(owns)), [in_refs.some(2) for _ in pairs]
-        rows, lows, gain_sum, all_ref, layer_out = out_refs.some(5)
+        late_cross, keys_ref, values_ref, present_ref = in_refs.some(4)
+        late_weight, output_hbm, late_x, gain_ref, extra_hbm, out_share_ref = in_refs.some(6)
+        own_refs, late_wide, late_narrow = in_refs.some(len(owns)), in_refs.some(2), in_refs.some(3)
+        rows, lows, gain_sum, keys_all, values_all, layer_out = out_refs.some(6)
         final_refs, nexts = out_refs.some(len(owns)), out_refs.some(len(ones))
         mine, got_core, got_z, got_rows = refs.some(4)
-        got_z_two = refs.one()
+        half, got_z_two, grad_mixed = refs.some(3)
+        grad_cross = late_cross.vmem
         twos = [
             RingTwo(net, own, i % 2 == 0, final_refs[i], refs.some(2), refs.one())
             for i, own in enumerate(own_refs)
         ]
+        pairs = [[late.vmem for late in late_wide], [late.vmem for late in late_narrow[:2]]]
+        pairs.append([late_narrow[2].vmem, grad_cross])
         rings = [
-            RingOne(
-                net, *[late.vmem for late in late_pairs[p]], c, x_first, nexts[i].vmem, refs.some(3)
-            )
+            RingOne(net, *pairs[p], c, x_first, nexts[i].vmem, refs.some(3))
             for i, (p, c, x_first) in enumerate(ones)
         ]
-        for pair in late_pairs:
-            every(pair, "start")
+        every(late_wide + late_narrow[:2], "start")
+        output_copy = net.load(output_hbm, lows.vmem)
+        every([late_cross, late_weight, late_narrow[2], late_x], "start")
         net.greet(NEAR + ALL + [("zhi", 1)])
+        weight_ref = late_weight.vmem
+        share = lambda core, n: back_product(
+            grad_cross[own_rows(core), :], weight_ref[pl.ds(n * 512, 512), :]
+        )
         work = norm_back_sum(
             net,
-            share_ref,
+            share,
             late_x.vmem,
             gain_ref,
-            late_extra.vmem,
-            rows.vmem,
+            half,
             lows.vmem,
             gain_sum,
             (mine, got_core, got_z, got_rows),
+            half,
         )
         layer = TensorSum(
             net,
@@ -718,24 +759,50 @@
             lows.vmem,
             (mine, got_core, got_z_two, got_rows),
         )
+        every(twos, "begin")
+        every(late_wide, "ref")
+        every(rings[:4], "begin")
+        every(late_narrow[:2], "ref")
+        output_copy.wait()
+        grad_mixed[...] = low(back_product(late_narrow[0].vmem[...], lows.vmem[...]))
+        query_ref = late_cross.ref()
+        for item, at, to in each_head(256, 16):
+            grad_query, grad_keys, grad_values = attend_backward(
+                query_ref[at],
+                keys_ref[to],
+                values_ref[to],
+                present_ref[pl.ds(item, 1), :],
+                grad_mixed[at],
+            )
+            grad_cross[at] = grad_query
+            keys_all[0, 0, to[0], to[1]] = grad_keys.astype(F32)
+            values_all[0, 0, to[0], to[1]] = grad_values.astype(F32)
+        late_weight.ref()
         work.begin()
-        kept = net.load(text_ref, all_ref.at[0, 0])
-        by_x = [net.push(text_ref, all_ref.at[0, k], "x", k) for k in (1, 2, 3)]
-        every([late_x, late_extra], "start")
-        for pair in late_pairs:
-            every(pair, "ref")
-        every(twos, "begin")
-        every(rings, "begin")
+        texts = [
+            net.push(ref.at[0, 0], ref.at[0, k], axis, k)
+            for ref, axis in ((keys_all, "x"), (values_all, "y"))
+            for k in (1, 2, 3)
+        ]
+        every(rings[4:5], "begin")
+        late_narrow[2].ref()
+        every(rings[5:], "begin")
         work.exchange()
+        work.free_half()
+        extra_copy = net.load(extra_hbm, half)
         every(twos, "relay")
         every(rings, "relay")
-        kept.wait()
-        for copy in by_x:
+        for copy in texts:
             copy.wait_recv()
-        by_y = [net.push(all_ref.at[0], all_ref.at[k], "y", k) for k in (1, 2, 3)]
-        every([late_x, late_extra], "ref")
+        texts += [
+            net.push(ref.at[0], ref.at[k], axis, k)
+            for ref, axis in ((keys_all, "y"), (values_all, "x"))
+            for k in (1, 2, 3)
+        ]
+        late_x.ref()
+        extra_copy.wait()
         work.work()
-        net.store(rows)
+        net.stores.append(net.load(half, rows))
         work.finish()
         net.release("core")
         lows_copy = net.load(lows.vmem, lows.hbm)
@@ -754,14 +821,14 @@
         for ring, own in zip(rings[2:4], nexts[2:4]):
             ring.close()
             net.store(own)
-        for copy in by_y:
+        for copy in texts[6:]:
             copy.wait_recv()
-        for copy in by_x + by_y:
+        for copy in texts:
             copy.wait_send()
         every(rings, "done")
 
-    copies = 2 * TensorSum.COPIES + 6 + len(owns) * RingTwo.COPIES + len(ones) * RingOne.COPIES
-    loads = 2 * TensorSum.LOADS + 2 + len(owns) * RingTwo.LOADS
+    copies = 2 * TensorSum.COPIES + 12 + len(owns) * RingTwo.COPIES + len(ones) * RingOne.COPIES
+    loads = TensorSum.LOADS + 5 + len(owns) * RingTwo.LOADS
     return call(body, ins, outs, scratch, copies, loads, 3, "backward_second")
 
 
@@ -913,9 +980,6 @@
     words = text.shape[1]
     count = items * length
     core = lax.axis_index("tensor") % 2
-    heads = self_query.shape[1] // HEAD
-    split = lambda rows: rows.reshape(items, -1, heads, HEAD)
-    flat = lambda value: value.reshape(-1, heads * HEAD)
     gains = [g.reshape(1, width) for g in (first_gain, second_gain, third_gain)]
     own = lambda rows: lax.dynamic_slice_in_dim(rows, core * length, length, axis=0)
 
@@ -934,7 +998,7 @@
     text_columns = low(text_columns.reshape(-1, text_columns.shape[-1]))
 
     present = (jnp.arange(words)[None, :] < text_len[:, None]).astype(F32)
-    second, normed_three, grad_active, cross_query, cross_rows = forward_cross(
+    second, normed_three, active, grad_raised, cross_query, cross_rows = forward_cross(
         normed_two,
         (text_query, text_output),
         cross_keys,
@@ -944,14 +1008,11 @@
         gains[2],
         upstream,
         contract,
+        expand,
     )
-
-    raised = product(normed_three, expand)
-    gelu, pull = jax.vjp(jax.nn.gelu, raised)
-    active = low(gelu)
-    grad_raised = low(pull(grad_active)[0])
     grad_second, cross_out_grad, third_sum, out_share, *owns = backward_first(
-        back_product(grad_raised, expand),
+        grad_raised,
+        expand,
         second,
         gains[2],
         own(upstream).astype(F32),
@@ -959,27 +1020,23 @@
         active,
         contract,
     )
-
-    grad_mixed = split(low(back_product(cross_out_grad, text_output)))
-    over = jax.vmap(jax.vmap(attend_backward, (1, 1, 1, None, 1), 1), (0, 0, 0, 0, 0))
-    grad_q, grad_k, grad_v = over(
-        split(cross_query), split(cross_keys), split(cross_values), present[:, None, :], grad_mixed
-    )
-    grad_cq = flat(grad_q)
-    text_kv = jnp.concatenate([flat(grad_k), flat(grad_v)], axis=1).astype(F32)
-    grad_first, self_out_grad, second_sum, gathered, layer_out, *rest = backward_second(
-        back_product(grad_cq, text_query),
+    grad_first, self_out_grad, second_sum, text_k, text_v, layer_out, *rest = backward_second(
+        (cross_query, cross_keys, cross_values),
+        (text_query, text_output),
+        present,
         first,
         gains[1],
         grad_second,
         owns,
         (normed_three, grad_raised),
-        [(cross_out_grad, cross_rows), (normed_two, grad_cq)],
-        text_kv,
+        cross_out_grad,
+        cross_rows,
+        normed_two,
         out_share,
     )
     contract_t, owns = rest[:4], rest[4:]
-    gathered = low(gathered.reshape(-1, gathered.shape[-1]))
+    text_v = text_v.transpose(1, 0, 2, 3)
+    gathered = low(jnp.concatenate([text_k, text_v], axis=3).reshape(text_columns.shape[0], -1))
     text_grads = outer_sum(text_columns, gathered)
 
     sums = jnp.zeros((8, width), F32)

time: 567 us -> 540 us (0.952)
  matrix products: 37.1 us -> 2.67 us
  Pallas kernels: 486 us -> 499 us
    dot_general x7 -> x0, matrix products: 32.5 us -> none  [the longest x5 18.6 us: back_product(): lax.dot_general(left, right, (((1,), (1,)), ((), ())), preferred_element_...]
    pallas_call x5, Pallas kernels: 486 us -> 499 us  [call(): pl.pallas_call(kernel, name=name, out_shape=[o for o, _ in outs], in_spec...]
where the time goes in v6:
time: 540 us; the launch traced here: 533 us
  Pallas kernels  499 us (92%)
  other arithmetic  15.2 us (3%)
  local copies, waits for them, and re-layouts  14.3 us (3%)
    pallas_call x5, Pallas kernels, call(): pl.pallas_call(kernel, name=name, out_shape=[o for o, _ in outs], in_spec...  499 us

profile of v6, /device:TPU:0, one launch (start us, length us, event | category | flops | bytes accessed | tf_op | source)
XLA Modules:
  0.0 532.5 jit_solution(408880367305515495)
XLA Ops:
  0.6 0.0 copy-start
  0.7 0.0 copy-start.16
  0.7 0.8 broadcast_compare_fusion
  1.5 0.0 copy-start.18
  1.5 2.2 select_reduce_fusion
  3.7 0.0 copy-done
  3.7 0.0 copy-done.16
  3.7 0.8 multiply_reduce_fusion
  4.6 0.0 copy-done.18
  4.6 3.9 bitcast_select_fusion
  8.5 1.5 constant_dynamic-slice_fusion.1.refs_5_.refs_10_
  10.1 0.0 copy-done.4
  10.1 0.4 reshape.190
  10.5 1.1 copy.55
  11.6 65.5 %forward_self.1 = (f32[256,2048]{1,0:T(8,128)}, bf16[512,2048]{1,0:T(8,128)(2,1)}, f32[4,4,32,256]{3,2,1,0:T(8,128)}, bf16[32,512]{1,0:T(8,128)(2,1)}, bf16[32,5...) custom-call(bf16[512,2048]{1,0:T(8,128)(2,1)} %get-tuple-element.145, ...), custom_call_target="tpu_custom_call" | custom-call | tf_op jit(solution)/shard_map/forward_self/pallas_call | solution.py:418
  77.1 0.0 copy-done.21
  77.1 0.6 compare_convert_fusion.refs_5_.refs_3_
  77.8 67.3 %forward_cross.1 = (f32[256,2048]{1,0:T(8,128)}, bf16[512,2048]{1,0:T(8,128)(2,1)}, bf16[512,2048]{1,0:T(8,128)(2,1)}, bf16[512,2048]{1,0:T(8,128)(2,1)}, bf16[5...) custom-call(bf16[512,2048]{1,0:T(8,128)(2,1)} %get-tuple-element.92.refs_0_.refs_18_, bf16[2048,512]{1,0:T(8,128)(2,1)} %refs_4_.4, ...), custom_call_target="tpu_custom_call" | custom-call | tf_op jit(solution)/shard_map/forward_cross/pallas_call | solution.py:418
  145.1 0.0 copy-done.1
  145.1 1.6 dynamic-slice_convert_fusion.refs_4_
  146.8 86.4 %backward_first.1 = (f32[256,2048]{1,0:T(8,128)}, bf16[512,2048]{1,0:T(8,128)(2,1)}, f32[8,2048]{1,0:T(8,128)}, f32[512,2048]{1,0:T(8,128)}, f32[4,128,512]{2,1,...) custom-call(bf16[512,2048]{1,0:T(8,128)(2,1)} %get-tuple-element.97.refs_0_.refs_15_, ...), custom_call_target="tpu_custom_call" | custom-call | tf_op jit(solution)/shard_map/backward_first/pallas_call | solution.py:418
  233.1 0.0 copy-start.17
  233.2 0.0 copy-start.20
  233.2 143.3 %backward_second.1 = (f32[256,2048]{1,0:T(8,128)}, bf16[512,2048]{1,0:T(8,128)(2,1)}, f32[8,2048]{1,0:T(8,128)}, f32[4,4,32,512]{3,2,1,0:T(8,128)}, f32[4,4,32,5...) custom-call(bf16[512,512]{1,0:T(8,128)(2,1)} %get-tuple-element.96.r, ...), custom_call_target="tpu_custom_call" | custom-call | tf_op jit(solution)/shard_map/backward_second/pallas_call | solution.py:418
  376.4 0.9 reduce_sum.38
  377.3 0.0 copy-done.17
  377.4 0.2 scatter.9.refs_15_
  377.6 0.0 copy-start.5
  377.6 1.3 convert_bitcast_fusion
  378.9 0.0 copy-done.20
  378.9 0.0 copy-start.19
  378.9 2.7 convolution_bitcast_fusion.refs_14_
  381.6 0.0 copy-done.5
  381.6 0.0 copy-done.19
  381.6 0.1 copy.45
  381.8 0.7 convert_subtract_fusion.refs_13_
  382.4 136.5 %backward_last.1 = (bf16[512,2048]{1,0:T(8,128)(2,1)}, f32[8,2048]{1,0:T(8,128)}, f32[128,1024]{1,0:T(8,128)}, f32[64,512]{1,0:T(8,128)}, f32[64,512]{1,0:T(8,12...) custom-call(bf16[512,512]{1,0:T(8,128)(2,1)} %get-tuple-element.110., ...), custom_call_target="tpu_custom_call" | custom-call | tf_op jit(solution)/shard_map/backward_last/pallas_call | solution.py:418
  519.0 0.0 copy-start.2
  519.0 0.0 copy-done.6
  519.0 0.0 copy-done.7
  519.0 0.0 copy-done.8
  519.0 0.0 copy-done.9
  519.0 2.3 pad_maximum_fusion.1
  521.3 1.9 fusion.3
  523.1 0.8 constant_dynamic-slice_fusion
  523.9 0.5 slice_bitcast_fusion
  524.4 0.0 copy-done.2
  524.4 1.3 copy.65
  525.8 1.0 copy-done.3
  526.8 0.0 copy-start.11
  526.8 0.0 copy-start.10
  526.8 1.3 copy.66
  528.1 0.0 copy-done.15
  528.1 0.7 copy.67
  528.8 0.0 copy-done.14
  528.8 0.7 copy.68
  529.4 0.0 copy-done.13
  529.5 0.7 copy.69
  530.1 0.0 copy-done.12
  530.1 0.7 copy.70
  530.8 0.0 copy-done.11
  530.8 0.7 copy.71
  531.4 0.0 copy-done.10
  531.4 0.7 copy.72
  (20 shorter events, 0.1 us)
Async XLA Ops:
  0.6 3.1 copy-start
  0.7 3.1 copy-start.16
  1.5 3.1 copy-start.18
  8.5 1.5 copy-start.4
  11.6 65.5 %copy-start.21 = (s32[2]{0:T(128)S(1)}, s32[2]{0:T(128)}, u32[]{:S(2)}) copy-start(s32[2]{0:T(128)} %param.26) | copy-start | bytes 28
  77.8 67.3 %copy-start.1 = (bf16[2,256,2048]{2,1,0:T(8,128)(2,1)S(1)}, bf16[2,256,2048]{2,1,0:T(8,128)(2,1)}, u32[]{:S(2)}) copy-start(bf16[2,256,2048]{2,1,0:T(8,128)(2,1)} %param.27) | copy-start | bytes 6291460
  233.1 144.2 %copy-start.17 = (f32[8,2048]{1,0:T(8,128)S(1)}, f32[8,2048]{1,0:T(8,128)}, u32[]{:S(2)}) copy-start(f32[8,2048]{1,0:T(8,128)} %get-tuple-element.120) | copy-start | bytes 196612
  233.2 145.7 %copy-start.20 = (f32[4,4,32,256]{3,2,1,0:T(8,128)S(1)}, f32[4,4,32,256]{3,2,1,0:T(8,128)}, u32[]{:S(2)}) copy-start(f32[4,4,32,256]{3,2,1,0:T(8,128)} %get-tuple-element.116) | copy-start | bytes 1572868
  377.6 4.0 copy-start.5
  378.9 2.7 copy-start.19
  382.4 136.5 %copy-start.6 = (f32[64,512]{1,0:T(8,128)S(1)}, f32[64,512]{1,0:T(8,128)}, u32[]{:S(2)}) copy-start(f32[64,512]{1,0:T(8,128)} %get-tuple-element.139) | copy-start | bytes 393220
  382.4 136.6 %copy-start.7 = (f32[64,512]{1,0:T(8,128)S(1)}, f32[64,512]{1,0:T(8,128)}, u32[]{:S(2)}) copy-start(f32[64,512]{1,0:T(8,128)} %get-tuple-element.140) | copy-start | bytes 393220
  382.4 136.6 %copy-start.8 = (f32[64,512]{1,0:T(8,128)S(1)}, f32[64,512]{1,0:T(8,128)}, u32[]{:S(2)}) copy-start(f32[64,512]{1,0:T(8,128)} %get-tuple-element.141) | copy-start | bytes 393220
  382.4 136.6 %copy-start.9 = (f32[64,512]{1,0:T(8,128)S(1)}, f32[64,512]{1,0:T(8,128)}, u32[]{:S(2)}) copy-start(f32[64,512]{1,0:T(8,128)} %get-tuple-element.142) | copy-start | bytes 393220
  519.0 5.5 %copy-start.2 = (bf16[512,2048]{1,0:T(8,128)(2,1)S(1)}, bf16[512,2048]{1,0:T(8,128)(2,1)}, u32[]{:S(2)}) copy-start(bf16[512,2048]{1,0:T(8,128)(2,1)} %get-tuple-element.109) | copy-start | bytes 6291460
  524.4 2.3 copy-start.3
  526.8 1.4 copy-start.15
  526.8 2.0 copy-start.14
  526.8 2.7 copy-start.13
  526.8 3.3 copy-start.12
  526.8 4.0 copy-start.11
  526.8 4.6 copy-start.10

commit v7 on v6

--- a/solution.py
+++ b/solution.py
@@ -294,6 +294,92 @@
         self.final.wait_recv()
         self.out[...] = self.got[5 - self.net.z] + self.got_last[...]
         for copy in self.far + self.near + self.last + [self.final]:
+            copy.wait_send()
+
+
+class RingHeads(RingOne):
+    WIDTH = 3 * HEAD
+    SCRATCH = (((2, 2, 128, WIDTH), F32),) * 3 + (((4, 128, WIDTH), F32),)
+    LAST = (((4, 128, WIDTH), F32), ((4, 64, WIDTH), F32))
+    COPIES_LAST = 4
+
+    def __init__(self, net, lefts, rights, out, scratch, last):
+        self.net, self.lefts, self.rights, self.out = net, lefts, rights, out
+        self.axis, self.one = "y", net.y
+        self.sending, self.got, self.beside, self.own = scratch
+        self.heads, self.got_last = last
+
+    def piece(self, step, half, target, add=False):
+        at, total = (self.one + step) % 4, 0.0
+        for left, right in zip(self.lefts, self.rights):
+            cut = lambda x: left[:, pl.ds(pl.multiple_of(x * 512 + at * 128, 128), 128)]
+            both = jnp.concatenate([cut(2 * half), cut(2 * half + 1)], axis=1)
+            total = total + outer_sum(both, right[...])
+        for j in range(2):
+            part = total[j * 128 : (j + 1) * 128]
+            if add:
+                part = part + target[j]
+            target[j] = part
+
+    def swap(self):
+        net = self.net
+        self.swaps = [
+            net.push(self.own.at[(net.x + k) % 4], self.heads.at[k], "x", k) for k in (1, 2, 3)
+        ]
+        self.heads[0] = self.own[net.x]
+
+    def third(self):
+        net = self.net
+        for copy in self.swaps:
+            copy.wait_recv()
+        rows = pl.ds(pl.multiple_of((1 - net.z) * 64, 64), 64)
+        self.final = net.push(self.heads.at[:, rows], self.got_last, "zhi")
+
+    def finish(self):
+        self.final.wait_recv()
+        rows = pl.ds(pl.multiple_of(self.net.z * 64, 64), 64)
+        for k in range(4):
+            self.out[(self.net.x + 4 - k) % 4] = self.heads[k, rows, :] + self.got_last[k]
+        for copy in self.swaps + [self.final]:
+            copy.wait_send()
+
+
+class Gather:
+    def __init__(self, net, source, steps, out, got, got_core):
+        self.net, self.out, self.got, self.got_core = net, out, got, got_core
+        self.slots = range(len(steps))
+        self.copies, self.handed = [], []
+        for j in range(4):
+            at = pl.ds(j * 128, 128)
+            self.copies.append(
+                [net.push(source.at[at], got.at[i, at], "x", step) for i, step in enumerate(steps)]
+            )
+
+    def hand(self, j):
+        at = pl.ds(j * 128, 128)
+        for i in self.slots:
+            self.copies[j][i].wait_recv()
+            self.handed.append(
+                self.net.push(self.got.at[i, at], self.got_core.at[i, at], "core")
+            )
+
+    def keep(self, source, core):
+        columns = pl.ds(pl.multiple_of(core * 1024, 1024), 1024)
+        for i in self.slots:
+
+            def body(n, carry, i=i):
+                at = pl.ds(pl.multiple_of(n * 16, 16), 16)
+                self.out[i, at, columns] = source[i, at, :].astype(BF16)
+                return carry
+
+            lax.fori_loop(0, 32, body, 0)
+
+    def finish(self):
+        self.keep(self.got, self.net.core)
+        for copy in self.handed:
+            copy.wait_recv()
+        self.keep(self.got_core, 1 - self.net.core)
+        for copy in [copy for step in self.copies for copy in step] + self.handed:
             copy.wait_send()
 
 
@@ -350,10 +436,12 @@
             add_rows(self.mine.at[j], self.got_core.at[j])
             self.over.append(self.net.push(self.mine.at[j], self.got_z.at[j], "zlo"))
 
-    def work(self):
+    def work(self, hook=None):
         net = self.net
         self.spread = []
         for j in self.steps:
+            if hook is not None:
+                hook(j)
             self.over[j].wait_recv()
 
             def body(i, carry, j=j):
@@ -461,25 +549,30 @@
     return pl.ds(pl.multiple_of(core * 256, 256), 256)
 
 
-def forward_self(normed, weights, rows, gain, text_blocks, text_rows, text_key, text_value):
-    ins = [(normed, "load")] + [(weight, "load") for weight in weights]
+def forward_self(
+    normed, columns, weights, rows, gain, text_blocks, text_rows, text_key, text_value
+):
+    ins = [(columns, "hbm"), (normed, "load")] + [(weight, "load") for weight in weights]
     ins += [(rows, "load"), (gain, "vmem"), (text_blocks, "hbm")]
     ins += [(text_rows, "load"), (text_key, "load"), (text_value, "load")]
     outs = [(shape(256, 2048), "store"), (shape(512, 2048, kind=BF16), "store")]
     outs += [(shape(4, 4, 32, 256), "vmem")] + [(shape(32, 512, kind=BF16), "vmem")] * 2
     outs += [(shape(512, 512, kind=BF16), "store")] * 4
+    outs += [(shape(2, 512, 2048, kind=BF16), "store")]
     scratch = list(TensorSum.SCRATCH + TensorSum.HALF) + [((4, 32, 1024), F32)]
+    scratch += [((2, 512, 1024), F32)] * 2
 
     def body(net, in_refs, out_refs, refs):
-        late_normed, late_weights = in_refs.one(), in_refs.some(4)
+        columns_hbm, late_normed, late_weights = in_refs.one(), in_refs.one(), in_refs.some(4)
         late_rows, gain_ref, text_ref, *late_text = in_refs.some(6)
         total, normed, columns_ref, *text_outs = out_refs.some(5)
-        attention = out_refs.some(4)
+        attention, beside = out_refs.some(4), out_refs.one()
         sum_scratch, half, got = refs.some(4), refs.one(), refs.one()
         every([late_normed] + late_weights, "start")
         net.greet(NEAR + ALL)
         own = net.load(text_ref.at[net.x], got.at[0])
         first = [net.push(text_ref.at[(net.x + k) % 4], got.at[k], "x", k) for k in (1, 2, 3)]
+        gather = Gather(net, columns_hbm, (1, -1), beside.vmem, refs.one(), refs.one())
         normed_in = late_normed.ref()
         for late, out in zip(late_weights[:3], attention):
             out.vmem[...] = low(product(normed_in[...], late.ref()[...]))
@@ -518,37 +611,43 @@
         for weight, out in zip(late_text[1:], text_outs):
             out[...] = low(product(text_rows_ref[...], weight.ref()[...]))
         late_rows.ref()
-        work.work()
+        work.work(gather.hand)
         net.store(total)
         work.finish()
         net.store(normed)
+        gather.finish()
+        net.store(beside)
         kept.wait()
         for copy in second:
             copy.wait_recv()
         for copy in first + second:
             copy.wait_send()
 
-    copies, loads = TensorSum.COPIES + 6, TensorSum.LOADS + 2
+    copies, loads = TensorSum.COPIES + 22, TensorSum.LOADS + 2
     return call(body, ins, outs, scratch, copies, loads, 0, "forward_self")
 
 
-def forward_cross(normed, weights, keys, values, present, rows, gain, upstream, contract, expand):
-    ins = [(normed, "load")] + [(weight, "load") for weight in weights]
+def forward_cross(
+    columns, normed, weights, keys, values, present, rows, gain, upstream, contract, expand
+):
+    ins = [(columns, "hbm"), (normed, "load")] + [(weight, "load") for weight in weights]
     ins += [(keys, "vmem"), (values, "vmem"), (present, "vmem")]
     ins += [(rows, "load"), (gain, "vmem"), (upstream, "load"), (contract, "load")]
     ins += [(expand, "load")]
     outs = [(shape(256, 2048), "store"), (shape(512, 2048, kind=BF16), "store")]
     outs += [(shape(512, 2048, kind=BF16), "store")] * 2
     outs += [(shape(512, 512, kind=BF16), "store")] * 2
+    outs += [(shape(1, 512, 2048, kind=BF16), "store")]
     scratch = list(TensorSum.SCRATCH + TensorSum.HALF) + [((512, 2048), F32)]
+    scratch += [((1, 512, 1024), F32)] * 2
 
     def body(net, in_refs, out_refs, refs):
-        late_normed, late_query, late_output = in_refs.some(3)
+        columns_hbm, late_normed, late_query, late_output = in_refs.some(4)
         keys_ref, values_ref, present_ref = in_refs.some(3)
         late_rows, gain_ref, late_upstream, late_contract, late_expand = in_refs.some(5)
-        total, normed, active, grad_raised, query, mixed = out_refs.some(6)
+        total, normed, active, grad_raised, query, mixed, beyond = out_refs.some(7)
         every([late_normed, late_query, late_output], "start")
-        net.greet(NEAR)
+        net.greet(NEAR + [("x", 2)])
         query_ref, mixed_ref = query.vmem, mixed.vmem
         query_ref[...] = low(product(late_normed.ref()[...], late_query.ref()[...]))
         for item, at, to in each_head(256, 16):
@@ -569,6 +668,7 @@
 
         work = TensorSum(net, share, epilogue, normed.vmem, refs.some(4), refs.one())
         grad_ref = refs.one()
+        gather = Gather(net, columns_hbm, (2,), beyond.vmem, refs.one(), refs.one())
         work.begin()
         every([late_upstream, late_contract, late_rows, late_expand], "start")
         work.exchange()
@@ -595,17 +695,19 @@
 
             blocks(8, 256, part)
 
-        work.work()
+        work.work(gather.hand)
         net.store(total)
         hidden(net.core)
         work.finish()
         net.store(normed)
         hidden(1 - net.core)
         net.store(active)
+        gather.finish()
+        net.store(beyond)
         net.store(grad_raised)
 
     return call(
-        body, ins, outs, scratch, TensorSum.COPIES, TensorSum.LOADS, 1, "forward_cross"
+        body, ins, outs, scratch, TensorSum.COPIES + 8, TensorSum.LOADS, 1, "forward_cross"
     )
 
 
@@ -833,28 +935,34 @@
 
 
 def backward_last(
-    attention, weights, upstream, normed, x_rows, gain, extra, keep, owns, text_grad, sums
+    attention, weights, upstream, normed, beside, beyond, x_rows, gain, extra, keep, owns, text_grad, sums
 ):
-    count = 4
+    count = 1
     ins = [(array, "load") for array in attention] + [(weights[3], "hbm")]
-    ins += [(weight, "load") for weight in weights[:3]]
-    ins += [(upstream, "load"), (normed, "load"), (x_rows, "load"), (gain, "vmem"), (extra, "hbm"), (keep, "vmem")]
+    ins += [(weight, "hbm") for weight in weights[:3]]
+    ins += [(upstream, "load"), (normed, "load"), (beside, "hbm"), (beyond, "hbm"), (x_rows, "load"), (gain, "vmem"), (extra, "hbm"), (keep, "vmem")]
     ins += [(text_grad, "hbm"), (sums, "vmem")] + [(own, "hbm") for own in owns]
     outs = [(shape(512, 2048, kind=BF16), "store"), (shape(8, 2048), "vmem")]
     outs += [(shape(128, 1024), "vmem")] + [(shape(64, JOB), "vmem")] * (len(owns) + count)
+    outs += [(shape(4, 64, RingHeads.WIDTH), "vmem")]
     scratch = list(TensorSum.SCRATCH + TensorSum.HALF) + [((512, 512), BF16)] * 4
+    scratch += [((512, 2048), BF16)] * 3 + [((512, RingHeads.WIDTH), BF16)] * 4
+    scratch += [((3, 512, RingHeads.WIDTH), F32)] * 2
+    scratch += list(RingHeads.SCRATCH + RingHeads.LAST)
     scratch += [((16, 2048), F32), ((128, 1024), F32), ((9, 8, 2048), F32)]
     scratch += list(RingTwo.SCRATCH + RingTwo.PARTS) * len(owns)
     scratch += (list(RingTwo.SCRATCH + RingOne.SCRATCH) + [((4, 128, JOB), F32)]) * count
 
     def body(net, in_refs, out_refs, refs):
-        late_attention, late_output, late_weights = in_refs.some(4), in_refs.one(), in_refs.some(3)
-        late_upstream, late_normed = in_refs.some(2)
+        late_attention, late_output, weights_hbm = in_refs.some(4), in_refs.one(), in_refs.some(3)
+        late_upstream, late_normed, beside_hbm, beyond_hbm = in_refs.some(4)
         late_x, gain_ref, extra_hbm, keep_ref, text_ref, sums_ref = in_refs.some(6)
         own_refs = in_refs.some(len(owns))
         image, small_ref, text_out = out_refs.some(3)
-        old_refs, new_refs = out_refs.some(len(owns)), out_refs.some(count)
+        old_refs, new_refs, heads_out = out_refs.some(len(owns)), out_refs.some(count), out_refs.one()
         sum_scratch, half, grad_mixed, grads = refs.some(4), refs.one(), refs.one(), refs.some(3)
+        rooms, rights, (leaving, arriving) = refs.some(3), refs.some(4), refs.some(2)
+        heads_scratch, heads_last = refs.some(4), refs.some(2)
         acc_ref, got_text, got_small = refs.some(3)
         old = [
             RingTwo(net, own, i % 2 == 0, old_refs[i], refs.some(2), refs.one())
@@ -863,13 +971,19 @@
         ones, twos = [], []
         for i in range(count):
             two_scratch, one_scratch, own = refs.some(2), refs.some(3), refs.one()
-            left = (late_normed if i else late_upstream).vmem
-            right = grads[i - 1] if i else late_attention[3].vmem
-            ones.append(RingOne(net, left, right, 0, i % 2 == 0, own, one_scratch))
-            twos.append(RingTwo(net, own, i % 2 == 0, new_refs[i], two_scratch))
+            left, right = late_upstream.vmem, late_attention[3].vmem
+            ones.append(RingOne(net, left, right, 0, False, own, one_scratch))
+            twos.append(RingTwo(net, own, False, new_refs[i], two_scratch))
+        lefts = [late_normed.vmem] + rooms
+        heads = RingHeads(net, lefts, rights, heads_out, heads_scratch, heads_last)
         output_copy = net.load(late_output, image.vmem)
         every([late_upstream, late_attention[3]] + late_attention[:3], "start")
-        every(late_weights + [late_normed], "start")
+        weight_copies = [
+            net.load(weight.at[pl.ds(n * 512, 512)], room.at[:, pl.ds(n * 512, 512)])
+            for weight, room in zip(weights_hbm, rooms)
+            for n in range(4)
+        ]
+        late_normed.start()
         net.greet(NEAR + ALL + [("zhi", 1)])
         acc_ref[...] = jnp.zeros_like(acc_ref)
         x_ref, extra_ref = late_x.vmem, half
@@ -898,25 +1012,42 @@
             )
             for ref, value in zip(grads, found):
                 ref[at] = value
-        weight_refs = [late.ref() for late in late_weights]
+        head = lambda x: pl.ds(pl.multiple_of(x * HEAD, HEAD), HEAD)
+        for i, ref in enumerate(grads):
+            columns = pl.ds(i * HEAD, HEAD)
+            rights[0][:, columns] = ref[:, head(net.x)]
+            for k in (1, 2, 3):
+                leaving[k - 1, :, columns] = ref[:, head((net.x + k) % 4)].astype(F32)
+        spread = [
+            net.push(leaving.at[k - 1], arriving.at[k - 1], "x", k) for k in (1, 2, 3)
+        ]
+        for copy in weight_copies:
+            copy.wait()
 
         def share(core, n):
             block, total = pl.ds(n * 512, 512), 0.0
-            for ref, weight in zip(grads, weight_refs):
-                total = total + back_product(ref[own_rows(core), :], weight[block, :])
+            for ref, weight in zip(grads, rooms):
+                total = total + back_product(ref[own_rows(core), :], weight[:, block])
             return total
 
         work = TensorSum(net, share, epilogue, image.vmem, sum_scratch, half)
         work.begin()
-        late_normed.ref()
-        every(ones[1:], "begin")
+        others = (beside_hbm.at[0], beyond_hbm.at[0], beside_hbm.at[1])
+        left_copies = [net.load(source, room) for source, room in zip(others, rooms)]
         work.exchange()
         work.free_half()
         extra_copy = net.load(extra_hbm, half)
         every(ones, "relay")
+        late_normed.ref()
+        for copy in left_copies:
+            copy.wait()
+        for k in range(3):
+            spread[k].wait_recv()
+            rights[k + 1][...] = low(arriving[k])
+        heads.begin()
         late_x.ref()
         extra_copy.wait()
-        work.work()
+        work.work(lambda j: heads.relay() if j == 3 else None)
         got_small[0] = sums_ref[...]
         got_small[0, 0:1, :] = jnp.sum(acc_ref[0:8, :], axis=0, keepdims=True)
         got_small[0, 3:4, :] = jnp.sum(acc_ref[8:16, :], axis=0, keepdims=True)
@@ -931,6 +1062,8 @@
         for one, two in zip(ones, twos):
             one.close()
             two.begin()
+        heads.close()
+        heads.swap()
         every(old, "finish")
         for copy in by_x:
             copy.wait()
@@ -942,16 +1075,22 @@
         got_small[0] += got_small[5] + got_small[6] + got_small[7]
         by_z = net.push(got_small.at[0], got_small.at[8], "zhi")
         every(twos, "third")
+        heads.third()
         text_copy.wait()
         text_push.wait()
         text_out[...] += got_text[...]
         by_z.wait()
         small_ref[...] = got_small[0] + got_small[8]
         every(twos, "finish")
+        heads.finish()
+        heads.done()
+        for copy in spread:
+            copy.wait_send()
         every(ones, "done")
 
     copies = TensorSum.COPIES + 9 + (len(owns) + count) * RingTwo.COPIES + count * RingOne.COPIES
-    loads = 3 + len(owns) * RingTwo.LOADS
+    copies += RingHeads.COPIES + RingHeads.COPIES_LAST + 3
+    loads = 18 + len(owns) * RingTwo.LOADS
     return call(body, ins, outs, scratch, copies, loads, 4, "backward_last")
 
 
@@ -992,13 +1131,24 @@
     normed_one = low(layer_norm(start, first_gain))
     weights = (self_query, self_key, self_value, self_output)
     start_own = own(start)
-    first, normed_two, text_columns, cross_keys, cross_values, *attention = forward_self(
-        normed_one, weights, start_own, gains[1], text_blocks, text_rows, text_key, text_value
+    columns = lax.dynamic_slice_in_dim(normed_one, core * (width // 2), width // 2, axis=1)
+    columns = columns.astype(F32)
+    first, normed_two, text_columns, cross_keys, cross_values, *attention, beside = forward_self(
+        normed_one,
+        columns,
+        weights,
+        start_own,
+        gains[1],
+        text_blocks,
+        text_rows,
+        text_key,
+        text_value,
     )
     text_columns = low(text_columns.reshape(-1, text_columns.shape[-1]))
 
     present = (jnp.arange(words)[None, :] < text_len[:, None]).astype(F32)
-    second, normed_three, active, grad_raised, cross_query, cross_rows = forward_cross(
+    second, normed_three, active, grad_raised, cross_query, cross_rows, beyond = forward_cross(
+        columns,
         normed_two,
         (text_query, text_output),
         cross_keys,
@@ -1047,6 +1197,8 @@
         weights,
         self_out_grad,
         normed_one,
+        beside,
+        beyond,
         start_own,
         gains[0],
         grad_first,
@@ -1055,7 +1207,9 @@
         text_grads,
         sums,
     )
-    expand_grad, (to, tq, so, sq, sk, sv) = rest[:4], rest[4:]
+    expand_grad, (to, tq, so, heads) = rest[:4], rest[4:]
+    heads = heads.reshape(4, -1, 3, HEAD).transpose(2, 1, 0, 3)
+    sq, sk, sv = heads.reshape(3, heads.shape[1], -1)
 
     share = width // 32
     small = lax.dynamic_slice_in_dim(small, lax.axis_index("dp") * share, share, axis=1)

time: 540 us -> 533 us (0.987)
  Pallas kernels: 499 us -> 493 us
    pallas_call x5, Pallas kernels: 499 us -> 493 us  [call(): pl.pallas_call(kernel, name=name, out_shape=[o for o, _ in outs], in_spec...]
where the time goes in v7:
time: 533 us; the launch traced here: 526 us
  Pallas kernels  493 us (92%)
  other arithmetic  15.2 us (3%)
  local copies, waits for them, and re-layouts  13.8 us (3%)
    pallas_call x5, Pallas kernels, call(): pl.pallas_call(kernel, name=name, out_shape=[o for o, _ in outs], in_spec...  493 us

profile of v7, /device:TPU:0, one launch (start us, length us, event | category | flops | bytes accessed | tf_op | source)
XLA Modules:
  0.0 526.2 jit_solution(15559217854541535752)
XLA Ops:
  0.6 0.0 copy-start.1
  0.7 0.0 copy-start.16
  0.7 0.8 broadcast_compare_fusion
  1.5 2.2 select_reduce_fusion
  3.7 0.0 copy-done.1
  3.7 0.0 copy-done.16
  3.7 0.8 multiply_reduce_fusion
  4.6 0.0 copy-done.18
  4.6 2.5 bitcast_select_fusion
  7.2 0.0 copy-start
  7.2 1.8 constant_dynamic-slice_fusion.1.refs_6_.refs_12_
  9.0 0.2 copy-done
  9.2 1.6 dynamic-slice_convert_fusion.1.refs_0_
  10.7 0.0 copy-done.5
  10.7 0.4 reshape.201
  11.2 1.1 copy.71
  12.3 67.5 %forward_self.1 = (f32[256,2048]{1,0:T(8,128)}, bf16[512,2048]{1,0:T(8,128)(2,1)}, f32[4,4,32,256]{3,2,1,0:T(8,128)}, bf16[32,512]{1,0:T(8,128)(2,1)}, bf16[32,5...) custom-call(f32[512,1024]{1,0:T(8,128)} %dynamic-slice_convert_fusio, ...), custom_call_target="tpu_custom_call" | custom-call | tf_op jit(solution)/shard_map/forward_self/pallas_call | solution.py:506
  79.8 0.0 copy-done.21
  79.8 0.6 compare_convert_fusion.refs_6_.refs_3_
  80.4 69.1 %forward_cross.1 = (f32[256,2048]{1,0:T(8,128)}, bf16[512,2048]{1,0:T(8,128)(2,1)}, bf16[512,2048]{1,0:T(8,128)(2,1)}, bf16[512,2048]{1,0:T(8,128)(2,1)}, bf16[5...) custom-call(f32[512,1024]{1,0:T(8,128)} %dynamic-slice_convert_fusion.1.refs_0_, ...), custom_call_target="tpu_custom_call" | custom-call | tf_op jit(solution)/shard_map/forward_cross/pallas_call | solution.py:506
  149.6 0.0 copy-done.2
  149.6 1.6 dynamic-slice_convert_fusion.refs_4_
  151.2 77.7 %backward_first.1 = (f32[256,2048]{1,0:T(8,128)}, bf16[512,2048]{1,0:T(8,128)(2,1)}, f32[8,2048]{1,0:T(8,128)}, f32[512,2048]{1,0:T(8,128)}, f32[4,128,512]{2,1,...) custom-call(bf16[512,2048]{1,0:T(8,128)(2,1)} %get-tuple-element.97.refs_0_.refs_15_, ...), custom_call_target="tpu_custom_call" | custom-call | tf_op jit(solution)/shard_map/backward_first/pallas_call | solution.py:506
  228.8 0.0 copy-start.17
  228.8 0.0 copy-start.20
  228.8 143.6 %backward_second.1 = (f32[256,2048]{1,0:T(8,128)}, bf16[512,2048]{1,0:T(8,128)(2,1)}, f32[8,2048]{1,0:T(8,128)}, f32[4,4,32,512]{3,2,1,0:T(8,128)}, f32[4,4,32,5...) custom-call(bf16[512,512]{1,0:T(8,128)(2,1)} %get-tuple-element.96.r, ...), custom_call_target="tpu_custom_call" | custom-call | tf_op jit(solution)/shard_map/backward_second/pallas_call | solution.py:506
  372.5 0.9 reduce_sum.38
  373.4 0.0 copy-done.17
  373.4 0.2 scatter.9.refs_17_
  373.6 0.0 copy-start.8
  373.6 1.3 convert_bitcast_fusion
  375.0 0.0 copy-done.20
  375.0 0.0 copy-start.19
  375.0 2.7 convolution_bitcast_fusion.refs_16_
  377.6 0.0 copy-done.8
  377.6 0.0 copy-done.19
  377.6 0.1 copy.55
  377.8 0.7 convert_subtract_fusion.refs_15_
  378.5 135.4 %backward_last.1 = (bf16[512,2048]{1,0:T(8,128)(2,1)}, f32[8,2048]{1,0:T(8,128)}, f32[128,1024]{1,0:T(8,128)}, f32[64,512]{1,0:T(8,128)}, f32[64,512]{1,0:T(8,12...) custom-call(bf16[512,512]{1,0:T(8,128)(2,1)} %get-tuple-element.110., ...), custom_call_target="tpu_custom_call" | custom-call | tf_op jit(solution)/shard_map/backward_last/pallas_call | solution.py:506
  513.9 0.0 copy-start.7
  513.9 0.0 copy-done.9
  513.9 0.0 copy-done.10
  513.9 0.0 copy-done.11
  513.9 0.0 copy-done.12
  513.9 2.2 pad_maximum_fusion.1
  516.1 0.0 copy-done.7
  516.1 0.2 reshape.199
  516.3 0.3 fusion.4
  516.6 0.1 copy.49
  516.7 0.1 copy.50
  516.8 0.7 copy_bitcast_fusion.1
  517.5 0.1 copy.48
  517.6 0.7 copy.72
  518.2 0.0 copy-done.6
  518.2 0.8 fusion.3
  519.1 0.7 constant_dynamic-slice_fusion
  519.8 0.5 slice_bitcast_fusion
  520.3 0.0 copy-done.3
  520.3 1.3 copy.79
  521.7 1.0 copy-done.4
  522.7 1.3 copy.80
  524.0 0.7 copy.81
  524.7 0.7 copy.82
  525.3 0.7 copy.83
  (25 shorter events, 0.1 us)
Async XLA Ops:
  0.6 3.1 copy-start.1
  0.7 3.1 copy-start.16
  1.5 3.1 copy-start.18
  7.2 2.0 copy-start
  9.0 1.8 copy-start.5
  12.3 67.5 %copy-start.21 = (s32[2]{0:T(128)S(1)}, s32[2]{0:T(128)}, u32[]{:S(2)}) copy-start(s32[2]{0:T(128)} %param.26) | copy-start | bytes 28
  80.4 69.2 %copy-start.2 = (bf16[2,256,2048]{2,1,0:T(8,128)(2,1)S(1)}, bf16[2,256,2048]{2,1,0:T(8,128)(2,1)}, u32[]{:S(2)}) copy-start(bf16[2,256,2048]{2,1,0:T(8,128)(2,1)} %param.27) | copy-start | bytes 6291460
  228.8 144.5 %copy-start.17 = (f32[8,2048]{1,0:T(8,128)S(1)}, f32[8,2048]{1,0:T(8,128)}, u32[]{:S(2)}) copy-start(f32[8,2048]{1,0:T(8,128)} %get-tuple-element.122) | copy-start | bytes 196612
  228.8 146.1 %copy-start.20 = (f32[4,4,32,256]{3,2,1,0:T(8,128)S(1)}, f32[4,4,32,256]{3,2,1,0:T(8,128)}, u32[]{:S(2)}) copy-start(f32[4,4,32,256]{3,2,1,0:T(8,128)} %get-tuple-element.118) | copy-start | bytes 1572868
  373.6 4.0 copy-start.8
  375.0 2.7 copy-start.19
  378.5 135.4 %copy-start.9 = (f32[64,512]{1,0:T(8,128)S(1)}, f32[64,512]{1,0:T(8,128)}, u32[]{:S(2)}) copy-start(f32[64,512]{1,0:T(8,128)} %get-tuple-element.139) | copy-start | bytes 393220
  378.5 135.4 %copy-start.10 = (f32[64,512]{1,0:T(8,128)S(1)}, f32[64,512]{1,0:T(8,128)}, u32[]{:S(2)}) copy-start(f32[64,512]{1,0:T(8,128)} %get-tuple-element.140) | copy-start | bytes 393220
  378.5 135.4 %copy-start.11 = (f32[64,512]{1,0:T(8,128)S(1)}, f32[64,512]{1,0:T(8,128)}, u32[]{:S(2)}) copy-start(f32[64,512]{1,0:T(8,128)} %get-tuple-element.141) | copy-start | bytes 393220
  378.5 135.4 %copy-start.12 = (f32[64,512]{1,0:T(8,128)S(1)}, f32[64,512]{1,0:T(8,128)}, u32[]{:S(2)}) copy-start(f32[64,512]{1,0:T(8,128)} %get-tuple-element.142) | copy-start | bytes 393220
  513.9 2.2 copy-start.7
  516.1 2.1 copy-start.6
  516.1 4.2 copy-start.3
  520.3 2.3 copy-start.4
  522.7 1.3 copy-start.15
  522.7 2.0 copy-start.14
  522.7 2.6 copy-start.13

commit v8 on v7

--- a/solution.py
+++ b/solution.py
@@ -996,13 +996,14 @@
             acc_ref[8:16, :] += jnp.where(kept, 0.0, result)
             return jnp.where(kept, result, 0.0)
 
+        text_rows = lambda z: pl.ds(pl.multiple_of(z * 128, 128), 128)
+        text_push = net.push(text_ref.at[text_rows(1 - net.z)], got_text, "zhi")
         every(old, "begin")
         every([late_upstream, late_attention[3]], "ref")
         ones[0].begin()
         output_copy.wait()
         grad_mixed[...] = low(back_product(late_upstream.vmem[...], image.vmem[...]))
         late_x.start()
-        text_rows = lambda z: pl.ds(pl.multiple_of(z * 128, 128), 128)
         text_copy = net.load(text_ref.at[text_rows(net.z)], text_out)
         query_ref, keys_ref, values_ref = [late.ref() for late in late_attention[:3]]
         every(old, "relay")
@@ -1047,18 +1048,16 @@
         heads.begin()
         late_x.ref()
         extra_copy.wait()
-        work.work(lambda j: heads.relay() if j == 3 else None)
+        work.work(lambda j: heads.relay() if j == 3 else every(old[3 * j : 3 * j + 3], "third"))
         got_small[0] = sums_ref[...]
         got_small[0, 0:1, :] = jnp.sum(acc_ref[0:8, :], axis=0, keepdims=True)
         got_small[0, 3:4, :] = jnp.sum(acc_ref[8:16, :], axis=0, keepdims=True)
         by_core = net.push(got_small.at[0], got_small.at[1], "core")
-        text_push = net.push(text_ref.at[text_rows(1 - net.z)], got_text, "zhi")
         work.finish()
         net.store(image)
         by_core.wait()
         got_small[0] += got_small[1]
         by_x = [net.push(got_small.at[0], got_small.at[1 + k], "x", k) for k in (1, 2, 3)]
-        every(old, "third")
         for one, two in zip(ones, twos):
             one.close()
             two.begin()

time: 533 us -> 525 us (0.985)
  Pallas kernels: 493 us -> 483 us
    pallas_call x5, Pallas kernels: 493 us -> 483 us  [call(): pl.pallas_call(kernel, name=name, out_shape=[o for o, _ in outs], in_spec...]
where the time goes in v8:
time: 525 us; the launch traced here: 516 us
  Pallas kernels  483 us (92%)
  other arithmetic  15.2 us (3%)
  local copies, waits for them, and re-layouts  13.8 us (3%)
    pallas_call x5, Pallas kernels, call(): pl.pallas_call(kernel, name=name, out_shape=[o for o, _ in outs], in_spec...  483 us

profile of v8, /device:TPU:0, one launch (start us, length us, event | category | flops | bytes accessed | tf_op | source)
XLA Modules:
  0.0 515.8 jit_solution(5082690219667934742)
XLA Ops:
  0.6 0.0 copy-start.1
  0.7 0.0 copy-start.16
  0.7 0.8 broadcast_compare_fusion
  1.5 2.2 select_reduce_fusion
  3.7 0.0 copy-done.1
  3.7 0.0 copy-done.16
  3.7 0.8 multiply_reduce_fusion
  4.6 0.0 copy-done.18
  4.6 2.5 bitcast_select_fusion
  7.2 0.0 copy-start
  7.2 1.8 constant_dynamic-slice_fusion.1.refs_6_.refs_12_
  9.0 0.2 copy-done
  9.2 1.6 dynamic-slice_convert_fusion.1.refs_0_
  10.7 0.0 copy-done.5
  10.7 0.4 reshape.201
  11.2 1.1 copy.71
  12.3 67.5 %forward_self.1 = (f32[256,2048]{1,0:T(8,128)}, bf16[512,2048]{1,0:T(8,128)(2,1)}, f32[4,4,32,256]{3,2,1,0:T(8,128)}, bf16[32,512]{1,0:T(8,128)(2,1)}, bf16[32,5...) custom-call(f32[512,1024]{1,0:T(8,128)} %dynamic-slice_convert_fusio, ...), custom_call_target="tpu_custom_call" | custom-call | tf_op jit(solution)/shard_map/forward_self/pallas_call | solution.py:506
  79.8 0.0 copy-done.21
  79.8 0.6 compare_convert_fusion.refs_6_.refs_3_
  80.4 69.1 %forward_cross.1 = (f32[256,2048]{1,0:T(8,128)}, bf16[512,2048]{1,0:T(8,128)(2,1)}, bf16[512,2048]{1,0:T(8,128)(2,1)}, bf16[512,2048]{1,0:T(8,128)(2,1)}, bf16[5...) custom-call(f32[512,1024]{1,0:T(8,128)} %dynamic-slice_convert_fusion.1.refs_0_, ...), custom_call_target="tpu_custom_call" | custom-call | tf_op jit(solution)/shard_map/forward_cross/pallas_call | solution.py:506
  149.6 0.0 copy-done.2
  149.6 1.6 dynamic-slice_convert_fusion.refs_4_
  151.2 77.7 %backward_first.1 = (f32[256,2048]{1,0:T(8,128)}, bf16[512,2048]{1,0:T(8,128)(2,1)}, f32[8,2048]{1,0:T(8,128)}, f32[512,2048]{1,0:T(8,128)}, f32[4,128,512]{2,1,...) custom-call(bf16[512,2048]{1,0:T(8,128)(2,1)} %get-tuple-element.97.refs_0_.refs_15_, ...), custom_call_target="tpu_custom_call" | custom-call | tf_op jit(solution)/shard_map/backward_first/pallas_call | solution.py:506
  228.8 0.0 copy-start.17
  228.8 0.0 copy-start.20
  228.8 143.6 %backward_second.1 = (f32[256,2048]{1,0:T(8,128)}, bf16[512,2048]{1,0:T(8,128)(2,1)}, f32[8,2048]{1,0:T(8,128)}, f32[4,4,32,512]{3,2,1,0:T(8,128)}, f32[4,4,32,5...) custom-call(bf16[512,512]{1,0:T(8,128)(2,1)} %get-tuple-element.96.r, ...), custom_call_target="tpu_custom_call" | custom-call | tf_op jit(solution)/shard_map/backward_second/pallas_call | solution.py:506
  372.5 0.9 reduce_sum.38
  373.4 0.0 copy-done.17
  373.4 0.2 scatter.9.refs_17_
  373.6 0.0 copy-start.8
  373.6 1.3 convert_bitcast_fusion
  375.0 0.0 copy-done.20
  375.0 0.0 copy-start.19
  375.0 2.7 convolution_bitcast_fusion.refs_16_
  377.6 0.0 copy-done.8
  377.6 0.0 copy-done.19
  377.6 0.1 copy.55
  377.8 0.7 convert_subtract_fusion.refs_15_
  378.5 125.0 %backward_last.1 = (bf16[512,2048]{1,0:T(8,128)(2,1)}, f32[8,2048]{1,0:T(8,128)}, f32[128,1024]{1,0:T(8,128)}, f32[64,512]{1,0:T(8,128)}, f32[64,512]{1,0:T(8,12...) custom-call(bf16[512,512]{1,0:T(8,128)(2,1)} %get-tuple-element.110., ...), custom_call_target="tpu_custom_call" | custom-call | tf_op jit(solution)/shard_map/backward_last/pallas_call | solution.py:506
  503.5 0.0 copy-start.7
  503.5 0.0 copy-done.9
  503.5 0.0 copy-done.10
  503.5 0.0 copy-done.11
  503.6 0.0 copy-done.12
  503.6 2.2 pad_maximum_fusion.1
  505.8 0.2 reshape.199
  505.9 0.3 fusion.4
  506.2 0.1 copy.49
  506.3 0.1 copy.50
  506.4 0.7 copy_bitcast_fusion.1
  507.1 0.1 copy.48
  507.2 0.7 copy.72
  507.9 0.0 copy-done.6
  507.9 0.8 fusion.3
  508.7 0.7 constant_dynamic-slice_fusion
  509.5 0.5 slice_bitcast_fusion
  510.0 0.0 copy-done.3
  510.0 1.3 copy.79
  511.3 1.0 copy-done.4
  512.4 1.3 copy.80
  513.7 0.0 copy-done.15
  513.7 0.7 copy.81
  514.3 0.7 copy.82
  515.0 0.7 copy.83
  (25 shorter events, 0.1 us)
Async XLA Ops:
  0.6 3.1 copy-start.1
  0.7 3.1 copy-start.16
  1.5 3.1 copy-start.18
  7.2 2.0 copy-start
  9.0 1.8 copy-start.5
  12.3 67.5 %copy-start.21 = (s32[2]{0:T(128)S(1)}, s32[2]{0:T(128)}, u32[]{:S(2)}) copy-start(s32[2]{0:T(128)} %param.26) | copy-start | bytes 28
  80.4 69.2 %copy-start.2 = (bf16[2,256,2048]{2,1,0:T(8,128)(2,1)S(1)}, bf16[2,256,2048]{2,1,0:T(8,128)(2,1)}, u32[]{:S(2)}) copy-start(bf16[2,256,2048]{2,1,0:T(8,128)(2,1)} %param.27) | copy-start | bytes 6291460
  228.8 144.5 %copy-start.17 = (f32[8,2048]{1,0:T(8,128)S(1)}, f32[8,2048]{1,0:T(8,128)}, u32[]{:S(2)}) copy-start(f32[8,2048]{1,0:T(8,128)} %get-tuple-element.122) | copy-start | bytes 196612
  228.8 146.1 %copy-start.20 = (f32[4,4,32,256]{3,2,1,0:T(8,128)S(1)}, f32[4,4,32,256]{3,2,1,0:T(8,128)}, u32[]{:S(2)}) copy-start(f32[4,4,32,256]{3,2,1,0:T(8,128)} %get-tuple-element.118) | copy-start | bytes 1572868
  373.6 4.0 copy-start.8
  375.0 2.7 copy-start.19
  378.5 125.1 %copy-start.9 = (f32[64,512]{1,0:T(8,128)S(1)}, f32[64,512]{1,0:T(8,128)}, u32[]{:S(2)}) copy-start(f32[64,512]{1,0:T(8,128)} %get-tuple-element.139) | copy-start | bytes 393220
  378.5 125.1 %copy-start.10 = (f32[64,512]{1,0:T(8,128)S(1)}, f32[64,512]{1,0:T(8,128)}, u32[]{:S(2)}) copy-start(f32[64,512]{1,0:T(8,128)} %get-tuple-element.140) | copy-start | bytes 393220
  378.5 125.1 %copy-start.11 = (f32[64,512]{1,0:T(8,128)S(1)}, f32[64,512]{1,0:T(8,128)}, u32[]{:S(2)}) copy-start(f32[64,512]{1,0:T(8,128)} %get-tuple-element.141) | copy-start | bytes 393220
  378.5 125.1 %copy-start.12 = (f32[64,512]{1,0:T(8,128)S(1)}, f32[64,512]{1,0:T(8,128)}, u32[]{:S(2)}) copy-start(f32[64,512]{1,0:T(8,128)} %get-tuple-element.142) | copy-start | bytes 393220
  503.5 2.2 copy-start.7
  505.8 2.1 copy-start.6
  505.8 4.2 copy-start.3
  510.0 2.3 copy-start.4
  512.4 1.3 copy-start.15
  512.4 2.0 copy-start.14
  512.4 2.6 copy-start.13

commit v9 on v8

--- a/solution.py
+++ b/solution.py
@@ -613,10 +613,10 @@
         late_rows.ref()
         work.work(gather.hand)
         net.store(total)
+        gather.finish()
+        net.store(beside)
         work.finish()
         net.store(normed)
-        gather.finish()
-        net.store(beside)
         kept.wait()
         for copy in second:
             copy.wait_recv()
@@ -697,13 +697,13 @@
 
         work.work(gather.hand)
         net.store(total)
+        gather.finish()
+        net.store(beyond)
         hidden(net.core)
         work.finish()
         net.store(normed)
         hidden(1 - net.core)
         net.store(active)
-        gather.finish()
-        net.store(beyond)
         net.store(grad_raised)
 
     return call(

time: 525 us -> 524 us (level)
  no operation moved by 1% of the time
where the time goes in v9:
time: 524 us; the launch traced here: 515 us
  Pallas kernels  482 us (92%)
  other arithmetic  15.2 us (3%)
  local copies, waits for them, and re-layouts  13.8 us (3%)
    pallas_call x5, Pallas kernels, call(): pl.pallas_call(kernel, name=name, out_shape=[o for o, _ in outs], in_spec...  482 us

profile of v9, /device:TPU:0, one launch (start us, length us, event | category | flops | bytes accessed | tf_op | source)
XLA Modules:
  0.0 514.9 jit_solution(18353268111303877227)
XLA Ops:
  0.6 0.0 copy-start.1
  0.7 0.0 copy-start.16
  0.7 0.8 broadcast_compare_fusion
  1.5 2.2 select_reduce_fusion
  3.7 0.0 copy-done.1
  3.7 0.0 copy-done.16
  3.7 0.8 multiply_reduce_fusion
  4.6 0.0 copy-done.18
  4.6 2.5 bitcast_select_fusion
  7.2 0.0 copy-start
  7.2 1.8 constant_dynamic-slice_fusion.1.refs_6_.refs_12_
  9.0 0.2 copy-done
  9.2 1.6 dynamic-slice_convert_fusion.1.refs_0_
  10.7 0.0 copy-done.5
  10.7 0.4 reshape.201
  11.2 1.1 copy.71
  12.3 66.7 %forward_self.1 = (f32[256,2048]{1,0:T(8,128)}, bf16[512,2048]{1,0:T(8,128)(2,1)}, f32[4,4,32,256]{3,2,1,0:T(8,128)}, bf16[32,512]{1,0:T(8,128)(2,1)}, bf16[32,5...) custom-call(f32[512,1024]{1,0:T(8,128)} %dynamic-slice_convert_fusio, ...), custom_call_target="tpu_custom_call" | custom-call | tf_op jit(solution)/shard_map/forward_self/pallas_call | solution.py:506
  79.0 0.0 copy-done.21
  79.0 0.6 compare_convert_fusion.refs_6_.refs_3_
  79.6 69.0 %forward_cross.1 = (f32[256,2048]{1,0:T(8,128)}, bf16[512,2048]{1,0:T(8,128)(2,1)}, bf16[512,2048]{1,0:T(8,128)(2,1)}, bf16[512,2048]{1,0:T(8,128)(2,1)}, bf16[5...) custom-call(f32[512,1024]{1,0:T(8,128)} %dynamic-slice_convert_fusion.1.refs_0_, ...), custom_call_target="tpu_custom_call" | custom-call | tf_op jit(solution)/shard_map/forward_cross/pallas_call | solution.py:506
  148.6 0.0 copy-done.2
  148.6 1.6 dynamic-slice_convert_fusion.refs_4_
  150.2 77.7 %backward_first.1 = (f32[256,2048]{1,0:T(8,128)}, bf16[512,2048]{1,0:T(8,128)(2,1)}, f32[8,2048]{1,0:T(8,128)}, f32[512,2048]{1,0:T(8,128)}, f32[4,128,512]{2,1,...) custom-call(bf16[512,2048]{1,0:T(8,128)(2,1)} %get-tuple-element.97.refs_0_.refs_15_, ...), custom_call_target="tpu_custom_call" | custom-call | tf_op jit(solution)/shard_map/backward_first/pallas_call | solution.py:506
  228.0 0.0 copy-start.17
  228.0 0.0 copy-start.20
  228.0 143.6 %backward_second.1 = (f32[256,2048]{1,0:T(8,128)}, bf16[512,2048]{1,0:T(8,128)(2,1)}, f32[8,2048]{1,0:T(8,128)}, f32[4,4,32,512]{3,2,1,0:T(8,128)}, f32[4,4,32,5...) custom-call(bf16[512,512]{1,0:T(8,128)(2,1)} %get-tuple-element.96.r, ...), custom_call_target="tpu_custom_call" | custom-call | tf_op jit(solution)/shard_map/backward_second/pallas_call | solution.py:506
  371.6 0.9 reduce_sum.38
  372.5 0.0 copy-done.17
  372.5 0.2 scatter.9.refs_17_
  372.7 0.0 copy-start.8
  372.7 1.3 convert_bitcast_fusion
  374.1 0.0 copy-done.20
  374.1 0.0 copy-start.19
  374.1 2.7 convolution_bitcast_fusion.refs_16_
  376.7 0.0 copy-done.8
  376.7 0.0 copy-done.19
  376.7 0.1 copy.55
  376.9 0.7 convert_subtract_fusion.refs_15_
  377.6 125.0 %backward_last.1 = (bf16[512,2048]{1,0:T(8,128)(2,1)}, f32[8,2048]{1,0:T(8,128)}, f32[128,1024]{1,0:T(8,128)}, f32[64,512]{1,0:T(8,128)}, f32[64,512]{1,0:T(8,12...) custom-call(bf16[512,512]{1,0:T(8,128)(2,1)} %get-tuple-element.110., ...), custom_call_target="tpu_custom_call" | custom-call | tf_op jit(solution)/shard_map/backward_last/pallas_call | solution.py:506
  502.6 0.0 copy-start.7
  502.6 0.0 copy-done.9
  502.6 0.0 copy-done.10
  502.6 0.0 copy-done.11
  502.6 0.0 copy-done.12
  502.6 2.2 pad_maximum_fusion.1
  504.8 0.0 copy-done.7
  504.8 0.2 reshape.199
  505.0 0.3 fusion.4
  505.3 0.1 copy.49
  505.4 0.1 copy.50
  505.5 0.7 copy_bitcast_fusion.1
  506.2 0.1 copy.48
  506.3 0.7 copy.72
  507.0 0.0 copy-done.6
  507.0 0.8 fusion.3
  507.8 0.7 constant_dynamic-slice_fusion
  508.5 0.5 slice_bitcast_fusion
  509.1 0.0 copy-done.3
  509.1 1.3 copy.79
  510.4 1.0 copy-done.4
  511.4 1.3 copy.80
  512.7 0.7 copy.81
  513.4 0.7 copy.82
  514.1 0.7 copy.83
  (25 shorter events, 0.1 us)
Async XLA Ops:
  0.6 3.1 copy-start.1
  0.7 3.1 copy-start.16
  1.5 3.1 copy-start.18
  7.2 2.0 copy-start
  9.0 1.8 copy-start.5
  12.3 66.7 %copy-start.21 = (s32[2]{0:T(128)S(1)}, s32[2]{0:T(128)}, u32[]{:S(2)}) copy-start(s32[2]{0:T(128)} %param.26) | copy-start | bytes 28
  79.6 69.0 %copy-start.2 = (bf16[2,256,2048]{2,1,0:T(8,128)(2,1)S(1)}, bf16[2,256,2048]{2,1,0:T(8,128)(2,1)}, u32[]{:S(2)}) copy-start(bf16[2,256,2048]{2,1,0:T(8,128)(2,1)} %param.27) | copy-start | bytes 6291460
  228.0 144.5 %copy-start.17 = (f32[8,2048]{1,0:T(8,128)S(1)}, f32[8,2048]{1,0:T(8,128)}, u32[]{:S(2)}) copy-start(f32[8,2048]{1,0:T(8,128)} %get-tuple-element.122) | copy-start | bytes 196612
  228.0 146.1 %copy-start.20 = (f32[4,4,32,256]{3,2,1,0:T(8,128)S(1)}, f32[4,4,32,256]{3,2,1,0:T(8,128)}, u32[]{:S(2)}) copy-start(f32[4,4,32,256]{3,2,1,0:T(8,128)} %get-tuple-element.118) | copy-start | bytes 1572868
  372.7 4.0 copy-start.8
  374.1 2.7 copy-start.19
  377.6 125.0 %copy-start.9 = (f32[64,512]{1,0:T(8,128)S(1)}, f32[64,512]{1,0:T(8,128)}, u32[]{:S(2)}) copy-start(f32[64,512]{1,0:T(8,128)} %get-tuple-element.139) | copy-start | bytes 393220
  377.6 125.0 %copy-start.10 = (f32[64,512]{1,0:T(8,128)S(1)}, f32[64,512]{1,0:T(8,128)}, u32[]{:S(2)}) copy-start(f32[64,512]{1,0:T(8,128)} %get-tuple-element.140) | copy-start | bytes 393220
  377.6 125.0 %copy-start.11 = (f32[64,512]{1,0:T(8,128)S(1)}, f32[64,512]{1,0:T(8,128)}, u32[]{:S(2)}) copy-start(f32[64,512]{1,0:T(8,128)} %get-tuple-element.141) | copy-start | bytes 393220
  377.6 125.0 %copy-start.12 = (f32[64,512]{1,0:T(8,128)S(1)}, f32[64,512]{1,0:T(8,128)}, u32[]{:S(2)}) copy-start(f32[64,512]{1,0:T(8,128)} %get-tuple-element.142) | copy-start | bytes 393220
  502.6 2.2 copy-start.7
  504.8 2.1 copy-start.6
  504.8 4.2 copy-start.3
  509.1 2.3 copy-start.4
  511.4 1.3 copy-start.15
  511.4 2.0 copy-start.14
  511.4 2.6 copy-start.13
